TPU v7x, 32 devices: a whole 2x2x4 slice. The times are simulated.
32 devices in a mesh: dp: 8 (over z, y), row: 2 (over x), col: 2 (over core).
Axes of the slice: x: 2, y: 2, z: 4, core: 2. Of those that a mesh axis runs over, the one named last changes fastest.
Arguments:
- inputs: bfloat16 [150, 192, 2000], P(None, 'dp', 'row'), may hold values from -6 to 6
- w_second: bfloat16 [2000, 2000], P('row', 'col'), may hold values from -0.125 to 0.125
- gain_second: float32 [2000], P('col'), may hold values from 0.5 to 1.5
- shift_second: float32 [2000], P('col'), may hold values from -3 to 3
- recur_second: float32 [2000], P('col'), may hold values from 0.2 to 0.9
- w_third: bfloat16 [2000, 2000], P('col', 'row'), may hold values from -0.125 to 0.125
- gain_third: float32 [2000], P('row'), may hold values from 0.5 to 1.5
- shift_third: float32 [2000], P('row'), may hold values from -3 to 3
- recur_third: float32 [2000], P('row'), may hold values from 0.2 to 0.9
- cotangent: bfloat16 [150, 192, 2000], P(None, ('dp', 'col'), 'row'), may hold values from -6 to 6
Outputs:
- output: float32 [150, 192, 2000], P(None, ('dp', 'col'), 'row')
- grad_inputs: float32 [150, 192, 2000], P(None, ('dp', 'col'), 'row')
- grad_w_second: float32 [2000, 2000], P('row', 'col')
- grad_gain_second: float32 [2000], P('col')
- grad_shift_second: float32 [2000], P('col')
- grad_recur_second: float32 [2000], P('col')
- grad_w_third: float32 [2000, 2000], P('col', 'row')
- grad_gain_third: float32 [2000], P('row')
- grad_shift_third: float32 [2000], P('row')
- grad_recur_third: float32 [2000], P('row')
All inputs are finite; a program needn't handle non-finite values.
Results may differ from a plain program's by a relative error of at most 0.0065.
Values may be sent and summed in bfloat16 or wider, within the bound.
No kernel may reach another device: no remote copies, remote signals or barrier semaphores. Data moves between devices by JAX's collectives and lax.ppermute only.
A program may use at most 256 MiB of HBM per device.

v0:
```python
import functools

import jax
import jax.numpy as jnp
from jax import lax
from jax.experimental import pallas as pl
from jax.experimental.pallas import tpu as pltpu
from jax.sharding import PartitionSpec as P

norm_eps = 1e-05
gelu_outer = 0.7978845608028654
gelu_inner = gelu_outer * 0.044715
LANES = 128
BLOCK = 256
WIDE = 512
f32 = jnp.float32
bf16 = jnp.bfloat16


def params(mebibytes=56):
    return pltpu.CompilerParams(vmem_limit_bytes=mebibytes * 2**20)


def round_up(value, unit):
    return -(-value // unit) * unit


def after(deps):
    return [pl.BlockSpec(memory_space=pl.ANY)] * len(deps)


def without(kernel, at, count, token=None):
    def body(*refs):
        refs = list(refs)
        if token is not None:
            refs.pop(token)[...] = jnp.zeros((8, LANES), f32)
        kernel(*refs[:at], *refs[at + count :])

    return body


token_spec = pl.BlockSpec((8, LANES), lambda *_: (0, 0))
token_shape = jax.ShapeDtypeStruct((8, LANES), f32)


def whole(shape):
    return pl.BlockSpec(shape, lambda *_: (0,) * len(shape), pipeline_mode=pl.Buffered(1))


def dot(left, right, dims):
    return lax.dot_general(left, right, (dims, ((), ())), preferred_element_type=f32)


def tile_of(j):
    return pl.ds(j * LANES, LANES)


def held(j, low, count):
    return jnp.clip(j - low, 0, count - 1)


def prep_kernel(seqs, pitch, width, base, at_ref, inputs, *refs):
    near, send, scratch, packed = refs[-4:]
    steps, group, block = inputs.shape
    lane = base + pl.program_id(0) * block + lax.broadcasted_iota(jnp.int32, (1, LANES), 1)
    rows = near.shape[0]
    for k in range(block // LANES):
        scratch[...] = inputs[:, :, tile_of(k)].astype(f32).reshape(steps * group, LANES)
        for place, out in ((0, near), (1, send)):
            first = at_ref[place]
            for s in range(seqs):
                packed[s * pitch : s * pitch + steps, :] = scratch[pl.ds(first + s, steps, stride=group), :]
                packed[s * pitch + steps : (s + 1) * pitch, :] = jnp.zeros((pitch - steps, LANES), f32)
            out[:, tile_of(k)] = jnp.where(lane + k * LANES < width, packed[...], 0.0).astype(bf16)


def prep(inputs, places, seqs, pitch, half, first, blocks, near=None, deps=()):
    steps, group, width = inputs.shape
    rows = seqs * pitch
    near_spec = pl.BlockSpec((rows, BLOCK), lambda j, at: (0, j + first))
    return pl.pallas_call(
        without(functools.partial(prep_kernel, seqs, pitch, width, first * BLOCK), 2, len(deps)),
        grid_spec=pltpu.PrefetchScalarGridSpec(
            num_scalar_prefetch=1,
            grid=(blocks,),
            in_specs=[pl.BlockSpec((steps, group, BLOCK), lambda j, at: (0, 0, j + first))]
            + after(deps)
            + ([] if near is None else [pl.BlockSpec(memory_space=pl.ANY)]),
            out_specs=[near_spec, pl.BlockSpec((rows, BLOCK), lambda j, at: (0, j))],
            scratch_shapes=[pltpu.VMEM((steps * group, LANES), f32), pltpu.VMEM((rows, LANES), f32)],
        ),
        out_shape=[
            jax.ShapeDtypeStruct((rows, half), bf16),
            jax.ShapeDtypeStruct((rows, blocks * BLOCK), bf16),
        ],
        input_output_aliases={} if near is None else {2 + len(deps): 0},
        compiler_params=params(),
        name="prep",
    )(places, inputs, *deps, *(() if near is None else (near,)))


def prep_grads_kernel(pitch, width, at_ref, own, other, near, send0, send1, packed):
    seqs, steps, block = own.shape
    lane = pl.program_id(0) * block + lax.broadcasted_iota(jnp.int32, (1, block), 1)
    for part in (own, other):
        for s in range(seqs):
            packed[s * pitch : s * pitch + steps, :] = part[s].astype(f32)
            packed[s * pitch + steps : (s + 1) * pitch, :] = jnp.zeros((pitch - steps, block), f32)
        value = jnp.where(lane < width, packed[...], 0.0).astype(bf16)
        if part is own:
            near[...] = value
        else:
            cut = pl.num_programs(0) // 2

            @pl.when(pl.program_id(0) < cut)
            def _():
                send0[...] = value

            @pl.when(pl.program_id(0) >= cut)
            def _():
                send1[...] = value


def prep_grads(grads, places, seqs, pitch, half):
    _, steps, width = grads.shape
    rows = seqs * pitch
    out = pl.BlockSpec((rows, BLOCK), lambda j, at: (0, j))
    cut = half // BLOCK // 2
    first = pl.BlockSpec((rows, BLOCK), lambda j, at: (0, held(j, 0, cut)))
    second = pl.BlockSpec((rows, BLOCK), lambda j, at: (0, held(j, cut, cut)))
    return pl.pallas_call(
        without(functools.partial(prep_grads_kernel, pitch, width), 0, 0, -2),
        grid_spec=pltpu.PrefetchScalarGridSpec(
            num_scalar_prefetch=1,
            grid=(half // BLOCK,),
            in_specs=[
                pl.BlockSpec((seqs, steps, BLOCK), lambda j, at: (at[0], 0, j)),
                pl.BlockSpec((seqs, steps, BLOCK), lambda j, at: (at[1], 0, j)),
            ],
            out_specs=[out, first, second, token_spec],
            scratch_shapes=[pltpu.VMEM((rows, BLOCK), f32)],
        ),
        out_shape=[jax.ShapeDtypeStruct((rows, half), bf16)]
        + [jax.ShapeDtypeStruct((rows, half // 2), bf16)] * 2
        + [token_shape],
        compiler_params=params(),
        name="prep_grads",
    )(places, grads, grads)


def combine_kernel(pitch, counts, at_ref, *refs):
    *parts, out = refs
    seqs, steps, width = out.shape

    def put(a, b):
        a, b = (jnp.concatenate([part[...].astype(f32) for part in x], axis=1) for x in (a, b))
        total = a + b
        for s in range(seqs):
            out[s] = total[s * pitch : s * pitch + steps, :width]

    near, b_near, *far = parts
    cut = counts[0]
    pl.when(pl.program_id(0) == 0)(lambda: put([near], [b_near]))
    pl.when(pl.program_id(0) == 1)(lambda: put(far[:cut], far[cut:]))


def combine(places, a_near, b_near, a_far, b_far, seqs, steps, width, deps=()):
    rows = a_near.shape[0]
    pitch = rows // seqs
    group = 2 if seqs % 2 == 0 and 2 * pitch % 16 == 0 else seqs
    nb = seqs // group
    near_at = lambda p, j, at: (jnp.where(p == 0, j, nb - 1), 0)
    far_at = lambda p, j, at: (jnp.where(p == 0, 0, j), 0)
    operands = [a_near, b_near, *a_far, *b_far]
    specs = [pl.BlockSpec((group * pitch, x.shape[1]), near_at if k < 2 else far_at) for k, x in enumerate(operands)]
    return pl.pallas_call(
        without(functools.partial(combine_kernel, pitch, [len(a_far)]), 1 + len(operands), len(deps), -1),
        grid_spec=pltpu.PrefetchScalarGridSpec(
            num_scalar_prefetch=1,
            grid=(2, nb),
            in_specs=specs + after(deps),
            out_specs=[pl.BlockSpec((group, steps, width), lambda p, j, at: (at[p] * nb + j, 0, 0)), token_spec],
        ),
        out_shape=[jax.ShapeDtypeStruct((2 * seqs, steps, width), f32), token_shape],
        compiler_params=params(24),
        name="combine",
    )(places, *operands, *deps)


def cut_kernel(pieces, chunks, limit, at_ref, second, third, out_second, out_third):
    tall, wide = out_second.shape
    j = pl.program_id(0)
    lane = lax.broadcasted_iota(jnp.int32, (tall, wide), 1)
    for block, weight, out in ((j * pieces + at_ref[j], second, out_second), (at_ref[0] * chunks + j, third, out_third)):
        row = block * tall + lax.broadcasted_iota(jnp.int32, (tall, wide), 0)
        out[...] = jnp.where((row < limit) & (lane < limit), weight[...].astype(f32), 0.0).astype(bf16)


def cut(second, third, places, chunks, pieces, half):
    tall = half // (chunks * pieces)
    out_spec = pl.BlockSpec((tall, half), lambda j, at: (j, 0))
    return pl.pallas_call(
        functools.partial(cut_kernel, pieces, chunks, second.shape[0]),
        grid_spec=pltpu.PrefetchScalarGridSpec(
            num_scalar_prefetch=1,
            grid=(chunks,),
            in_specs=[
                pl.BlockSpec((tall, half), lambda j, at: (j * pieces + at[j], 0)),
                pl.BlockSpec((tall, half), lambda j, at: (at[0] * chunks + j, 0)),
            ],
            out_specs=[out_spec, out_spec],
        ),
        out_shape=[jax.ShapeDtypeStruct((chunks * tall, half), bf16)] * 2,
        compiler_params=params(),
        name="cut",
    )(jnp.stack(places).astype(jnp.int32), second, third)


def project_kernel(parts, halves, add, nb, *refs):
    xs = refs[:parts]
    ws = [refs[parts * (1 + h) : parts * (2 + h)] for h in range(halves)]
    refs = refs[parts * (1 + halves) :]
    proj, sums = refs[-2:]
    j = pl.program_id(0)

    def go(weights):
        acc = sum(dot(x[...], w[...], ((1,), (0,))) for x, w in zip(xs, weights))
        if add:
            acc = acc + jnp.concatenate([refs[0][k] for k in range(WIDE // LANES)], axis=1)
        for k in range(WIDE // LANES):
            proj[k] = acc[:, k * LANES : (k + 1) * LANES]
        sums[0:1, :] = jnp.sum(acc, axis=0, keepdims=True)
        sums[1:2, :] = jnp.sum(acc * acc, axis=0, keepdims=True)

    for h in range(halves):
        pl.when((j >= h * nb) & (j < (h + 1) * nb))(functools.partial(go, ws[h]))


def project(xs, ws, tiles, first=0, before=None, add=False, deps=()):
    rows = xs[0][0].shape[0]
    half = ws[0][0].shape[1]
    nb = half // WIDE
    specs, operands = [], []
    for x, at, depth in xs:
        specs.append(pl.BlockSpec((rows, depth), lambda j, at=at: (0, at), pipeline_mode=pl.Buffered(1)))
        operands.append(x)
    for h, weights in enumerate(ws):
        for w, (_, _, depth) in zip(weights, xs):
            specs.append(pl.BlockSpec((depth, WIDE), lambda j, h=h: (0, held(j, h * nb, nb))))
            operands.append(w)
    tile_spec = pl.BlockSpec((WIDE // LANES, rows, LANES), lambda j: (j + first, 0, 0))
    aliases = {}
    if before is not None:
        aliases = {len(operands): 0}
        operands.append(before)
        specs.append(tile_spec if add else pl.BlockSpec(memory_space=pl.ANY))
    width = len(ws) * half
    kernel = functools.partial(project_kernel, len(xs), len(ws), add, nb)
    return pl.pallas_call(
        without(kernel, len(operands), len(deps)),
        grid=(len(ws) * nb,),
        in_specs=specs + after(deps),
        out_specs=[tile_spec, pl.BlockSpec((2, WIDE), lambda j: (0, j))],
        out_shape=[
            jax.ShapeDtypeStruct((tiles, rows, LANES), f32),
            jax.ShapeDtypeStruct((2, width), f32),
        ],
        input_output_aliases=aliases,
        compiler_params=params(),
        name="project",
    )(*operands, *deps)


def stats_of(sums, gains, count, j):
    mean = sums[0:1, tile_of(j)] / count
    var = sums[1:2, tile_of(j)] / count - mean * mean
    scale = lax.rsqrt(var + norm_eps)
    return mean, scale


def clear_pads(steps, seqs, array):
    tiles, rows, _ = array.shape
    pitch = rows // seqs
    if pitch > steps:
        for j in range(tiles):
            for s in range(seqs):
                array[j, s * pitch + steps : (s + 1) * pitch, :] = jnp.zeros((pitch - steps, LANES), f32)


def run_forward(steps, seqs, tiles, norm, gains, states, slopes):
    recur = [jnp.broadcast_to(gains[2:3, tile_of(j)], (seqs, LANES)) for j in range(tiles)]
    pitch = norm.shape[1] // seqs

    def advance(t, before):
        now = []
        at = pl.ds(t, seqs, stride=pitch)
        for j in range(tiles):
            arg = norm[j, at, :] + recur[j] * before[j]
            poly = gelu_inner * (arg * arg) + gelu_outer
            tanh = jnp.tanh(arg * poly)
            half = 0.5 * arg
            state = half + half * tanh
            states[j, at, :] = state
            inner = 3.0 * poly - 2.0 * gelu_outer
            slopes[j, at, :] = (0.5 * tanh + 0.5) + half * (1.0 - tanh * tanh) * inner
            now.append(state)
        return tuple(now)

    unroll = 2 if steps % 2 == 0 else 1

    def several(i, before):
        for k in range(unroll):
            before = advance(i * unroll + k, before)
        return before

    zero = jnp.zeros((seqs, LANES), f32)
    lax.fori_loop(0, steps // unroll, several, (zero,) * tiles)
    clear_pads(steps, seqs, states)


def run_backward(steps, seqs, tiles, grads, gains, slopes, arg_grads):
    recur = [jnp.broadcast_to(gains[2:3, tile_of(j)], (seqs, LANES)) for j in range(tiles)]
    pitch = arg_grads.shape[1] // seqs

    def retreat(t, after):
        now = []
        at = pl.ds(t, seqs, stride=pitch)
        for j in range(tiles):
            grad = (grads[j, at, :] + recur[j] * after[j]) * slopes[j, at, :]
            arg_grads[j, at, :] = grad
            now.append(grad)
        return tuple(now)

    unroll = 2 if steps % 2 == 0 else 1

    def several(i, after):
        for k in range(unroll):
            after = retreat(steps - 1 - (i * unroll + k), after)
        return after

    zero = jnp.zeros((seqs, LANES), f32)
    lax.fori_loop(0, steps // unroll, several, (zero,) * tiles)
    clear_pads(steps, seqs, arg_grads)


def back_sums(tiles, arg_grads, proj, states, sums, gains, count, out, shifted):
    rows = proj.shape[1]
    for j in range(tiles):
        mean, scale = stats_of(sums, gains, count, j)
        grad = arg_grads[j]
        out[0:1, tile_of(j)] = scale * jnp.sum(grad * (proj[j] - mean), axis=0, keepdims=True)
        out[1:2, tile_of(j)] = jnp.sum(grad, axis=0, keepdims=True)
        shifted[...] = states(j)
        out[2:3, tile_of(j)] = jnp.sum(
            arg_grads[j, 1:rows, :] * shifted[0 : rows - 1, :], axis=0, keepdims=True
        )


def make_norm(tiles, proj, sums, gains, count, norm):
    for j in tiles:
        mean, scale = stats_of(sums, gains, count, j)
        norm[j] = (proj[j] - mean) * (gains[0:1, tile_of(j)] * scale) + gains[1:2, tile_of(j)]


def load_norm(parts, proj_hbm, proj, sems, sums, gains, count, norm):
    tiles = proj.shape[0]
    size = tiles // parts
    copies = [
        pltpu.make_async_copy(proj_hbm.at[pl.ds(k * size, size)], proj.at[pl.ds(k * size, size)], sems.at[k])
        for k in range(parts)
    ]
    for copy in copies:
        copy.start()

    def finish():
        for k, copy in enumerate(copies):
            copy.wait()
            make_norm(range(k * size, (k + 1) * size), proj, sums, gains, count, norm)

    return finish


parts_in = 4


def first_layer_kernel(
    steps, seqs, count, proj_hbm, sums, gains, top_hbm, bottom_hbm,
    hidden, slopes_hbm, totals, proj_out, moments,
    proj, norm, states, slopes, top, bottom, sems, out_sems,
):
    tiles, rows, _ = proj.shape
    half = tiles * LANES // 2
    finish = load_norm(parts_in, proj_hbm, proj, sems, sums, gains, count, norm)
    weights = [
        pltpu.make_async_copy(top_hbm, top, sems.at[parts_in]),
        pltpu.make_async_copy(bottom_hbm, bottom, sems.at[parts_in + 1]),
    ]
    for copy in weights:
        copy.start()
    finish()
    run_forward(steps, seqs, tiles, norm, gains, states, slopes)
    keep = pltpu.make_async_copy(slopes, slopes_hbm, out_sems.at[0])
    keep.start()
    for j in range(tiles):
        hidden[:, tile_of(j)] = states[j].astype(bf16)
        totals[0:1, tile_of(j)] = jnp.sum(states[j], axis=0, keepdims=True)
    for copy in weights:
        copy.wait()
    sends = []
    for k in range(half // WIDE):
        lanes = pl.ds(k * WIDE, WIDE)
        acc = dot(hidden[:, :half], top[:, lanes], ((1,), (0,))) + dot(hidden[:, half:], bottom[:, lanes], ((1,), (0,)))
        moments[0:1, lanes] = jnp.sum(acc, axis=0, keepdims=True)
        moments[1:2, lanes] = jnp.sum(acc * acc, axis=0, keepdims=True)
        size = WIDE // LANES
        for i in range(size):
            norm[k * size + i] = acc[:, i * LANES : (i + 1) * LANES]
        place = pl.ds(k * size, size)
        sends.append(pltpu.make_async_copy(norm.at[place], proj_out.at[place], out_sems.at[1 + k]))
        sends[-1].start()
    for copy in [keep, *sends]:
        copy.wait()


def first_layer(steps, seqs, count, proj, sums, gains, top, bottom):
    tiles, rows, _ = proj.shape
    width = tiles * LANES
    half = width // 2
    vmem, hbm = pl.BlockSpec(memory_space=pltpu.VMEM), pl.BlockSpec(memory_space=pl.ANY)
    tiled = pltpu.VMEM((tiles, rows, LANES), f32)
    return pl.pallas_call(
        functools.partial(first_layer_kernel, steps, seqs, count),
        in_specs=[hbm, vmem, vmem, hbm, hbm],
        out_specs=[vmem, hbm, vmem, hbm, vmem],
        out_shape=[
            jax.ShapeDtypeStruct((rows, width), bf16),
            jax.ShapeDtypeStruct((tiles, rows, LANES), f32),
            jax.ShapeDtypeStruct((1, width), f32),
            jax.ShapeDtypeStruct((tiles, rows, LANES), f32),
            jax.ShapeDtypeStruct((2, half), f32),
        ],
        scratch_shapes=[tiled] * 4
        + [pltpu.VMEM((half, half), bf16)] * 2
        + [pltpu.SemaphoreType.DMA((parts_in + 2,)), pltpu.SemaphoreType.DMA((1 + half // WIDE,))],
        compiler_params=params(),
        name="first_layer",
    )(proj, sums, gains, top, bottom)


def second_layer_kernel(
    steps, seqs, count, proj_hbm, sums, gains, near_hbm, far_hbm0, far_hbm1,
    near_out, far_out0, far_out1, grads_out, out,
    proj, norm, states, slopes, near, far, shifted, sems, out_sems,
):
    tiles, rows, _ = proj.shape
    half = tiles // 2
    cut = far.shape[1] // 2
    finish = load_norm(parts_in, proj_hbm, proj, sems, sums, gains, count, norm)
    upstream = [
        pltpu.make_async_copy(near_hbm, near, sems.at[parts_in]),
        pltpu.make_async_copy(far_hbm0, far.at[:, :cut], sems.at[parts_in + 1]),
        pltpu.make_async_copy(far_hbm1, far.at[:, cut:], sems.at[parts_in + 2]),
    ]
    for copy in upstream:
        copy.start()
    finish()
    run_forward(steps, seqs, tiles, norm, gains, states, slopes)
    for copy in upstream:
        copy.wait()
    for j in range(half):
        for part, at in ((near, j), (far, half + j)):
            norm[at] = part[:, tile_of(j)].astype(f32)
            part[:, tile_of(j)] = states[at].astype(bf16)
    sends = [
        pltpu.make_async_copy(near, near_out, out_sems.at[0]),
        pltpu.make_async_copy(far.at[:, :cut], far_out0, out_sems.at[1]),
        pltpu.make_async_copy(far.at[:, cut:], far_out1, out_sems.at[2]),
        pltpu.make_async_copy(norm, grads_out, out_sems.at[3]),
    ]
    for copy in sends[:3]:
        copy.start()
    run_backward(steps, seqs, tiles, norm, gains, slopes, norm)
    sends[3].start()
    back_sums(tiles, norm, proj, lambda j: states[j], sums, gains, count, out, shifted)
    for copy in sends:
        copy.wait()


def second_layer(steps, seqs, count, proj, sums, gains, cot_near, cot_far):
    tiles, rows, _ = proj.shape
    width = tiles * LANES
    vmem, hbm = pl.BlockSpec(memory_space=pltpu.VMEM), pl.BlockSpec(memory_space=pl.ANY)
    low = jax.ShapeDtypeStruct((rows, width // 2), bf16)
    low_half = jax.ShapeDtypeStruct((rows, width // 4), bf16)
    return pl.pallas_call(
        functools.partial(second_layer_kernel, steps, seqs, count),
        in_specs=[hbm, vmem, vmem, hbm, hbm, hbm],
        out_specs=[hbm, hbm, hbm, hbm, vmem],
        out_shape=[low, low_half, low_half, jax.ShapeDtypeStruct((tiles, rows, LANES), f32), jax.ShapeDtypeStruct((3, width), f32)],
        scratch_shapes=[pltpu.VMEM((tiles, rows, LANES), f32)] * 4
        + [pltpu.VMEM((rows, width // 2), bf16)] * 2
        + [
            pltpu.VMEM((rows, LANES), f32),
            pltpu.SemaphoreType.DMA((parts_in + 3,)),
            pltpu.SemaphoreType.DMA((4,)),
        ],
        compiler_params=params(),
        name="second_layer",
    )(proj, sums, gains, cot_near, *cot_far)


def first_back_kernel(
    steps, seqs, count, nb, low, w_nn, w_nf, w_fn, w_ff, slopes_hbm, hidden_hbm, proj_hbm, sums, gains,
    grads_out, out, grads, slopes, hidden, proj, shifted, sems,
):
    tiles = proj.shape[0]
    half = w_nn.shape[1]
    j = pl.program_id(0)
    copies = [
        pltpu.make_async_copy(slopes_hbm, slopes, sems.at[0]),
        pltpu.make_async_copy(hidden_hbm, hidden, sems.at[1]),
        pltpu.make_async_copy(proj_hbm, proj, sems.at[2]),
    ]

    @pl.when(j == 0)
    def _():
        for copy in copies:
            copy.start()

    def go(left, right):
        acc = dot(low[:, :half], left[...], ((1,), (1,))) + dot(low[:, half:], right[...], ((1,), (1,)))
        for k in range(WIDE // LANES):
            grads[j * (WIDE // LANES) + k] = acc[:, k * LANES : (k + 1) * LANES]

    pl.when(j < nb)(functools.partial(go, w_nn, w_nf))
    pl.when((j >= nb) & (j < 2 * nb))(functools.partial(go, w_fn, w_ff))

    @pl.when(j == 2 * nb)
    def _():
        for copy in copies:
            copy.wait()
        run_backward(steps, seqs, tiles, grads, gains, slopes, grads)
        send = pltpu.make_async_copy(grads, grads_out, sems.at[3])
        send.start()
        states = lambda k: hidden[:, tile_of(k)].astype(f32)
        back_sums(tiles, grads, proj, states, sums, gains, count, out, shifted)
        send.wait()


def first_back(steps, seqs, count, low, quarters, slopes, hidden, proj, sums, gains, deps=()):
    tiles, rows, _ = proj.shape
    width = tiles * LANES
    half = width // 2
    nb = half // WIDE
    hbm = pl.BlockSpec(memory_space=pl.ANY)
    weights = [pl.BlockSpec((WIDE, half), lambda j, k=k: (held(j, k // 2 * nb, nb), 0)) for k in range(4)]
    return pl.pallas_call(
        without(functools.partial(first_back_kernel, steps, seqs, count, nb), 10, len(deps)),
        grid=(2 * nb + 1,),
        in_specs=[whole((rows, width)), *weights, hbm, hbm, hbm, whole((2, width)), whole((3, width))] + after(deps),
        out_specs=[hbm, pl.BlockSpec((3, width), lambda j: (0, 0))],
        out_shape=[
            jax.ShapeDtypeStruct((tiles, rows, LANES), f32),
            jax.ShapeDtypeStruct((3, width), f32),
        ],
        scratch_shapes=[
            pltpu.VMEM((tiles, rows, LANES), f32),
            pltpu.VMEM((tiles, rows, LANES), f32),
            pltpu.VMEM((rows, width), bf16),
            pltpu.VMEM((tiles, rows, LANES), f32),
            pltpu.VMEM((rows, LANES), f32),
            pltpu.SemaphoreType.DMA((4,)),
        ],
        compiler_params=params(),
        name="first_back",
    )(low, *quarters, slopes, hidden, proj, sums, gains, *deps)


def norm_back(steps, seqs, arg_grads, proj, sums, gains, totals, count, low_ref, columns):
    tiles, rows, _ = proj.shape
    pitch = rows // seqs
    first = steps // 16 * 16
    row = first + lax.broadcasted_iota(jnp.int32, (16, LANES), 0)
    for j in range(tiles):
        mean, scale = stats_of(sums, gains, count, j)
        factor = gains[0:1, tile_of(j)] * scale
        shift_part = factor * totals[1:2, tile_of(j)] / count
        unit_part = factor * scale * totals[0:1, tile_of(j)] / count
        low = (factor * arg_grads[j] - shift_part - (proj[j] - mean) * unit_part).astype(bf16)
        low_ref[:, tile_of(j)] = low
        if columns is None:
            continue
        past = (mean * unit_part - shift_part).astype(bf16).astype(f32)
        column = jnp.sum(low.astype(f32), axis=0, keepdims=True) - (rows - seqs * steps) * past
        high_part = column.astype(bf16).astype(f32)
        low_part = (column - high_part).astype(bf16).astype(f32)
        columns[0:1, tile_of(j)] = high_part + low_part
        edge = low_ref[first : first + 16, tile_of(j)].astype(f32)
        edge = jnp.where(row == steps, high_part, jnp.where(row == steps + 1, low_part, edge))
        low_ref[first : first + 16, tile_of(j)] = edge.astype(bf16)


def weight_kernel(steps, seqs, count, parts, centred, norm_steps, *refs):
    xs, refs = refs[: len(parts)], refs[len(parts) :]
    if centred:
        centre, *refs = refs
    j = pl.program_id(0)
    if norm_steps:
        arg_grads, proj, sums, gains, totals, low_out, columns, left, right, low = refs

        @pl.when(j < norm_steps)
        def _():
            norm_back(steps, seqs, arg_grads, proj, sums, gains, totals, count, low_out, columns if centred else None)
            if not centred:
                columns[...] = jnp.zeros_like(columns)
            low[:, pl.ds(pl.multiple_of(j * BLOCK, BLOCK), BLOCK)] = low_out[...]
    else:
        low, left, right = refs
    half = low.shape[1] // 2

    def go(x):
        value = x[...]
        if centred:
            row = lax.broadcasted_iota(jnp.int32, value.shape, 0)
            minus = jnp.broadcast_to(-centre[...], value.shape)
            value = jnp.where((row == steps) | (row == steps + 1), minus, value.astype(f32)).astype(bf16)
        acc = dot(value, low[...], ((0,), (0,)))
        left[...] = acc[:, :half].astype(left.dtype)
        right[...] = acc[:, half:].astype(right.dtype)

    at = norm_steps
    for x, blocks in zip(xs, parts):
        pl.when((j >= at) & (j < at + blocks))(functools.partial(go, x))
        at += blocks


def weight_grad(steps, seqs, count, xs, grads, centre=None, centre_at=0, deps=()):
    rows = grads[0].shape[-2]
    made = len(grads) == 1
    width = grads[0].shape[1] if made else grads[0].shape[0] * LANES
    half = width // 2
    nb = half // WIDE
    norm_steps = 0 if made else width // BLOCK
    specs, start = [], norm_steps
    for _, first, blocks in xs:
        specs.append(
            pl.BlockSpec((rows, WIDE), lambda j, start=start, first=first, blocks=blocks: (0, first + held(j, start, blocks)))
        )
        start += blocks
    operands = [x for x, _, _ in xs]
    if centre is not None:
        specs.append(pl.BlockSpec((1, WIDE), lambda j: (0, centre_at + held(j, norm_steps, nb))))
        operands.append(centre)
    quarter = pl.BlockSpec((WIDE, half), lambda j: (held(j, norm_steps, nb), 0))
    out_specs, out_shape, scratch = [quarter] * 2, [jax.ShapeDtypeStruct((half, half), bf16)] * 2, []
    if made:
        specs.append(whole((rows, width)))
    else:
        tile_spec = pl.BlockSpec((BLOCK // LANES, rows, LANES), lambda j: (held(j, 0, norm_steps), 0, 0))
        lanes = lambda tall: pl.BlockSpec((tall, BLOCK), lambda j: (0, held(j, 0, norm_steps)))
        specs += [tile_spec, tile_spec, lanes(2), lanes(3), lanes(3)]
        out_specs = [lanes(rows), lanes(1)] + out_specs
        out_shape = [jax.ShapeDtypeStruct((rows, width), bf16), jax.ShapeDtypeStruct((1, width), f32)] + out_shape
        scratch = [pltpu.VMEM((rows, width), bf16)]
    kernel = functools.partial(
        weight_kernel, steps, seqs, count, [b for _, _, b in xs], centre is not None, norm_steps
    )
    return pl.pallas_call(
        without(kernel, len(specs), len(deps), -1 - len(scratch)),
        grid=(norm_steps + nb,),
        in_specs=specs + after(deps),
        out_specs=out_specs + [token_spec],
        out_shape=out_shape + [token_shape],
        scratch_shapes=scratch,
        compiler_params=params(),
        name="weight_grad",
    )(*operands, *grads, *deps)


def pull_kernel(nb, tiled, low, *refs):
    *weights, out = refs
    j = pl.program_id(0)
    half = weights[0].shape[1]

    def go(left, right):
        acc = dot(low[:, :half], left[...], ((1,), (1,))) + dot(low[:, half:], right[...], ((1,), (1,)))
        if tiled:
            for k in range(WIDE // LANES):
                out[k] = acc[:, k * LANES : (k + 1) * LANES]
        else:
            out[...] = acc.astype(out.dtype)

    for k in range(len(weights) // 2):
        pl.when((j >= k * nb) & (j < (k + 1) * nb))(functools.partial(go, *weights[2 * k : 2 * k + 2]))


def pull(low, quarters, tiled, dtype, deps=()):
    rows, width = low.shape
    half = width // 2
    nb = half // WIDE
    halves = len(quarters) // 2
    specs = [pl.BlockSpec((WIDE, half), lambda j, k=k: (held(j, k // 2 * nb, nb), 0)) for k in range(2 * halves)]
    if tiled:
        out_spec = pl.BlockSpec((WIDE // LANES, rows, LANES), lambda j: (j, 0, 0))
        shape = (halves * half // LANES, rows, LANES)
    else:
        out_spec = pl.BlockSpec((rows, WIDE), lambda j: (0, j))
        shape = (rows, halves * half)
    return pl.pallas_call(
        without(functools.partial(pull_kernel, nb, tiled), 1 + len(quarters), len(deps), -1),
        grid=(halves * nb,),
        in_specs=[whole((rows, width))] + specs + after(deps),
        out_specs=[out_spec, token_spec],
        out_shape=[jax.ShapeDtypeStruct(shape, dtype), token_shape],
        compiler_params=params(),
        name="pull",
    )(low, *quarters, *deps)


def fold_kernel(counts, at_ref, *refs):
    kept, sent = refs[-2:]
    at = 0
    for k, n in enumerate(counts):
        parts = refs[at : at + 2 * n]
        kept[k] = sum(p[...].astype(f32) for p in parts[:n])
        sent[k] = sum(p[...].astype(f32) for p in parts[n:]).astype(bf16)
        at += 2 * n


def fold(mine, stacks, rows, deps=(), mebibytes=16):
    specs, operands = [], []
    width = stacks[0][0][0].shape[-1]
    lanes = width // 2
    for stack in stacks:
        for side in (0, 1):
            for array, index, base in stack:
                operands.append(array)
                specs.append(
                    pl.BlockSpec(
                        (None, rows, lanes),
                        lambda j, at, side=side, index=index, base=base: (index, base + (at[0] + side) % 2, j),
                    )
                )
    count = len(stacks)
    out_spec = pl.BlockSpec((count, rows, lanes), lambda j, at: (0, 0, j))
    kernel = functools.partial(fold_kernel, [len(stack) for stack in stacks])
    return pl.pallas_call(
        without(kernel, 1 + len(operands), len(deps), -1),
        grid_spec=pltpu.PrefetchScalarGridSpec(
            num_scalar_prefetch=1, grid=(2,), in_specs=specs + after(deps), out_specs=[out_spec, out_spec, token_spec]
        ),
        out_shape=[
            jax.ShapeDtypeStruct((count, rows, width), f32),
            jax.ShapeDtypeStruct((count, rows, width), bf16),
            token_shape,
        ],
        compiler_params=params(mebibytes),
        name="fold",
    )(jnp.reshape(mine, (1,)).astype(jnp.int32), *operands, *deps)


def total_kernel(counts, *refs):
    *parts, out = refs
    at = 0
    for k, n in enumerate(counts):
        out[k] = sum(p[...].astype(f32) for p in parts[at : at + n]).astype(bf16)
        at += n


def total(stacks, rows, deps=(), mebibytes=16):
    parts = [part for stack in stacks for part in stack]
    count, width = len(stacks), parts[0][0].shape[-1]
    lanes = width // 2
    specs = [
        pl.BlockSpec((None, rows, lanes), lambda j, index=index, block=block: (index, block, j)) for _, index, block in parts
    ]
    out, done = pl.pallas_call(
        without(functools.partial(total_kernel, [len(stack) for stack in stacks]), len(parts), len(deps), -1),
        grid=(2,),
        in_specs=specs + after(deps),
        out_specs=[pl.BlockSpec((count, rows, lanes), lambda j: (0, 0, j)), token_spec],
        out_shape=[jax.ShapeDtypeStruct((count, rows, width), bf16), token_shape],
        compiler_params=params(mebibytes),
        name="total",
    )(*[array for array, _, _ in parts], *deps)
    return out.reshape(count * rows, width), done


def join_kernel(at_ref, own, other, out):
    @pl.when(pl.program_id(0) == 0)
    def _():
        out[...] = own[...]

    @pl.when(pl.program_id(0) == 1)
    def _():
        out[...] = other[...]


def join(mine, own, other, deps=()):
    rows, width = own.shape
    spec = pl.BlockSpec((rows, width), lambda j, at: (0, 0))
    return pl.pallas_call(
        without(join_kernel, 3, len(deps), -1),
        grid_spec=pltpu.PrefetchScalarGridSpec(
            num_scalar_prefetch=1,
            grid=(2,),
            in_specs=[spec, spec] + after(deps),
            out_specs=[pl.BlockSpec((rows, width), lambda j, at: ((at[0] + j) % 2, 0)), token_spec],
        ),
        out_shape=[jax.ShapeDtypeStruct((2 * rows, width), bf16), token_shape],
        compiler_params=params(16),
        name="join",
    )(jnp.reshape(mine, (1,)).astype(jnp.int32), own, other, *deps)


def over(value, axis):
    return lax.ppermute(value, axis, [(0, 1), (1, 0)])


def across(value, bit):
    size = lax.axis_size("dp")
    return lax.ppermute(value, "dp", [(i, i ^ bit) for i in range(size)])


def dp_bits():
    return [1 << k for k in range((lax.axis_size("dp") - 1).bit_length())]


def swap_halves(value):
    half = value.shape[-1] // 2
    return jnp.concatenate([value[:, half:], value[:, :half]], axis=1)


def sum_step(value, step, swaps):
    if step not in ("col", "row"):
        return value + across(value, step)
    other = over(value, step)
    rows = [swap_halves(other[k : k + 1]) if axis == step else other[k : k + 1] for k, axis in enumerate(swaps)]
    return value + jnp.concatenate(rows, axis=0)


def on_device(
    inputs,
    w_second,
    gain_second,
    shift_second,
    recur_second,
    w_third,
    gain_third,
    shift_third,
    recur_third,
    cotangent,
):
    steps, seq_group, width = inputs.shape
    share = cotangent.shape[1]
    seqs = share // lax.axis_size("row")
    pitch = round_up(steps + 2, 8)
    rows = seqs * pitch
    half = round_up(width, 2 * BLOCK)
    nb = half // BLOCK
    tiles = 2 * half // LANES
    pieces = lax.axis_size("dp")
    count = steps * seq_group * pieces
    row, col, place = lax.axis_index("row"), lax.axis_index("col"), lax.axis_index("dp")
    bits = dp_bits()

    def turned(order):
        return sum(((place // bit) % 2) << k for k, bit in enumerate(order))


    def pad_weight(w):
        return jnp.pad(w, ((0, half - w.shape[0]), (0, half - w.shape[1])))

    def pad_params(*vectors):
        return jnp.pad(jnp.stack(vectors), ((0, 0), (0, half - width)))

    def bit_of(bit):
        return (place // bit) % 2

    chunks = 2
    spread = len(bits) > 1 and half // (chunks * pieces) >= 16
    orders = [bits[::-1], bits[:1] + bits[:0:-1]]
    places = jnp.stack([col * share + row * seqs, col * share + (1 - row) * seqs]).astype(jnp.int32)
    parts = jnp.stack([row, 1 - row]).astype(jnp.int32)
    own_second = pad_params(gain_second, shift_second, recur_second)
    own_third = pad_params(gain_third, shift_third, recur_third)
    gains_second = jnp.concatenate([own_second, over(own_second, "col")], axis=1)
    gains_third = jnp.concatenate([own_third, over(own_third, "row")], axis=1)
    nn2, nn3 = pad_weight(w_second), pad_weight(w_third)
    nf2, fn3 = over(nn2, "col"), over(nn3, "col")
    deps = ()
    if spread:
        cut_second, cut_third = cut(w_second, w_third, [turned(order) for order in orders], chunks, pieces, half)
        tall = half // (chunks * pieces)
        far_second, far_third = over(cut_second, "row"), over(cut_third, "row")
        deps = (cut_second, cut_third)
    x_near, send0 = prep(inputs, places, seqs, pitch, half, 0, nb // 2, None, deps)
    x_near, send1 = prep(inputs, places, seqs, pitch, half, nb // 2, nb // 2, x_near)
    if spread:
        send0, send1, far_second, far_third, gains_second, gains_third = lax.optimization_barrier(
            (send0, send1, far_second, far_third, gains_second, gains_third)
        )
    x_far0 = over(send0, "row")
    x_far1 = over(send1, "row")
    proj_second, near_done = project([(x_near, 0, half)], [[nn2], [nf2]], tiles)
    cot_near, cot_send0, cot_send1, cot_done = prep_grads(jnp.transpose(cotangent, (1, 0, 2)), parts, seqs, pitch, half)
    if spread:
        fn2 = [far_second[k * tall : (k + 1) * tall] for k in range(chunks)]
        nf3 = far_third
        deps = (near_done,)
        for k in range(len(bits)):
            others = [across(piece, order[k]) for piece, order in zip(fn2, orders)]
            if k > 0:
                nf3_other = across(nf3, orders[0][k - 1])
            joined = [join(bit_of(order[k]), piece, other, deps) for piece, order, other in zip(fn2, orders, others)]
            fn2 = [piece for piece, _ in joined]
            if k == len(bits) - 1:
                break
            deps = (cot_done,)
            if k > 0:
                nf3, done = join(bit_of(orders[0][k - 1]), nf3, nf3_other, tuple(done for _, done in joined))
                deps = (done,)
            if k == len(bits) - 2:
                x_far0, *fn2 = lax.optimization_barrier((x_far0, *fn2))
        x_far1, *fn2 = lax.optimization_barrier((x_far1, *fn2))
    else:
        far = over(nn2, "row")
        fn2 = [far[: half // 2], far[half // 2 :]]
        nf3 = over(nn3, "row")
    ff2 = [over(chunk, "col") for chunk in fn2]
    x_parts = [(x_far0, 0, half // 2), (x_far1, 0, half // 2)]
    proj_second, sums_near = project(x_parts, [fn2], tiles, 0, proj_second, True, (cot_done, nn3))
    proj_second, sums_far = project(x_parts, [ff2], tiles, half // WIDE, proj_second, True)
    sums = jnp.concatenate([sums_near, sums_far], axis=1)
    if spread:
        nf3, done = join(bit_of(bits[1]), nf3, nf3_other, (sums,))
        sums, done = lax.optimization_barrier((sums, done))

    swaps = ("col", "col")
    sums = sum_step(sums, "row", swaps)
    sums, cot_send0, cot_send1 = lax.optimization_barrier((sums, cot_send0, cot_send1))
    cot_far0, cot_far1 = over(cot_send0, "row"), over(cot_send1, "row")
    if spread:
        sums = sum_step(sums, bits[0], swaps)
        sums, nf3 = lax.optimization_barrier((sums, nf3))
        nf3_other = across(nf3, bits[0])
    sums = sum_step(sums, "col", swaps)
    for bit in bits[1:] if spread else bits:
        sums = sum_step(sums, bit, swaps)
    sums_second, cot_far0 = lax.optimization_barrier((sums, cot_far0))
    hidden, slopes_second, hidden_sums, proj_third, sums_near = first_layer(
        steps, seqs, count, proj_second, sums_second, gains_second, nn3, fn3
    )
    if spread:
        nf3, done = join(bit_of(bits[0]), nf3, nf3_other, (hidden_sums,))
    ff3 = over(nf3, "col")
    hidden_parts = [(hidden, 0, half), (hidden, 1, half)]
    proj_third, sums_far = project(
        hidden_parts, [[nf3, ff3]], tiles, half // WIDE, proj_third, False
    )

    swaps = ("row", "row", "col")
    sums = jnp.concatenate([jnp.concatenate([sums_near, sums_far], axis=1), hidden_sums], axis=0)
    for step in ("col", *bits):
        sums = sum_step(sums, step, swaps)
    sums, cot_far1 = lax.optimization_barrier((sums, cot_far1))
    sums = sum_step(sums, "row", swaps)
    sums_third, centre = sums[:2], (sums[2:3] / count).astype(bf16).astype(f32)
    states_near, out_send0, out_send1, arg_grads_third, sums = second_layer(
        steps, seqs, count, proj_third, sums_third, gains_third, cot_near, (cot_far0, cot_far1)
    )
    swaps = ("row", "row", "row")
    sums = sum_step(sums, "col", swaps)
    sums = sum_step(sums, "row", swaps)
    sums, out_send0 = lax.optimization_barrier((sums, out_send0))
    out_far0 = over(out_send0, "row")
    for bit in bits:
        sums = sum_step(sums, bit, swaps)
    totals_third = sums

    wide = half // WIDE
    cutting = half // 2
    grads = (arg_grads_third, proj_third, sums_third, gains_third, totals_third)
    low_third, columns, fn, ff, _ = weight_grad(steps, seqs, count, [(hidden, wide, wide)], grads, centre, wide)
    from_fn, from_ff = over(fn, "col"), over(ff, "col")
    nn, nf, done = weight_grad(steps, seqs, count, [(hidden, 0, wide)], (low_third,), centre, 0)

    def begin_across(nn, from_fn, nf, from_ff, deps):
        own, other = [(nn[None], 0), (from_fn[None], 0)], [(nf[None], 0), (from_ff[None], 0)]
        tall = cutting // 2
        stacks = [[(array, index, 2) for array, index in part] for part in (own, other)]
        return fold(bit_of(bits[0]), stacks, tall, deps, 56)

    class Chain:
        def __init__(self, stacks, rows, left):
            self.stacks, self.rows, self.left = stacks, rows, list(left)

        def step(self, deps):
            bit = self.left.pop(0)
            self.rows //= 2
            stacks = [[(array, index, 0) for array, index in stack] for stack in self.stacks]
            kept, sent, done = fold(bit_of(bit), stacks, self.rows, deps)
            other = across(sent, bit)
            self.stacks = [[(kept, k), (other, k)] for k in range(len(stacks))]
            return (done,)

        def piece(self, deps):
            while self.left:
                deps = self.step(deps)
            stacks = [[(array, index, 0) for array, index in stack] for stack in self.stacks]
            self.whole, done = total(stacks, self.rows, deps)
            self.back = list(reversed(bits))
            self.other = across(self.whole, self.back[0])
            return (done,)

        def gather(self, deps):
            bit = self.back.pop(0)
            self.whole, done = join(bit_of(bit), self.whole, self.other, deps)
            if self.back:
                self.other = across(self.whole, self.back[0])
            return (done,)

    x3, done = total([[(nf[None], 0, 0), (from_ff[None], 0, 0)]], cutting, (done,), 56)
    x3_come = over(x3, "row")
    kept, sent, done = begin_across(nn, from_fn, nf, from_ff, (done,))
    b3_kept, b3_other = kept, across(sent, bits[0])
    arg_grads_second, sums = first_back(
        steps, seqs, count, low_third, [nn3, nf3, fn3, ff3], slopes_second, hidden, proj_second, sums_second, gains_second,
        (done, out_far0),
    )
    swaps = ("col", "col", "col", "row")
    sums = jnp.concatenate([sums, columns], axis=0)
    sums, b3_other, x3_come = lax.optimization_barrier((sums, b3_other, x3_come))
    sums = sum_step(sums, "col", swaps)
    sums = sum_step(sums, "row", swaps)
    sums, b3_other = lax.optimization_barrier((sums, b3_other))

    def to_row(kept, other, deps):
        sent, done = total([[(kept, 1, 0), (other, 1, 0)]], cutting // 2, deps)
        return over(sent, "row")[None], done

    def to_across(nn, from_other, come, deps):
        stack = [(nn[None], 0, 0), (from_other[None], 0, 0), (come[None], 0, 0)]
        kept, sent, done = fold(bit_of(bits[0]), [stack], cutting // 2, deps, 56)
        return [(kept, 0), (across(sent, bits[0]), 0)], done

    b3_row, done = to_row(b3_kept, b3_other, ())
    sums = sum_step(sums, bits[0], swaps)
    sums, x3_come = lax.optimization_barrier((sums, x3_come))
    a3, done = to_across(nn, from_fn, x3_come, (done,))
    for bit in bits[1:]:
        sums = sum_step(sums, bit, swaps)
    totals_second, columns = sums[:3], sums[3:4]
    c3 = Chain([a3, [(b3_kept, 0), (b3_other, 0), (b3_row, 0)]], cutting // 2, bits[1:])
    totals_second, done = lax.optimization_barrier((totals_second, done))
    seen = c3.step((done,))

    grads = (arg_grads_second, proj_second, sums_second, gains_second, totals_second)
    low_second, seen, fn, ff, _ = weight_grad(steps, seqs, count, [(x_far0, 0, 1), (x_far1, 0, 1)], grads, deps=seen)
    from_ff = over(ff, "col")
    seen = c3.step((seen,)) if c3.left else (seen,)
    nn, nf, done = weight_grad(steps, seqs, count, [(x_near, 0, wide)], (low_second,), deps=seen)
    from_nf = over(nf, "col")
    x2, done = total([[(fn[None], 0, 0), (from_ff[None], 0, 0)]], cutting, (done,), 56)
    x2_come = over(x2, "row")
    kept, sent, done = begin_across(nn, from_nf, fn, from_ff, (done,))
    b2_kept, b2_other = kept, across(sent, bits[0])
    far_rows = [jnp.concatenate(fn2, axis=0), jnp.concatenate(ff2, axis=0)]
    grad_far, done = pull(low_second, far_rows, False, bf16, (done,))
    seen = c3.piece((done,))
    b2_row, done = to_row(b2_kept, b2_other, seen)
    a2, done = to_across(nn, from_nf, x2_come, (done,))
    seen = c3.gather((done,))
    grad_near, done = pull(low_second, [nn2, nf2], False, f32, seen)
    seen = (done,)
    b2 = Chain([[(b2_kept, 0), (b2_other, 0), (b2_row, 0)]], cutting // 2, bits[1:])
    seen = b2.step(seen)
    grad_far, done = lax.optimization_barrier((grad_far, *seen))
    grad_far = over(grad_far, "row")
    a2 = Chain([a2], cutting // 2, bits[1:])
    seen = a2.step((done,))
    out_send1, done = lax.optimization_barrier((out_send1, *seen))
    out_far1 = over(out_send1, "row")
    seen = c3.gather((done,)) if c3.back else (done,)
    seen = b2.step(seen) if b2.left else seen
    seen = a2.step(seen) if a2.left else seen
    seen = b2.piece(seen)
    seen = c3.gather(seen) if c3.back else seen
    seen = a2.piece(seen)
    seen = b2.gather(seen)
    seen = a2.gather(seen)
    seen = b2.gather(seen)
    seen = a2.gather(seen)
    grad_inputs, done = combine(
        parts, cot_near, grad_near, (cot_send0, cot_send1), (grad_far,), seqs, steps, width, seen
    )
    output, done = combine(
        parts, x_near, states_near, (send0, send1), (out_far0, out_far1), seqs, steps, width, (done,)
    )
    seen = (done,)
    chains = [c3, b2, a2]
    while any(chain.back for chain in chains):
        for chain in chains:
            if chain.back:
                seen = chain.gather(seen)
    grad_w_third = jnp.transpose(c3.whole.reshape(pieces, 2, -1, half), (1, 0, 2, 3)).reshape(half, half)
    grad_w_second = jnp.concatenate([a2.whole, b2.whole], axis=0)

    output = jnp.transpose(output, (1, 0, 2))
    grad_inputs = jnp.transpose(grad_inputs, (1, 0, 2))
    restore = centre[0, :width, None] * columns[0, None, :width]
    return (
        output,
        grad_inputs,
        grad_w_second[:width, :width].astype(f32),
        totals_second[0, :width],
        totals_second[1, :width],
        totals_second[2, :width],
        grad_w_third[:width, :width].astype(f32) + restore,
        totals_third[0, :width],
        totals_third[1, :width],
        totals_third[2, :width],
    )


def solution(mesh):
    in_specs = (
        P(None, "dp", "row"),
        P("row", "col"),
        P("col"),
        P("col"),
        P("col"),
        P("col", "row"),
        P("row"),
        P("row"),
        P("row"),
        P(None, ("dp", "col"), "row"),
    )
    out_specs = (
        P(None, ("dp", "col"), "row"),
        P(None, ("dp", "col"), "row"),
        P("row", "col"),
        P("col"),
        P("col"),
        P("col"),
        P("col", "row"),
        P("row"),
        P("row"),
        P("row"),
    )
    return jax.shard_map(
        on_device, mesh=mesh, in_specs=in_specs, out_specs=out_specs, check_vma=False
    )
```

profile of v0, /device:TPU:0, one launch (start us, length us, event | category | flops | bytes accessed | tf_op | source)
XLA Modules:
  0.0 469.5 jit_solution(16930079401336675976)
XLA Ops:
  6.2 2.6 collective-permute-start
  11.6 4.7 prep.2
  16.3 4.8 %prep.3 = (bf16[912,1024]{1,0:T(8,128)(2,1)}, bf16[912,512]{1,0:T(8,128)(2,1)}) custom-call(s32[2]{0:T(128)} %pad_add_fusion.1.refs_0_, bf16[150,24,1000]{2,1,0:T(8,128)(2,1)} %refs_1_.3, bf16[912,1024]{1,0:T(8,128)(2,1)} %get-tuple-element.173.refs_2_), custom_call_target="tpu_custom_call", output_to_operand_aliasing={{0}: (2, {})} | custom-call | tf_op jit(solution)/shard_map/prep/pallas_call | solution.py:81
  27.4 2.6 collective-permute-start.5
  30.0 8.8 %project.4 = (f32[16,912,128]{2,1,0:T(8,128)}, f32[2,2048]{1,0:T(2,128)}) custom-call(bf16[912,1024]{1,0:T(8,128)(2,1)} %get-tuple-element.174.refs_0_.refs_1_, bf16[1024,1024]{1,0:T(8,128)(2,1)} %copy-done.37, bf16[1024,1024]{1,0:T(8,128)(2,1)} %collective-permute-done.6.refs_2_), custom_call_target="tpu_custom_call" | custom-call | tf_op jit(solution)/shard_map/project/pallas_call | solution.py:259
  43.3 5.8 %prep_grads.1 = (bf16[912,1024]{1,0:T(8,128)(2,1)}, bf16[912,512]{1,0:T(8,128)(2,1)}, bf16[912,512]{1,0:T(8,128)(2,1)}, f32[8,128]{1,0:T(8,128)}) custom-call(s32[2]{0:T(128)} %pad_add_fusion.refs_0_, bf16[12,150,1000]{2,1,0:T(8,128)(2,1)} %bitcast.89, bf16[12,150,1000]{2,1,0:T(8,128)(2,1)} %bitcast.90), custom_call_target="tpu_custom_call" | custom-call | tf_op jit(solution)/shard_map/prep_grads/pallas_call | solution.py:131
  49.1 4.5 collective-permute-done.9.refs_2_
  55.1 3.0 collective-permute-start.12
  58.1 12.9 %collective-permute-done.12.refs_2_ = bf16[128,1024]{1,0:T(8,128)(2,1)S(1)} collective-permute-done((bf16[128,1024]{1,0:T(8,128)(2,1)S(1)}, bf16[128,1024]{1,0:T(8,128)(2,1)S(1)}, u32[]{:S(2)}, u32[]{:S(2)}) %collective-permute-start.12) | collective-permute-done | bytes 262176 | tf_op jit(solution)/shard_map/ppermute | solution.py:822
  77.8 6.2 %project.5 = (f32[16,912,128]{2,1,0:T(8,128)}, f32[2,1024]{1,0:T(2,128)}) custom-call(bf16[912,512]{1,0:T(8,128)(2,1)} %copy-done.39, bf16[912,512]{1,0:T(8,128)(2,1)} %copy-done.40, bf16[512,1024]{1,0:T(8,128)(2,1)} %copy-done.6, bf16[512,1024]{1,0:T(8,128)(2,1)} %copy-done.8, ...), custom_call_target="tpu_custom_call", output_to_operand_aliasing={{0}: (4, {})} | custom-call | tf_op jit(solution)/shard_map/project/pallas_call | solution.py:259
  85.7 6.4 %project.6 = (f32[16,912,128]{2,1,0:T(8,128)}, f32[2,1024]{1,0:T(2,128)}) custom-call(bf16[912,512]{1,0:T(8,128)(2,1)} %copy-done.39, bf16[912,512]{1,0:T(8,128)(2,1)} %copy-done.40, bf16[512,1024]{1,0:T(8,128)(2,1)} %copy-done.44, bf16[512,1024]{1,0:T(8,128)(2,1)} %collective-permute-done.15.refs_3_, ...), custom_call_target="tpu_custom_call", output_to_operand_aliasing={{0}: (4, {})} | custom-call | tf_op jit(solution)/shard_map/project/pallas_call | solution.py:259
  104.3 3.0 collective-permute-done.20
  108.2 3.8 collective-permute-done.21
  112.6 11.0 %collective-permute-done.22.far_hbm0 = bf16[912,512]{1,0:T(8,128)(2,1)S(1)} collective-permute-done((bf16[912,512]{1,0:T(8,128)(2,1)S(1)}, bf16[912,512]{1,0:T(8,128)(2,1)S(1)}, u32[]{:S(2)}, u32[]{:S(2)}) %collective-permute-start.22) | collective-permute-done | bytes 933920 | tf_op jit(solution)/shard_map/ppermute | solution.py:817
  123.6 21.1 %first_layer.1 = (bf16[912,2048]{1,0:T(8,128)(2,1)}, f32[16,912,128]{2,1,0:T(8,128)}, f32[1,2048]{1,0:T(1,128)}, f32[16,912,128]{2,1,0:T(8,128)}, f32[2,1024]{1,0:T(2,128)}) custom-call(f32[16,912,128]{2,1,0:T(8,128)} %get-tuple-element.200.proj_hbm.refs_7_.refs_3_, f32[2,2048]{1,0:T(2,128)} %add.146.sums.refs_8_.refs_4_, ...), custom_call_target="tpu_custom_call" | custom-call | tf_op jit(solution)/shard_map/first_layer/pallas_call | solution.py:431
  147.7 2.7 collective-permute-done.25.refs_3_.refs_4_
  151.9 8.2 %project.7 = (f32[16,912,128]{2,1,0:T(8,128)}, f32[2,1024]{1,0:T(2,128)}) custom-call(bf16[912,2048]{1,0:T(8,128)(2,1)} %get-tuple-element.212.refs_0_.refs_1_.refs_6_, bf16[912,2048]{1,0:T(8,128)(2,1)} %get-tuple-element.212.refs_0_.refs_1_.refs_6_, bf16[1024,1024]{1,0:T(8,128)(2,1)} %copy-done.3, ...), custom_call_target="tpu_custom_call", output_to_operand_aliasing={{0}: (4, {})} | custom-call | tf_op jit(solution)/shard_map/project/pallas_call | solution.py:259
  167.7 3.2 collective-permute-done.28
  171.8 4.3 collective-permute-done.29
  177.5 2.6 collective-permute-done.31
  180.8 22.6 %second_layer.1 = (bf16[912,1024]{1,0:T(8,128)(2,1)}, bf16[912,512]{1,0:T(8,128)(2,1)}, bf16[912,512]{1,0:T(8,128)(2,1)}, f32[16,912,128]{2,1,0:T(8,128)}, f32[3,2048]{1,0:T(4,128)}) custom-call(f32[16,912,128]{2,1,0:T(8,128)} %get-tuple-element.217.proj_hbm.refs_3_, f32[2,2048]{1,0:T(2,128)} %slice.234.sums.refs_4_, ...), custom_call_target="tpu_custom_call" | custom-call | tf_op jit(solution)/shard_map/second_layer/pallas_call | solution.py:495
  207.1 2.6 collective-permute-done.33
  214.3 3.4 collective-permute-done.36
  219.0 4.0 collective-permute-done.37
  223.6 17.1 %weight_grad.4 = (bf16[912,2048]{1,0:T(8,128)(2,1)}, f32[1,2048]{1,0:T(1,128)}, bf16[1024,1024]{1,0:T(8,128)(2,1)}, bf16[1024,1024]{1,0:T(8,128)(2,1)}, f32[8,128]{1,0:T(8,128)}) custom-call(bf16[912,2048]{1,0:T(8,128)(2,1)} %get-tuple-element.212.refs_0_.refs_1_.refs_6_, f32[1,2048]{1,0:T(1,128)} %fusion.2.refs_1_, ...), custom_call_target="tpu_custom_call" | custom-call | tf_op jit(solution)/shard_map/weight_grad/pallas_call | solution.py:668
  242.6 8.4 %weight_grad.5 = (bf16[1024,1024]{1,0:T(8,128)(2,1)}, bf16[1024,1024]{1,0:T(8,128)(2,1)}, f32[8,128]{1,0:T(8,128)}) custom-call(bf16[912,2048]{1,0:T(8,128)(2,1)} %get-tuple-element.212.refs_0_.refs_1_.refs_6_, f32[1,2048]{1,0:T(1,128)} %fusion.2.refs_1_, bf16[912,2048]{1,0:T(8,128)(2,1)} %get-tuple-element.233.refs_2_.refs_0_), custom_call_target="tpu_custom_call" | custom-call | tf_op jit(solution)/shard_map/weight_grad/pallas_call | solution.py:668
  256.2 3.6 fold.10
  262.1 2.7 collective-permute-done.34.refs_11_.refs_5_
  265.7 21.3 %first_back.1 = (f32[16,912,128]{2,1,0:T(8,128)}, f32[3,2048]{1,0:T(4,128)}) custom-call(bf16[912,2048]{1,0:T(8,128)(2,1)} %get-tuple-element.233.refs_2_.refs_0_, bf16[1024,1024]{1,0:T(8,128)(2,1)} %copy-done.34, bf16[1024,1024]{1,0:T(8,128)(2,1)} %copy-done.3, bf16[1024,1024]{1,0:T(8,128)(2,1)} %collective-permute-done.23.bottom_hbm.refs_3_, ...), custom_call_target="tpu_custom_call" | custom-call | tf_op jit(solution)/shard_map/first_back/pallas_call | solution.py:557
  297.3 2.9 fold.11
  302.4 3.5 collective-permute-done.45
  306.2 4.8 %collective-permute-done.46 = f32[4,2048]{1,0:T(4,128)S(1)} collective-permute-done((f32[4,2048]{1,0:T(4,128)S(1)}, f32[4,2048]{1,0:T(4,128)S(1)}, u32[]{:S(2)}, u32[]{:S(2)}) %collective-permute-start.46) | collective-permute-done | bytes 32800 | tf_op jit(solution)/shard_map/ppermute | solution.py:822
  315.9 16.5 %weight_grad.6 = (bf16[912,2048]{1,0:T(8,128)(2,1)}, f32[1,2048]{1,0:T(1,128)}, bf16[1024,1024]{1,0:T(8,128)(2,1)}, bf16[1024,1024]{1,0:T(8,128)(2,1)}, f32[8,128]{1,0:T(8,128)}) custom-call(bf16[912,512]{1,0:T(8,128)(2,1)} %copy-done.39, bf16[912,512]{1,0:T(8,128)(2,1)} %copy-done.40, f32[16,912,128]{2,1,0:T(8,128)} %get-tuple-element.242.refs_2_, ...), custom_call_target="tpu_custom_call" | custom-call | tf_op jit(solution)/shard_map/weight_grad/pallas_call | solution.py:668
  334.3 8.4 %weight_grad.7 = (bf16[1024,1024]{1,0:T(8,128)(2,1)}, bf16[1024,1024]{1,0:T(8,128)(2,1)}, f32[8,128]{1,0:T(8,128)}) custom-call(bf16[912,1024]{1,0:T(8,128)(2,1)} %get-tuple-element.174.refs_0_.refs_1_, bf16[912,2048]{1,0:T(8,128)(2,1)} %get-tuple-element.263.refs_1_.refs_0_, f32[8,128]{1,0:T(8,128)} %copy-done.32), custom_call_target="tpu_custom_call" | custom-call | tf_op jit(solution)/shard_map/weight_grad/pallas_call | solution.py:668
  348.5 3.7 fold.14
  358.2 2.7 pad_maximum_fusion.1.refs_2_
  360.9 8.2 %pull.2 = (bf16[912,1024]{1,0:T(8,128)(2,1)}, f32[8,128]{1,0:T(8,128)}) custom-call(bf16[912,2048]{1,0:T(8,128)(2,1)} %get-tuple-element.263.refs_1_.refs_0_, bf16[1024,1024]{1,0:T(8,128)(2,1)} %pad_maximum_fusion.refs_1_, bf16[1024,1024]{1,0:T(8,128)(2,1)} %pad_maximum_fusion.1.refs_2_, f32[8,128]{1,0:T(8,128)} %get-tuple-element.279.refs_3_), custom_call_target="tpu_custom_call" | custom-call | tf_op jit(solution)/shard_map/pull/pallas_call | solution.py:709
  371.5 6.4 %collective-permute-done.53.refs_1_.refs_2_.refs_5_ = bf16[2,256,1024]{2,1,0:T(8,128)(2,1)S(1)} collective-permute-done((bf16[2,256,1024]{2,1,0:T(8,128)(2,1)}, bf16[2,256,1024]{2,1,0:T(8,128)(2,1)S(1)}, u32[]{:S(2)}, u32[]{:S(2)}) %collective-permute-start.53) | collective-permute-done | bytes 1048608 | tf_op jit(solution)/shard_map/ppermute | solution.py:822
  380.2 2.9 fold.15
  387.5 8.2 %pull.3 = (f32[912,1024]{1,0:T(8,128)}, f32[8,128]{1,0:T(8,128)}) custom-call(bf16[912,2048]{1,0:T(8,128)(2,1)} %get-tuple-element.263.refs_1_.refs_0_, bf16[1024,1024]{1,0:T(8,128)(2,1)} %copy-done.37, bf16[1024,1024]{1,0:T(8,128)(2,1)} %collective-permute-done.6.refs_2_, f32[8,128]{1,0:T(8,128)} %copy-done.29), custom_call_target="tpu_custom_call" | custom-call | tf_op jit(solution)/shard_map/pull/pallas_call | solution.py:709
  403.0 8.6 %collective-permute-done.61.refs_2_.refs_4_ = bf16[1,128,1024]{2,1,0:T(8,128)(2,1)S(1)} collective-permute-done((bf16[1,128,1024]{2,1,0:T(8,128)(2,1)S(1)}, bf16[1,128,1024]{2,1,0:T(8,128)(2,1)S(1)}, u32[]{:S(2)}, u32[]{:S(2)}) %collective-permute-start.61) | collective-permute-done | bytes 262176 | tf_op jit(solution)/shard_map/ppermute | solution.py:822
  416.4 7.6 %collective-permute-done.65.refs_1_ = bf16[1,64,1024]{2,1,0:T(8,128)(2,1)S(1)} collective-permute-done((bf16[1,64,1024]{2,1,0:T(8,128)(2,1)S(1)}, bf16[1,64,1024]{2,1,0:T(8,128)(2,1)S(1)}, u32[]{:S(2)}, u32[]{:S(2)}) %collective-permute-start.65) | collective-permute-done | bytes 131104 | tf_op jit(solution)/shard_map/ppermute | solution.py:822
  428.9 5.1 %collective-permute-done.67.refs_2_ = bf16[64,1024]{1,0:T(8,128)(2,1)S(1)} collective-permute-done((bf16[64,1024]{1,0:T(8,128)(2,1)S(1)}, bf16[64,1024]{1,0:T(8,128)(2,1)S(1)}, u32[]{:S(2)}, u32[]{:S(2)}) %collective-permute-start.67) | collective-permute-done | bytes 131104 | tf_op jit(solution)/shard_map/ppermute | solution.py:822
  437.8 4.6 collective-permute-done.69.refs_2_
  448.2 2.6 multiply_add_fusion
  452.3 4.5 combine.2
  456.8 4.7 %collective-permute-done.58.refs_6_ = bf16[912,512]{1,0:T(8,128)(2,1)S(1)} collective-permute-done((bf16[912,512]{1,0:T(8,128)(2,1)S(1)}, bf16[912,512]{1,0:T(8,128)(2,1)S(1)}, u32[]{:S(2)}, u32[]{:S(2)}) %collective-permute-start.58) | collective-permute-done | bytes 933920 | tf_op jit(solution)/shard_map/ppermute | solution.py:817
  461.6 4.5 combine.3
  (325 shorter events, 149.6 us)
Async XLA Ops:
  2.5 27.5 %collective-permute-start.6 = (bf16[1024,1024]{1,0:T(8,128)(2,1)S(1)}, bf16[1024,1024]{1,0:T(8,128)(2,1)}, u32[]{:S(2)}, u32[]{:S(2)}) collective-permute-start(bf16[1024,1024]{1,0:T(8,128)(2,1)S(1)} %pad.16.refs_1_), channel_id=1, source_target_pairs={{0,1},{1,0},{2,3},{3,2},{4,5},{5,4},{6,7},{7,6},{8,9},{9,8},{10,11... | collective-permute-start | bytes 6291464 | tf_op jit(solution)/shard_map/ppermute | solution.py:817
  6.2 16.3 %collective-permute-start = (bf16[128,1024]{1,0:T(8,128)(2,1)}, bf16[128,1024]{1,0:T(8,128)(2,1)}, u32[]{:S(2)}, u32[]{:S(2)}) collective-permute-start(bf16[128,1024]{1,0:T(8,128)(2,1)} %get-tuple-element.171.refs_2_), channel_id=1, source_target_pairs={{0,2},{2,0},{1,3},{3,1},{4,6},{6,4},{5,7},{7,5},{8,10},{10,8},{9,1... | collective-permute-start | bytes 786440 | tf_op jit(solution)/shard_map/ppermute | solution.py:817
  8.8 13.7 %collective-permute-start.1 = (bf16[128,1024]{1,0:T(8,128)(2,1)}, bf16[128,1024]{1,0:T(8,128)(2,1)S(1)}, u32[]{:S(2)}, u32[]{:S(2)}) collective-permute-start(bf16[128,1024]{1,0:T(8,128)(2,1)} %get-tuple-element.172.refs_3_), channel_id=1, source_target_pairs={{0,2},{2,0},{1,3},{3,1},{4,6},{6,4},{5,7},{7,5},{8,10},{10,8},{9,1... | collective-permute-start | bytes 786440 | tf_op jit(solution)/shard_map/ppermute | solution.py:817
  8.9 12.2 %collective-permute-start.2 = (f32[3,1024]{1,0:T(4,128)S(1)}, f32[3,1024]{1,0:T(4,128)S(1)}, u32[]{:S(2)}, u32[]{:S(2)}) collective-permute-start(f32[3,1024]{1,0:T(4,128)S(1)} %select_maximum_fusion.2), channel_id=1, source_target_pairs={{0,1},{1,0},{2,3},{3,2},{4,5},{5,4},{6,7},{7,6},{8,9},{9,8},{10,11... | collective-permute-start | bytes 36872 | tf_op jit(solution)/shard_map/ppermute | solution.py:817
  9.1 12.7 %collective-permute-start.3 = (f32[3,1024]{1,0:T(4,128)S(1)}, f32[3,1024]{1,0:T(4,128)S(1)}, u32[]{:S(2)}, u32[]{:S(2)}) collective-permute-start(f32[3,1024]{1,0:T(4,128)S(1)} %select_maximum_fusion), channel_id=1, source_target_pairs={{0,2},{2,0},{1,3},{3,1},{4,6},{6,4},{5,7},{7,5},{8,10},{10,8},{9,1... | collective-permute-start | bytes 36872 | tf_op jit(solution)/shard_map/ppermute | solution.py:817
  22.5 32.0 %collective-permute-start.4 = (bf16[912,512]{1,0:T(8,128)(2,1)S(1)}, bf16[912,512]{1,0:T(8,128)(2,1)S(1)}, u32[]{:S(2)}, u32[]{:S(2)}) collective-permute-start(bf16[912,512]{1,0:T(8,128)(2,1)S(1)} %copy-done.17), channel_id=1, source_target_pairs={{0,2},{2,0},{1,3},{3,1},{4,6},{6,4},{5,7},{7,5},{8,10},{10,8},{9,1... | collective-permute-start | bytes 2801672 | tf_op jit(solution)/shard_map/ppermute | solution.py:817
  24.3 49.7 %collective-permute-start.10 = (bf16[912,512]{1,0:T(8,128)(2,1)}, bf16[912,512]{1,0:T(8,128)(2,1)S(1)}, u32[]{:S(2)}, u32[]{:S(2)}) collective-permute-start(bf16[912,512]{1,0:T(8,128)(2,1)} %get-tuple-element.186.refs_4_), channel_id=1, source_target_pairs={{0,2},{2,0},{1,3},{3,1},{4,6},{6,4},{5,7},{7,5},{8,10},{10,8},{9,1... | collective-permute-start | bytes 2801672 | tf_op jit(solution)/shard_map/ppermute | solution.py:817
  25.5 13.3 %collective-permute-start.8 = (bf16[64,1024]{1,0:T(8,128)(2,1)S(1)}, bf16[64,1024]{1,0:T(8,128)(2,1)S(1)}, u32[]{:S(2)}, u32[]{:S(2)}) collective-permute-start(bf16[64,1024]{1,0:T(8,128)(2,1)S(1)} %get-tuple-element.332.refs_1_), channel_id=1, source_target_pairs={{0,4},{4,0},{8,12},{12,8},{16,20},{20,16},{24,28},{28,24},{1,5},{5... | collective-permute-start | bytes 393224 | tf_op jit(solution)/shard_map/ppermute | solution.py:822
  27.4 13.1 %collective-permute-start.5 = (bf16[64,1024]{1,0:T(8,128)(2,1)S(1)}, bf16[64,1024]{1,0:T(8,128)(2,1)S(1)}, u32[]{:S(2)}, u32[]{:S(2)}) collective-permute-start(bf16[64,1024]{1,0:T(8,128)(2,1)S(1)} %get-tuple-element.333.refs_1_), channel_id=1, source_target_pairs={{0,16},{4,20},{8,24},{12,28},{16,0},{20,4},{24,8},{28,12},{1,17},{... | collective-permute-start | bytes 393224 | tf_op jit(solution)/shard_map/ppermute | solution.py:822
  40.2 13.4 %collective-permute-start.9 = (bf16[128,1024]{1,0:T(8,128)(2,1)S(1)}, bf16[128,1024]{1,0:T(8,128)(2,1)S(1)}, u32[]{:S(2)}, u32[]{:S(2)}) collective-permute-start(bf16[128,1024]{1,0:T(8,128)(2,1)S(1)} %get-tuple-element.183.refs_1_), channel_id=1, source_target_pairs={{0,16},{4,20},{8,24},{12,28},{16,0},{20,4},{24,8},{28,12},{1,17},{... | collective-permute-start | bytes 786440 | tf_op jit(solution)/shard_map/ppermute | solution.py:822
  41.1 13.2 %collective-permute-start.7 = (bf16[128,1024]{1,0:T(8,128)(2,1)S(1)}, bf16[128,1024]{1,0:T(8,128)(2,1)S(1)}, u32[]{:S(2)}, u32[]{:S(2)}) collective-permute-start(bf16[128,1024]{1,0:T(8,128)(2,1)S(1)} %get-tuple-element.180.refs_1_), channel_id=1, source_target_pairs={{0,8},{4,12},{8,0},{12,4},{16,24},{20,28},{24,16},{28,20},{1,9},{5... | collective-permute-start | bytes 786440 | tf_op jit(solution)/shard_map/ppermute | solution.py:822
  54.5 16.6 %collective-permute-start.11 = (bf16[256,1024]{1,0:T(8,128)(2,1)S(1)}, bf16[256,1024]{1,0:T(8,128)(2,1)S(1)}, u32[]{:S(2)}, u32[]{:S(2)}) collective-permute-start(bf16[256,1024]{1,0:T(8,128)(2,1)S(1)} %get-tuple-element.187.refs_1_), channel_id=1, source_target_pairs={{0,4},{4,0},{8,12},{12,8},{16,20},{20,16},{24,28},{28,24},{1,5},{5... | collective-permute-start | bytes 1572872 | tf_op jit(solution)/shard_map/ppermute | solution.py:822
  55.1 18.1 %collective-permute-start.13 = (bf16[256,1024]{1,0:T(8,128)(2,1)S(1)}, bf16[256,1024]{1,0:T(8,128)(2,1)S(1)}, u32[]{:S(2)}, u32[]{:S(2)}) collective-permute-start(bf16[256,1024]{1,0:T(8,128)(2,1)S(1)} %get-tuple-element.193.refs_1_), channel_id=1, source_target_pairs={{0,8},{4,12},{8,0},{12,4},{16,24},{20,28},{24,16},{28,20},{1,9},{5... | collective-permute-start | bytes 1572872 | tf_op jit(solution)/shard_map/ppermute | solution.py:822
  55.1 15.9 %collective-permute-start.12 = (bf16[128,1024]{1,0:T(8,128)(2,1)S(1)}, bf16[128,1024]{1,0:T(8,128)(2,1)S(1)}, u32[]{:S(2)}, u32[]{:S(2)}) collective-permute-start(bf16[128,1024]{1,0:T(8,128)(2,1)S(1)} %collective-permute-done.1.refs_1_), channel_id=1, source_target_pairs={{0,16},{4,20},{8,24},{12,28},{16,0},{20,4},{24,8},{28,12},{1,17},{... | collective-permute-start | bytes 786440 | tf_op jit(solution)/shard_map/ppermute | solution.py:822
  73.9 10.8 %collective-permute-start.14 = (bf16[512,1024]{1,0:T(8,128)(2,1)S(1)}, bf16[512,1024]{1,0:T(8,128)(2,1)S(1)}, u32[]{:S(2)}, u32[]{:S(2)}) collective-permute-start(bf16[512,1024]{1,0:T(8,128)(2,1)S(1)} %get-tuple-element.196.refs_2_), channel_id=1, source_target_pairs={{0,1},{1,0},{2,3},{3,2},{4,5},{5,4},{6,7},{7,6},{8,9},{9,8},{10,11... | collective-permute-start | bytes 3145736 | tf_op jit(solution)/shard_map/ppermute | solution.py:817
  74.9 9.8 %collective-permute-start.15 = (bf16[512,1024]{1,0:T(8,128)(2,1)S(1)}, bf16[512,1024]{1,0:T(8,128)(2,1)}, u32[]{:S(2)}, u32[]{:S(2)}) collective-permute-start(bf16[512,1024]{1,0:T(8,128)(2,1)S(1)} %get-tuple-element.197.refs_3_), channel_id=1, source_target_pairs={{0,1},{1,0},{2,3},{3,2},{4,5},{5,4},{6,7},{7,6},{8,9},{9,8},{10,11... | collective-permute-start | bytes 3145736 | tf_op jit(solution)/shard_map/ppermute | solution.py:817
  75.2 48.4 %collective-permute-start.23 = (bf16[1024,1024]{1,0:T(8,128)(2,1)S(1)}, bf16[1024,1024]{1,0:T(8,128)(2,1)}, u32[]{:S(2)}, u32[]{:S(2)}) collective-permute-start(bf16[1024,1024]{1,0:T(8,128)(2,1)S(1)} %pad.17.refs_6_.top_hbm.refs_1_), channel_id=1, source_target_pairs={{0,1},{1,0},{2,3},{3,2},{4,5},{5,4},{6,7},{7,6},{8,9},{9,8},{10,11... | collective-permute-start | bytes 6291464 | tf_op jit(solution)/shard_map/ppermute | solution.py:817
  75.8 22.3 %collective-permute-start.18 = (bf16[256,1024]{1,0:T(8,128)(2,1)S(1)}, bf16[256,1024]{1,0:T(8,128)(2,1)S(1)}, u32[]{:S(2)}, u32[]{:S(2)}) collective-permute-start(bf16[256,1024]{1,0:T(8,128)(2,1)S(1)} %get-tuple-element.206.refs_1_), channel_id=1, source_target_pairs={{0,8},{4,12},{8,0},{12,4},{16,24},{20,28},{24,16},{28,20},{1,9},{5... | collective-permute-start | bytes 1572872 | tf_op jit(solution)/shard_map/ppermute | solution.py:822
  100.5 23.1 %collective-permute-start.22 = (bf16[912,512]{1,0:T(8,128)(2,1)S(1)}, bf16[912,512]{1,0:T(8,128)(2,1)S(1)}, u32[]{:S(2)}, u32[]{:S(2)}) collective-permute-start(bf16[912,512]{1,0:T(8,128)(2,1)S(1)} %copy-done.15), channel_id=1, source_target_pairs={{0,2},{2,0},{1,3},{3,1},{4,6},{6,4},{5,7},{7,5},{8,10},{10,8},{9,1... | collective-permute-start | bytes 2801672 | tf_op jit(solution)/shard_map/ppermute | solution.py:817
  101.9 42.8 %collective-permute-start.24 = (bf16[512,1024]{1,0:T(8,128)(2,1)S(1)}, bf16[512,1024]{1,0:T(8,128)(2,1)S(1)}, u32[]{:S(2)}, u32[]{:S(2)}) collective-permute-start(bf16[512,1024]{1,0:T(8,128)(2,1)S(1)} %get-tuple-element.213.refs_1_), channel_id=1, source_target_pairs={{0,4},{4,0},{8,12},{12,8},{16,20},{20,16},{24,28},{28,24},{1,5},{5... | collective-permute-start | bytes 3145736 | tf_op jit(solution)/shard_map/ppermute | solution.py:822
  146.3 29.8 %collective-permute-start.30 = (bf16[912,512]{1,0:T(8,128)(2,1)S(1)}, bf16[912,512]{1,0:T(8,128)(2,1)S(1)}, u32[]{:S(2)}, u32[]{:S(2)}) collective-permute-start(bf16[912,512]{1,0:T(8,128)(2,1)S(1)} %copy-done.16), channel_id=1, source_target_pairs={{0,2},{2,0},{1,3},{3,1},{4,6},{6,4},{5,7},{7,5},{8,10},{10,8},{9,1... | collective-permute-start | bytes 2801672 | tf_op jit(solution)/shard_map/ppermute | solution.py:817
  240.7 10.4 %collective-permute-start.39 = (bf16[1024,1024]{1,0:T(8,128)(2,1)}, bf16[1024,1024]{1,0:T(8,128)(2,1)S(1)}, u32[]{:S(2)}, u32[]{:S(2)}) collective-permute-start(bf16[1024,1024]{1,0:T(8,128)(2,1)} %get-tuple-element.238), channel_id=1, source_target_pairs={{0,1},{1,0},{2,3},{3,2},{4,5},{5,4},{6,7},{7,6},{8,9},{9,8},{10,11... | collective-permute-start | bytes 6291464 | tf_op jit(solution)/shard_map/ppermute | solution.py:817
  240.8 14.2 %collective-permute-start.38 = (bf16[1024,1024]{1,0:T(8,128)(2,1)}, bf16[1024,1024]{1,0:T(8,128)(2,1)S(1)}, u32[]{:S(2)}, u32[]{:S(2)}) collective-permute-start(bf16[1024,1024]{1,0:T(8,128)(2,1)} %get-tuple-element.236), channel_id=1, source_target_pairs={{0,1},{1,0},{2,3},{3,2},{4,5},{5,4},{6,7},{7,6},{8,9},{9,8},{10,11... | collective-permute-start | bytes 6291464 | tf_op jit(solution)/shard_map/ppermute | solution.py:817
  241.3 23.5 %collective-permute-start.34 = (bf16[912,512]{1,0:T(8,128)(2,1)}, bf16[912,512]{1,0:T(8,128)(2,1)S(1)}, u32[]{:S(2)}, u32[]{:S(2)}) collective-permute-start(bf16[912,512]{1,0:T(8,128)(2,1)} %get-tuple-element.229), channel_id=1, source_target_pairs={{0,2},{2,0},{1,3},{3,1},{4,6},{6,4},{5,7},{7,5},{8,10},{10,8},{9,1... | collective-permute-start | bytes 2801672 | tf_op jit(solution)/shard_map/ppermute | solution.py:817
  259.9 28.0 %collective-permute-start.40 = (bf16[2,256,1024]{2,1,0:T(8,128)(2,1)}, bf16[2,256,1024]{2,1,0:T(8,128)(2,1)S(1)}, u32[]{:S(2)}, u32[]{:S(2)}) collective-permute-start(bf16[2,256,1024]{2,1,0:T(8,128)(2,1)} %get-tuple-element.245), channel_id=1, source_target_pairs={{0,4},{4,0},{8,12},{12,8},{16,20},{20,16},{24,28},{28,24},{1,5},{5... | collective-permute-start | bytes 3145736 | tf_op jit(solution)/shard_map/ppermute | solution.py:822
  261.4 26.4 %collective-permute-start.41 = (bf16[512,1024]{1,0:T(8,128)(2,1)S(1)}, bf16[512,1024]{1,0:T(8,128)(2,1)S(1)}, u32[]{:S(2)}, u32[]{:S(2)}) collective-permute-start(bf16[512,1024]{1,0:T(8,128)(2,1)S(1)} %bitcast.114), channel_id=1, source_target_pairs={{0,2},{2,0},{1,3},{3,1},{4,6},{6,4},{5,7},{7,5},{8,10},{10,8},{9,1... | collective-permute-start | bytes 3145736 | tf_op jit(solution)/shard_map/ppermute | solution.py:817
  295.5 16.1 %collective-permute-start.48 = (bf16[256,1024]{1,0:T(8,128)(2,1)S(1)}, bf16[256,1024]{1,0:T(8,128)(2,1)S(1)}, u32[]{:S(2)}, u32[]{:S(2)}) collective-permute-start(bf16[256,1024]{1,0:T(8,128)(2,1)S(1)} %bitcast.62), channel_id=1, source_target_pairs={{0,2},{2,0},{1,3},{3,1},{4,6},{6,4},{5,7},{7,5},{8,10},{10,8},{9,1... | collective-permute-start | bytes 1572872 | tf_op jit(solution)/shard_map/ppermute | solution.py:817
  300.1 12.1 %collective-permute-start.47 = (bf16[1,256,1024]{2,1,0:T(8,128)(2,1)}, bf16[1,256,1024]{2,1,0:T(8,128)(2,1)S(1)}, u32[]{:S(2)}, u32[]{:S(2)}) collective-permute-start(bf16[1,256,1024]{2,1,0:T(8,128)(2,1)} %get-tuple-element.259), channel_id=1, source_target_pairs={{0,4},{4,0},{8,12},{12,8},{16,20},{20,16},{24,28},{28,24},{1,5},{5... | collective-permute-start | bytes 1572872 | tf_op jit(solution)/shard_map/ppermute | solution.py:822
  315.3 17.1 %collective-permute-start.49 = (bf16[2,128,1024]{2,1,0:T(8,128)(2,1)S(1)}, bf16[2,128,1024]{2,1,0:T(8,128)(2,1)S(1)}, u32[]{:S(2)}, u32[]{:S(2)}) collective-permute-start(bf16[2,128,1024]{2,1,0:T(8,128)(2,1)S(1)} %get-tuple-element.265), channel_id=1, source_target_pairs={{0,8},{4,12},{8,0},{12,4},{16,24},{20,28},{24,16},{28,20},{1,9},{5... | collective-permute-start | bytes 1572872 | tf_op jit(solution)/shard_map/ppermute | solution.py:822
  332.4 10.9 %collective-permute-start.51 = (bf16[1024,1024]{1,0:T(8,128)(2,1)}, bf16[1024,1024]{1,0:T(8,128)(2,1)}, u32[]{:S(2)}, u32[]{:S(2)}) collective-permute-start(bf16[1024,1024]{1,0:T(8,128)(2,1)} %get-tuple-element.271), channel_id=1, source_target_pairs={{0,1},{1,0},{2,3},{3,2},{4,5},{5,4},{6,7},{7,6},{8,9},{9,8},{10,11... | collective-permute-start | bytes 6291464 | tf_op jit(solution)/shard_map/ppermute | solution.py:817
  352.2 25.7 %collective-permute-start.53 = (bf16[2,256,1024]{2,1,0:T(8,128)(2,1)}, bf16[2,256,1024]{2,1,0:T(8,128)(2,1)S(1)}, u32[]{:S(2)}, u32[]{:S(2)}) collective-permute-start(bf16[2,256,1024]{2,1,0:T(8,128)(2,1)} %get-tuple-element.276), channel_id=1, source_target_pairs={{0,4},{4,0},{8,12},{12,8},{16,20},{20,16},{24,28},{28,24},{1,5},{5... | collective-permute-start | bytes 3145736 | tf_op jit(solution)/shard_map/ppermute | solution.py:822
  353.9 26.4 %collective-permute-start.52 = (bf16[512,1024]{1,0:T(8,128)(2,1)}, bf16[512,1024]{1,0:T(8,128)(2,1)}, u32[]{:S(2)}, u32[]{:S(2)}) collective-permute-start(bf16[512,1024]{1,0:T(8,128)(2,1)} %bitcast.113), channel_id=1, source_target_pairs={{0,2},{2,0},{1,3},{3,1},{4,6},{6,4},{5,7},{7,5},{8,10},{10,8},{9,1... | collective-permute-start | bytes 3145736 | tf_op jit(solution)/shard_map/ppermute | solution.py:817
  355.2 14.5 %collective-permute-start.54 = (bf16[2,64,1024]{2,1,0:T(8,128)(2,1)S(1)}, bf16[2,64,1024]{2,1,0:T(8,128)(2,1)S(1)}, u32[]{:S(2)}, u32[]{:S(2)}) collective-permute-start(bf16[2,64,1024]{2,1,0:T(8,128)(2,1)S(1)} %get-tuple-element.278), channel_id=1, source_target_pairs={{0,16},{4,20},{8,24},{12,28},{16,0},{20,4},{24,8},{28,12},{1,17},{... | collective-permute-start | bytes 786440 | tf_op jit(solution)/shard_map/ppermute | solution.py:822
  370.6 14.0 %collective-permute-start.57 = (bf16[128,1024]{1,0:T(8,128)(2,1)S(1)}, bf16[128,1024]{1,0:T(8,128)(2,1)S(1)}, u32[]{:S(2)}, u32[]{:S(2)}) collective-permute-start(bf16[128,1024]{1,0:T(8,128)(2,1)S(1)} %bitcast.56), channel_id=1, source_target_pairs={{0,16},{4,20},{8,24},{12,28},{16,0},{20,4},{24,8},{28,12},{1,17},{... | collective-permute-start | bytes 786440 | tf_op jit(solution)/shard_map/ppermute | solution.py:822
  378.8 16.9 %collective-permute-start.56 = (bf16[256,1024]{1,0:T(8,128)(2,1)S(1)}, bf16[256,1024]{1,0:T(8,128)(2,1)S(1)}, u32[]{:S(2)}, u32[]{:S(2)}) collective-permute-start(bf16[256,1024]{1,0:T(8,128)(2,1)S(1)} %bitcast.63), channel_id=1, source_target_pairs={{0,2},{2,0},{1,3},{3,1},{4,6},{6,4},{5,7},{7,5},{8,10},{10,8},{9,1... | collective-permute-start | bytes 1572872 | tf_op jit(solution)/shard_map/ppermute | solution.py:817
  383.1 13.9 %collective-permute-start.55 = (bf16[1,256,1024]{2,1,0:T(8,128)(2,1)}, bf16[1,256,1024]{2,1,0:T(8,128)(2,1)S(1)}, u32[]{:S(2)}, u32[]{:S(2)}) collective-permute-start(bf16[1,256,1024]{2,1,0:T(8,128)(2,1)} %get-tuple-element.284), channel_id=1, source_target_pairs={{0,4},{4,0},{8,12},{12,8},{16,20},{20,16},{24,28},{28,24},{1,5},{5... | collective-permute-start | bytes 1572872 | tf_op jit(solution)/shard_map/ppermute | solution.py:822
  386.0 13.5 %collective-permute-start.62 = (bf16[256,1024]{1,0:T(8,128)(2,1)S(1)}, bf16[256,1024]{1,0:T(8,128)(2,1)S(1)}, u32[]{:S(2)}, u32[]{:S(2)}) collective-permute-start(bf16[256,1024]{1,0:T(8,128)(2,1)S(1)} %get-tuple-element.301.refs_1_), channel_id=1, source_target_pairs={{0,8},{4,12},{8,0},{12,4},{16,24},{20,28},{24,16},{28,20},{1,9},{5... | collective-permute-start | bytes 1572872 | tf_op jit(solution)/shard_map/ppermute | solution.py:822
  399.8 24.3 %collective-permute-start.64 = (bf16[512,1024]{1,0:T(8,128)(2,1)S(1)}, bf16[512,1024]{1,0:T(8,128)(2,1)S(1)}, u32[]{:S(2)}, u32[]{:S(2)}) collective-permute-start(bf16[512,1024]{1,0:T(8,128)(2,1)S(1)} %get-tuple-element.307.refs_1_), channel_id=1, source_target_pairs={{0,4},{4,0},{8,12},{12,8},{16,20},{20,16},{24,28},{28,24},{1,5},{5... | collective-permute-start | bytes 3145736 | tf_op jit(solution)/shard_map/ppermute | solution.py:822
  400.4 50.4 %collective-permute-start.59 = (bf16[912,1024]{1,0:T(8,128)(2,1)S(1)}, bf16[912,1024]{1,0:T(8,128)(2,1)S(1)}, u32[]{:S(2)}, u32[]{:S(2)}) collective-permute-start(bf16[912,1024]{1,0:T(8,128)(2,1)S(1)} %copy-done.57), channel_id=1, source_target_pairs={{0,2},{2,0},{1,3},{3,1},{4,6},{6,4},{5,7},{7,5},{8,10},{10,8},{9,1... | collective-permute-start | bytes 5603336 | tf_op jit(solution)/shard_map/ppermute | solution.py:817
  401.0 10.6 %collective-permute-start.61 = (bf16[1,128,1024]{2,1,0:T(8,128)(2,1)S(1)}, bf16[1,128,1024]{2,1,0:T(8,128)(2,1)S(1)}, u32[]{:S(2)}, u32[]{:S(2)}) collective-permute-start(bf16[1,128,1024]{2,1,0:T(8,128)(2,1)S(1)} %get-tuple-element.300), channel_id=1, source_target_pairs={{0,8},{4,12},{8,0},{12,4},{16,24},{20,28},{24,16},{28,20},{1,9},{5... | collective-permute-start | bytes 786440 | tf_op jit(solution)/shard_map/ppermute | solution.py:822
  401.9 12.5 %collective-permute-start.60 = (bf16[1,128,1024]{2,1,0:T(8,128)(2,1)S(1)}, bf16[1,128,1024]{2,1,0:T(8,128)(2,1)S(1)}, u32[]{:S(2)}, u32[]{:S(2)}) collective-permute-start(bf16[1,128,1024]{2,1,0:T(8,128)(2,1)S(1)} %get-tuple-element.298), channel_id=1, source_target_pairs={{0,8},{4,12},{8,0},{12,4},{16,24},{20,28},{24,16},{28,20},{1,9},{5... | collective-permute-start | bytes 786440 | tf_op jit(solution)/shard_map/ppermute | solution.py:822
  411.9 12.0 %collective-permute-start.65 = (bf16[1,64,1024]{2,1,0:T(8,128)(2,1)S(1)}, bf16[1,64,1024]{2,1,0:T(8,128)(2,1)S(1)}, u32[]{:S(2)}, u32[]{:S(2)}) collective-permute-start(bf16[1,64,1024]{2,1,0:T(8,128)(2,1)S(1)} %get-tuple-element.309), channel_id=1, source_target_pairs={{0,16},{4,20},{8,24},{12,28},{16,0},{20,4},{24,8},{28,12},{1,17},{... | collective-permute-start | bytes 393224 | tf_op jit(solution)/shard_map/ppermute | solution.py:822
  414.7 11.9 %collective-permute-start.63 = (bf16[1,64,1024]{2,1,0:T(8,128)(2,1)S(1)}, bf16[1,64,1024]{2,1,0:T(8,128)(2,1)S(1)}, u32[]{:S(2)}, u32[]{:S(2)}) collective-permute-start(bf16[1,64,1024]{2,1,0:T(8,128)(2,1)S(1)} %get-tuple-element.306), channel_id=1, source_target_pairs={{0,16},{4,20},{8,24},{12,28},{16,0},{20,4},{24,8},{28,12},{1,17},{... | collective-permute-start | bytes 393224 | tf_op jit(solution)/shard_map/ppermute | solution.py:822
  424.1 10.0 %collective-permute-start.67 = (bf16[64,1024]{1,0:T(8,128)(2,1)S(1)}, bf16[64,1024]{1,0:T(8,128)(2,1)S(1)}, u32[]{:S(2)}, u32[]{:S(2)}) collective-permute-start(bf16[64,1024]{1,0:T(8,128)(2,1)S(1)} %bitcast.58), channel_id=1, source_target_pairs={{0,16},{4,20},{8,24},{12,28},{16,0},{20,4},{24,8},{28,12},{1,17},{... | collective-permute-start | bytes 393224 | tf_op jit(solution)/shard_map/ppermute | solution.py:822
  427.5 34.1 %collective-permute-start.58 = (bf16[912,512]{1,0:T(8,128)(2,1)S(1)}, bf16[912,512]{1,0:T(8,128)(2,1)S(1)}, u32[]{:S(2)}, u32[]{:S(2)}) collective-permute-start(bf16[912,512]{1,0:T(8,128)(2,1)S(1)} %copy-done.59), channel_id=1, source_target_pairs={{0,2},{2,0},{1,3},{3,1},{4,6},{6,4},{5,7},{7,5},{8,10},{10,8},{9,1... | collective-permute-start | bytes 2801672 | tf_op jit(solution)/shard_map/ppermute | solution.py:817
  435.5 9.6 %collective-permute-start.68 = (bf16[128,1024]{1,0:T(8,128)(2,1)S(1)}, bf16[128,1024]{1,0:T(8,128)(2,1)S(1)}, u32[]{:S(2)}, u32[]{:S(2)}) collective-permute-start(bf16[128,1024]{1,0:T(8,128)(2,1)S(1)} %get-tuple-element.317.refs_1_), channel_id=1, source_target_pairs={{0,8},{4,12},{8,0},{12,4},{16,24},{20,28},{24,16},{28,20},{1,9},{5... | collective-permute-start | bytes 786440 | tf_op jit(solution)/shard_map/ppermute | solution.py:822
  442.4 23.6 %collective-permute-start.71 = (bf16[256,1024]{1,0:T(8,128)(2,1)S(1)}, bf16[256,1024]{1,0:T(8,128)(2,1)S(1)}, u32[]{:S(2)}, u32[]{:S(2)}) collective-permute-start(bf16[256,1024]{1,0:T(8,128)(2,1)S(1)} %get-tuple-element.326.refs_1_), channel_id=1, source_target_pairs={{0,4},{4,0},{8,12},{12,8},{16,20},{20,16},{24,28},{28,24},{1,5},{5... | collective-permute-start | bytes 1572872 | tf_op jit(solution)/shard_map/ppermute | solution.py:822
  445.2 21.0 %collective-permute-start.70 = (bf16[256,1024]{1,0:T(8,128)(2,1)S(1)}, bf16[256,1024]{1,0:T(8,128)(2,1)S(1)}, u32[]{:S(2)}, u32[]{:S(2)}) collective-permute-start(bf16[256,1024]{1,0:T(8,128)(2,1)S(1)} %get-tuple-element.325.refs_1_), channel_id=1, source_target_pairs={{0,4},{4,0},{8,12},{12,8},{16,20},{20,16},{24,28},{28,24},{1,5},{5... | collective-permute-start | bytes 1572872 | tf_op jit(solution)/shard_map/ppermute | solution.py:822
  (85 other events, 470.4 us)
where the time goes:
time: 478 us; the launch traced here: 470 us
  Pallas kernels  217 us (45%)
  waiting for transfers between devices  134 us (28%)
  starting transfers between devices  72.2 us (15%)
  local copies, waits for them, and re-layouts  27.3 us (6%)
  other arithmetic  17.9 us (4%)
    ppermute x40, waiting for transfers between devices, across(): return lax.ppermute(value, 'dp', [(i, i ^ bit) for i in range(size)])  97.5 us
    pallas_call x4, Pallas kernels, weight_grad(): pl.pallas_call(without(kernel, len(specs), len(deps), -1 - len(scratch)),...  50.5 us
    ppermute x40, starting transfers between devices, across(): return lax.ppermute(value, 'dp', [(i, i ^ bit) for i in range(size)])  45.7 us
    ppermute x32, waiting for transfers between devices, over(): return lax.ppermute(value, axis, [(0, 1), (1, 0)])  36.3 us
    pallas_call x4, Pallas kernels, project(): pl.pallas_call(without(kernel, len(operands), len(deps)), grid=(len(ws) *...  29.6 us
    ppermute x32, starting transfers between devices, over(): return lax.ppermute(value, axis, [(0, 1), (1, 0)])  26.5 us
    pallas_call x1, Pallas kernels, second_layer(): pl.pallas_call(functools.partial(second_layer_kernel, steps, seqs, count)...  22.6 us
    pallas_call x1, Pallas kernels, first_back(): pl.pallas_call(without(functools.partial(first_back_kernel, steps, seqs,...  21.3 us
  transfers between devices with their start and end apart: 72, of which 40 were waited for; matrix products, arithmetic and copies ran while one was open for 4% of the time, Pallas kernels for 36%

commit v1 on v0

--- a/solution.py
+++ b/solution.py
@@ -102,32 +102,22 @@
 def prep_grads_kernel(pitch, width, at_ref, own, other, near, send0, send1, packed):
     seqs, steps, block = own.shape
     lane = pl.program_id(0) * block + lax.broadcasted_iota(jnp.int32, (1, block), 1)
-    for part in (own, other):
+
+    def pack(part, out):
         for s in range(seqs):
             packed[s * pitch : s * pitch + steps, :] = part[s].astype(f32)
             packed[s * pitch + steps : (s + 1) * pitch, :] = jnp.zeros((pitch - steps, block), f32)
-        value = jnp.where(lane < width, packed[...], 0.0).astype(bf16)
-        if part is own:
-            near[...] = value
-        else:
-            cut = pl.num_programs(0) // 2
-
-            @pl.when(pl.program_id(0) < cut)
-            def _():
-                send0[...] = value
-
-            @pl.when(pl.program_id(0) >= cut)
-            def _():
-                send1[...] = value
+        out[...] = jnp.where(lane < width, packed[...], 0.0).astype(bf16)
+
+    pack(own, near)
+    pl.when(pl.program_id(0) == 0)(lambda: pack(other, send0))
+    pl.when(pl.program_id(0) > 0)(lambda: pack(other, send1))
 
 
 def prep_grads(grads, places, seqs, pitch, half):
     _, steps, width = grads.shape
     rows = seqs * pitch
     out = pl.BlockSpec((rows, BLOCK), lambda j, at: (0, j))
-    cut = half // BLOCK // 2
-    first = pl.BlockSpec((rows, BLOCK), lambda j, at: (0, held(j, 0, cut)))
-    second = pl.BlockSpec((rows, BLOCK), lambda j, at: (0, held(j, cut, cut)))
     return pl.pallas_call(
         without(functools.partial(prep_grads_kernel, pitch, width), 0, 0, -2),
         grid_spec=pltpu.PrefetchScalarGridSpec(
@@ -137,12 +127,15 @@
                 pl.BlockSpec((seqs, steps, BLOCK), lambda j, at: (at[0], 0, j)),
                 pl.BlockSpec((seqs, steps, BLOCK), lambda j, at: (at[1], 0, j)),
             ],
-            out_specs=[out, first, second, token_spec],
+            out_specs=[
+                out,
+                pl.BlockSpec((rows, BLOCK), lambda j, at: (0, 0)),
+                pl.BlockSpec((rows, BLOCK), lambda j, at: (0, jnp.maximum(j - 1, 0))),
+                token_spec,
+            ],
             scratch_shapes=[pltpu.VMEM((rows, BLOCK), f32)],
         ),
-        out_shape=[jax.ShapeDtypeStruct((rows, half), bf16)]
-        + [jax.ShapeDtypeStruct((rows, half // 2), bf16)] * 2
-        + [token_shape],
+        out_shape=[jax.ShapeDtypeStruct((rows, lanes), bf16) for lanes in (half, BLOCK, half - BLOCK)] + [token_shape],
         compiler_params=params(),
         name="prep_grads",
     )(places, grads, grads)
@@ -306,7 +299,7 @@
             now.append(state)
         return tuple(now)
 
-    unroll = 2 if steps % 2 == 0 else 1
+    unroll = next(k for k in (5, 3, 2, 1) if steps % k == 0)
 
     def several(i, before):
         for k in range(unroll):
@@ -331,7 +324,7 @@
             now.append(grad)
         return tuple(now)
 
-    unroll = 2 if steps % 2 == 0 else 1
+    unroll = next(k for k in (2, 3, 1) if steps % k == 0)
 
     def several(i, after):
         for k in range(unroll):
@@ -458,8 +451,8 @@
     finish = load_norm(parts_in, proj_hbm, proj, sems, sums, gains, count, norm)
     upstream = [
         pltpu.make_async_copy(near_hbm, near, sems.at[parts_in]),
-        pltpu.make_async_copy(far_hbm0, far.at[:, :cut], sems.at[parts_in + 1]),
-        pltpu.make_async_copy(far_hbm1, far.at[:, cut:], sems.at[parts_in + 2]),
+        pltpu.make_async_copy(far_hbm0, far.at[:, :BLOCK], sems.at[parts_in + 1]),
+        pltpu.make_async_copy(far_hbm1, far.at[:, BLOCK:], sems.at[parts_in + 2]),
     ]
     for copy in upstream:
         copy.start()
@@ -510,11 +503,12 @@
 
 
 def first_back_kernel(
-    steps, seqs, count, nb, low, w_nn, w_nf, w_fn, w_ff, slopes_hbm, hidden_hbm, proj_hbm, sums, gains,
-    grads_out, out, grads, slopes, hidden, proj, shifted, sems,
+    steps, seqs, count, nb, low, *refs,
 ):
+    weights, refs = refs[: 2 * nb], refs[2 * nb :]
+    slopes_hbm, hidden_hbm, proj_hbm, sums, gains, grads_out, out, grads, slopes, hidden, proj, shifted, sems = refs
     tiles = proj.shape[0]
-    half = w_nn.shape[1]
+    half = weights[0].shape[1]
     j = pl.program_id(0)
     copies = [
         pltpu.make_async_copy(slopes_hbm, slopes, sems.at[0]),
@@ -532,10 +526,10 @@
         for k in range(WIDE // LANES):
             grads[j * (WIDE // LANES) + k] = acc[:, k * LANES : (k + 1) * LANES]
 
-    pl.when(j < nb)(functools.partial(go, w_nn, w_nf))
-    pl.when((j >= nb) & (j < 2 * nb))(functools.partial(go, w_fn, w_ff))
-
-    @pl.when(j == 2 * nb)
+    for k in range(nb):
+        pl.when(j == k)(functools.partial(go, *weights[2 * k : 2 * k + 2]))
+
+    @pl.when(j == nb)
     def _():
         for copy in copies:
             copy.wait()
@@ -547,16 +541,17 @@
         send.wait()
 
 
-def first_back(steps, seqs, count, low, quarters, slopes, hidden, proj, sums, gains, deps=()):
+def first_back(steps, seqs, count, low, blocks, slopes, hidden, proj, sums, gains, deps=()):
     tiles, rows, _ = proj.shape
     width = tiles * LANES
     half = width // 2
-    nb = half // WIDE
+    nb = len(blocks)
     hbm = pl.BlockSpec(memory_space=pl.ANY)
-    weights = [pl.BlockSpec((WIDE, half), lambda j, k=k: (held(j, k // 2 * nb, nb), 0)) for k in range(4)]
+    operands = [x for pair in blocks for x, _ in pair]
+    weights = [pl.BlockSpec((WIDE, half), lambda j, at=at: (at, 0)) for pair in blocks for _, at in pair]
     return pl.pallas_call(
-        without(functools.partial(first_back_kernel, steps, seqs, count, nb), 10, len(deps)),
-        grid=(2 * nb + 1,),
+        without(functools.partial(first_back_kernel, steps, seqs, count, nb), 6 + 2 * nb, len(deps)),
+        grid=(nb + 1,),
         in_specs=[whole((rows, width)), *weights, hbm, hbm, hbm, whole((2, width)), whole((3, width))] + after(deps),
         out_specs=[hbm, pl.BlockSpec((3, width), lambda j: (0, 0))],
         out_shape=[
@@ -573,7 +568,7 @@
         ],
         compiler_params=params(),
         name="first_back",
-    )(low, *quarters, slopes, hidden, proj, sums, gains, *deps)
+    )(low, *operands, slopes, hidden, proj, sums, gains, *deps)
 
 
 def norm_back(steps, seqs, arg_grads, proj, sums, gains, totals, count, low_ref, columns):
@@ -677,6 +672,16 @@
     )(*operands, *grads, *deps)
 
 
+def row_blocks(left, right):
+    pairs = []
+    for x in (left, right):
+        if isinstance(x, (list, tuple)):
+            pairs.append([(part, 0) for part in x])
+        else:
+            pairs.append([(x, k) for k in range(x.shape[0] // WIDE)])
+    return list(zip(*pairs))
+
+
 def pull_kernel(nb, tiled, low, *refs):
     *weights, out = refs
     j = pl.program_id(0)
@@ -694,27 +699,21 @@
         pl.when((j >= k * nb) & (j < (k + 1) * nb))(functools.partial(go, *weights[2 * k : 2 * k + 2]))
 
 
-def pull(low, quarters, tiled, dtype, deps=()):
+def pull(low, left, right, dtype, deps=()):
     rows, width = low.shape
     half = width // 2
-    nb = half // WIDE
-    halves = len(quarters) // 2
-    specs = [pl.BlockSpec((WIDE, half), lambda j, k=k: (held(j, k // 2 * nb, nb), 0)) for k in range(2 * halves)]
-    if tiled:
-        out_spec = pl.BlockSpec((WIDE // LANES, rows, LANES), lambda j: (j, 0, 0))
-        shape = (halves * half // LANES, rows, LANES)
-    else:
-        out_spec = pl.BlockSpec((rows, WIDE), lambda j: (0, j))
-        shape = (rows, halves * half)
+    blocks = row_blocks(left, right)
+    operands = [x for pair in blocks for x, _ in pair]
+    specs = [pl.BlockSpec((WIDE, half), lambda j, at=at: (at, 0)) for pair in blocks for _, at in pair]
     return pl.pallas_call(
-        without(functools.partial(pull_kernel, nb, tiled), 1 + len(quarters), len(deps), -1),
-        grid=(halves * nb,),
+        without(functools.partial(pull_kernel, 1, False), 1 + len(operands), len(deps), -1),
+        grid=(len(blocks),),
         in_specs=[whole((rows, width))] + specs + after(deps),
-        out_specs=[out_spec, token_spec],
-        out_shape=[jax.ShapeDtypeStruct(shape, dtype), token_shape],
+        out_specs=[pl.BlockSpec((rows, WIDE), lambda j: (0, j)), token_spec],
+        out_shape=[jax.ShapeDtypeStruct((rows, len(blocks) * WIDE), dtype), token_shape],
         compiler_params=params(),
         name="pull",
-    )(low, *quarters, *deps)
+    )(low, *operands, *deps)
 
 
 def fold_kernel(counts, at_ref, *refs):
@@ -730,7 +729,8 @@
 def fold(mine, stacks, rows, deps=(), mebibytes=16):
     specs, operands = [], []
     width = stacks[0][0][0].shape[-1]
-    lanes = width // 2
+    cuts = 2
+    lanes = width // cuts
     for stack in stacks:
         for side in (0, 1):
             for array, index, base in stack:
@@ -747,7 +747,7 @@
     return pl.pallas_call(
         without(kernel, 1 + len(operands), len(deps), -1),
         grid_spec=pltpu.PrefetchScalarGridSpec(
-            num_scalar_prefetch=1, grid=(2,), in_specs=specs + after(deps), out_specs=[out_spec, out_spec, token_spec]
+            num_scalar_prefetch=1, grid=(cuts,), in_specs=specs + after(deps), out_specs=[out_spec, out_spec, token_spec]
         ),
         out_shape=[
             jax.ShapeDtypeStruct((count, rows, width), f32),
@@ -770,13 +770,14 @@
 def total(stacks, rows, deps=(), mebibytes=16):
     parts = [part for stack in stacks for part in stack]
     count, width = len(stacks), parts[0][0].shape[-1]
-    lanes = width // 2
+    cuts = 2
+    lanes = width // cuts
     specs = [
         pl.BlockSpec((None, rows, lanes), lambda j, index=index, block=block: (index, block, j)) for _, index, block in parts
     ]
     out, done = pl.pallas_call(
         without(functools.partial(total_kernel, [len(stack) for stack in stacks]), len(parts), len(deps), -1),
-        grid=(2,),
+        grid=(cuts,),
         in_specs=specs + after(deps),
         out_specs=[pl.BlockSpec((count, rows, lanes), lambda j: (0, 0, j)), token_spec],
         out_shape=[jax.ShapeDtypeStruct((count, rows, width), bf16), token_shape],
@@ -885,25 +886,24 @@
     own_second = pad_params(gain_second, shift_second, recur_second)
     own_third = pad_params(gain_third, shift_third, recur_third)
     gains_second = jnp.concatenate([own_second, over(own_second, "col")], axis=1)
-    gains_third = jnp.concatenate([own_third, over(own_third, "row")], axis=1)
-    nn2, nn3 = pad_weight(w_second), pad_weight(w_third)
-    nf2, fn3 = over(nn2, "col"), over(nn3, "col")
     deps = ()
     if spread:
         cut_second, cut_third = cut(w_second, w_third, [turned(order) for order in orders], chunks, pieces, half)
         tall = half // (chunks * pieces)
+        deps = (cut_second, cut_third)
+    if spread:
+        cut_second, w_second, w_third = lax.optimization_barrier((cut_second, w_second, w_third))
         far_second, far_third = over(cut_second, "row"), over(cut_third, "row")
-        deps = (cut_second, cut_third)
+    nn2, nn3 = pad_weight(w_second), pad_weight(w_third)
+    nf2, fn3 = over(nn2, "col"), over(nn3, "col")
     x_near, send0 = prep(inputs, places, seqs, pitch, half, 0, nb // 2, None, deps)
     x_near, send1 = prep(inputs, places, seqs, pitch, half, nb // 2, nb // 2, x_near)
     if spread:
-        send0, send1, far_second, far_third, gains_second, gains_third = lax.optimization_barrier(
-            (send0, send1, far_second, far_third, gains_second, gains_third)
-        )
+        send0, send1, far_second, far_third = lax.optimization_barrier((send0, send1, far_second, far_third))
     x_far0 = over(send0, "row")
     x_far1 = over(send1, "row")
     proj_second, near_done = project([(x_near, 0, half)], [[nn2], [nf2]], tiles)
-    cot_near, cot_send0, cot_send1, cot_done = prep_grads(jnp.transpose(cotangent, (1, 0, 2)), parts, seqs, pitch, half)
+    cot_near, *cot_send, cot_done = prep_grads(jnp.transpose(cotangent, (1, 0, 2)), parts, seqs, pitch, half)
     if spread:
         fn2 = [far_second[k * tall : (k + 1) * tall] for k in range(chunks)]
         nf3 = far_third
@@ -921,7 +921,7 @@
                 nf3, done = join(bit_of(orders[0][k - 1]), nf3, nf3_other, tuple(done for _, done in joined))
                 deps = (done,)
             if k == len(bits) - 2:
-                x_far0, *fn2 = lax.optimization_barrier((x_far0, *fn2))
+                x_far0, nn3, *fn2 = lax.optimization_barrier((x_far0, nn3, *fn2))
         x_far1, *fn2 = lax.optimization_barrier((x_far1, *fn2))
     else:
         far = over(nn2, "row")
@@ -929,8 +929,9 @@
         nf3 = over(nn3, "row")
     ff2 = [over(chunk, "col") for chunk in fn2]
     x_parts = [(x_far0, 0, half // 2), (x_far1, 0, half // 2)]
-    proj_second, sums_near = project(x_parts, [fn2], tiles, 0, proj_second, True, (cot_done, nn3))
-    proj_second, sums_far = project(x_parts, [ff2], tiles, half // WIDE, proj_second, True)
+    proj_second, sums_near = project(x_parts, [fn2], tiles, 0, proj_second, True, (cot_done,))
+    cot_far0 = over(cot_send[0], "row")
+    proj_second, sums_far = project(x_parts, [ff2], tiles, half // WIDE, proj_second, True, (cot_far0,))
     sums = jnp.concatenate([sums_near, sums_far], axis=1)
     if spread:
         nf3, done = join(bit_of(bits[1]), nf3, nf3_other, (sums,))
@@ -938,8 +939,8 @@
 
     swaps = ("col", "col")
     sums = sum_step(sums, "row", swaps)
-    sums, cot_send0, cot_send1 = lax.optimization_barrier((sums, cot_send0, cot_send1))
-    cot_far0, cot_far1 = over(cot_send0, "row"), over(cot_send1, "row")
+    sums, cot_send1 = lax.optimization_barrier((sums, cot_send[1]))
+    cot_far1 = over(cot_send1, "row")
     if spread:
         sums = sum_step(sums, bits[0], swaps)
         sums, nf3 = lax.optimization_barrier((sums, nf3))
@@ -947,24 +948,25 @@
     sums = sum_step(sums, "col", swaps)
     for bit in bits[1:] if spread else bits:
         sums = sum_step(sums, bit, swaps)
-    sums_second, cot_far0 = lax.optimization_barrier((sums, cot_far0))
+    sums_second = sums
     hidden, slopes_second, hidden_sums, proj_third, sums_near = first_layer(
         steps, seqs, count, proj_second, sums_second, gains_second, nn3, fn3
     )
     if spread:
         nf3, done = join(bit_of(bits[0]), nf3, nf3_other, (hidden_sums,))
-    ff3 = over(nf3, "col")
-    hidden_parts = [(hidden, 0, half), (hidden, 1, half)]
+    ff3 = [over(nf3[k * WIDE : (k + 1) * WIDE], "col") for k in range(half // WIDE)]
+    hidden_parts = [(hidden, 0, half)] + [(hidden, (half + k * WIDE) // WIDE, WIDE) for k in range(half // WIDE)]
     proj_third, sums_far = project(
-        hidden_parts, [[nf3, ff3]], tiles, half // WIDE, proj_third, False
+        hidden_parts, [[nf3, *ff3]], tiles, half // WIDE, proj_third, False, (cot_far1,)
     )
 
     swaps = ("row", "row", "col")
     sums = jnp.concatenate([jnp.concatenate([sums_near, sums_far], axis=1), hidden_sums], axis=0)
     for step in ("col", *bits):
         sums = sum_step(sums, step, swaps)
-    sums, cot_far1 = lax.optimization_barrier((sums, cot_far1))
-    sums = sum_step(sums, "row", swaps)
+    other = over(jnp.concatenate([sums, own_third], axis=1), "row")
+    sums = sums + jnp.concatenate([swap_halves(other[:2, : 2 * half]), other[2:3, : 2 * half]], axis=0)
+    gains_third = jnp.concatenate([own_third, other[:, 2 * half :]], axis=1)
     sums_third, centre = sums[:2], (sums[2:3] / count).astype(bf16).astype(f32)
     states_near, out_send0, out_send1, arg_grads_third, sums = second_layer(
         steps, seqs, count, proj_third, sums_third, gains_third, cot_near, (cot_far0, cot_far1)
@@ -1025,7 +1027,7 @@
     kept, sent, done = begin_across(nn, from_fn, nf, from_ff, (done,))
     b3_kept, b3_other = kept, across(sent, bits[0])
     arg_grads_second, sums = first_back(
-        steps, seqs, count, low_third, [nn3, nf3, fn3, ff3], slopes_second, hidden, proj_second, sums_second, gains_second,
+        steps, seqs, count, low_third, row_blocks(nn3, nf3) + row_blocks(fn3, ff3), slopes_second, hidden, proj_second, sums_second, gains_second,
         (done, out_far0),
     )
     swaps = ("col", "col", "col", "row")
@@ -1052,26 +1054,27 @@
         sums = sum_step(sums, bit, swaps)
     totals_second, columns = sums[:3], sums[3:4]
     c3 = Chain([a3, [(b3_kept, 0), (b3_other, 0), (b3_row, 0)]], cutting // 2, bits[1:])
-    totals_second, done = lax.optimization_barrier((totals_second, done))
+    totals_second, done, out_send1 = lax.optimization_barrier((totals_second, done, out_send1))
+    out_far1 = over(out_send1, "row")
     seen = c3.step((done,))
 
     grads = (arg_grads_second, proj_second, sums_second, gains_second, totals_second)
     low_second, seen, fn, ff, _ = weight_grad(steps, seqs, count, [(x_far0, 0, 1), (x_far1, 0, 1)], grads, deps=seen)
     from_ff = over(ff, "col")
-    seen = c3.step((seen,)) if c3.left else (seen,)
+    seen = c3.step((seen, out_far1)) if c3.left else (seen, out_far1)
     nn, nf, done = weight_grad(steps, seqs, count, [(x_near, 0, wide)], (low_second,), deps=seen)
     from_nf = over(nf, "col")
     x2, done = total([[(fn[None], 0, 0), (from_ff[None], 0, 0)]], cutting, (done,), 56)
     x2_come = over(x2, "row")
     kept, sent, done = begin_across(nn, from_nf, fn, from_ff, (done,))
     b2_kept, b2_other = kept, across(sent, bits[0])
-    far_rows = [jnp.concatenate(fn2, axis=0), jnp.concatenate(ff2, axis=0)]
-    grad_far, done = pull(low_second, far_rows, False, bf16, (done,))
+    grad_far, done = pull(low_second, fn2, ff2, bf16, (done,))
     seen = c3.piece((done,))
-    b2_row, done = to_row(b2_kept, b2_other, seen)
+    output, done = combine(parts, x_near, states_near, (send0, send1), (out_far0, out_far1), seqs, steps, width, seen)
+    b2_row, done = to_row(b2_kept, b2_other, (done,))
     a2, done = to_across(nn, from_nf, x2_come, (done,))
     seen = c3.gather((done,))
-    grad_near, done = pull(low_second, [nn2, nf2], False, f32, seen)
+    grad_near, done = pull(low_second, nn2, nf2, f32, seen)
     seen = (done,)
     b2 = Chain([[(b2_kept, 0), (b2_other, 0), (b2_row, 0)]], cutting // 2, bits[1:])
     seen = b2.step(seen)
@@ -1079,9 +1082,7 @@
     grad_far = over(grad_far, "row")
     a2 = Chain([a2], cutting // 2, bits[1:])
     seen = a2.step((done,))
-    out_send1, done = lax.optimization_barrier((out_send1, *seen))
-    out_far1 = over(out_send1, "row")
-    seen = c3.gather((done,)) if c3.back else (done,)
+    seen = c3.gather(seen) if c3.back else seen
     seen = b2.step(seen) if b2.left else seen
     seen = a2.step(seen) if a2.left else seen
     seen = b2.piece(seen)
@@ -1092,10 +1093,7 @@
     seen = b2.gather(seen)
     seen = a2.gather(seen)
     grad_inputs, done = combine(
-        parts, cot_near, grad_near, (cot_send0, cot_send1), (grad_far,), seqs, steps, width, seen
-    )
-    output, done = combine(
-        parts, x_near, states_near, (send0, send1), (out_far0, out_far1), seqs, steps, width, (done,)
+        parts, cot_near, grad_near, cot_send, (grad_far,), seqs, steps, width, seen
     )
     seen = (done,)
     chains = [c3, b2, a2]

time: 478 us -> 467 us (0.977)
  waiting for transfers between devices: 134 us -> 116 us
  starting transfers between devices: 72.2 us -> 77.4 us
    ppermute x32, waiting for transfers between devices: 36.3 us -> 26.9 us  [over(): return lax.ppermute(value, axis, [(0, 1), (1, 0)])]
    ppermute x40, waiting for transfers between devices: 97.5 us -> 89.5 us  [across(): return lax.ppermute(value, 'dp', [(i, i ^ bit) for i in range(size)])]
    ppermute x40, starting transfers between devices: 45.7 us -> 51.7 us  [across(): return lax.ppermute(value, 'dp', [(i, i ^ bit) for i in range(size)])]
    unnamed x121 -> x119, local copies, waits for them, and re-layouts: 20.1 us -> 22.2 us
  transfers between devices with their start and end apart: 72 -> 72, of which waited for: 40 -> 41; matrix products, arithmetic and copies ran while one was open for 4% -> 3% of each run, Pallas kernels for 36% -> 36%
where the time goes in v1:
time: 467 us; the launch traced here: 459 us
  Pallas kernels  219 us (47%)
  waiting for transfers between devices  116 us (25%)
  starting transfers between devices  77.4 us (17%)
  local copies, waits for them, and re-layouts  30 us (6%)
  other arithmetic  13.7 us (3%)
    ppermute x40, waiting for transfers between devices, across(): return lax.ppermute(value, 'dp', [(i, i ^ bit) for i in range(size)])  89.5 us
    ppermute x40, starting transfers between devices, across(): return lax.ppermute(value, 'dp', [(i, i ^ bit) for i in range(size)])  51.7 us
    pallas_call x4, Pallas kernels, weight_grad(): pl.pallas_call(without(kernel, len(specs), len(deps), -1 - len(scratch)),...  50.3 us
    pallas_call x4, Pallas kernels, project(): pl.pallas_call(without(kernel, len(operands), len(deps)), grid=(len(ws) *...  30 us
    ppermute x32, waiting for transfers between devices, over(): return lax.ppermute(value, axis, [(0, 1), (1, 0)])  26.9 us
    ppermute x32, starting transfers between devices, over(): return lax.ppermute(value, axis, [(0, 1), (1, 0)])  25.6 us
    unnamed x119, local copies, waits for them, and re-layouts  22.2 us
    pallas_call x1, Pallas kernels, first_back(): pl.pallas_call(without(functools.partial(first_back_kernel, steps, seqs,...  22.1 us
  transfers between devices with their start and end apart: 72, of which 41 were waited for; matrix products, arithmetic and copies ran while one was open for 3% of the time, Pallas kernels for 36%

profile of v1, /device:TPU:0, one launch (start us, length us, event | category | flops | bytes accessed | tf_op | source)
XLA Modules:
  0.0 458.6 jit_solution(9773548795683370937)
XLA Ops:
  1.3 2.5 cut.1
  6.2 2.6 collective-permute-start
  9.5 4.7 %prep.2 = (bf16[912,1024]{1,0:T(8,128)(2,1)}, bf16[912,512]{1,0:T(8,128)(2,1)}) custom-call(s32[2]{0:T(128)} %pad_add_fusion.1.refs_0_, bf16[150,24,1000]{2,1,0:T(8,128)(2,1)} %refs_1_.3, bf16[128,1024]{1,0:T(8,128)(2,1)} %get-tuple-element.173.refs_2_, bf16[128,1024]{1,0:T(8,128)(2,1)} %get-tuple-element.168.refs_3_), custom_call_target="tpu_custom_call" | custom-call | tf_op jit(solution)/shard_map/prep/pallas_call | solution.py:81
  14.2 4.8 %prep.3 = (bf16[912,1024]{1,0:T(8,128)(2,1)}, bf16[912,512]{1,0:T(8,128)(2,1)}) custom-call(s32[2]{0:T(128)} %pad_add_fusion.1.refs_0_, bf16[150,24,1000]{2,1,0:T(8,128)(2,1)} %refs_1_.3, bf16[912,1024]{1,0:T(8,128)(2,1)} %get-tuple-element.169.refs_2_), custom_call_target="tpu_custom_call", output_to_operand_aliasing={{0}: (2, {})} | custom-call | tf_op jit(solution)/shard_map/prep/pallas_call | solution.py:81
  25.2 2.6 collective-permute-start.3
  27.8 8.9 %project.4 = (f32[16,912,128]{2,1,0:T(8,128)}, f32[2,2048]{1,0:T(2,128)}) custom-call(bf16[912,1024]{1,0:T(8,128)(2,1)} %get-tuple-element.170.refs_0_.refs_1_, bf16[1024,1024]{1,0:T(8,128)(2,1)} %copy-done.33, bf16[1024,1024]{1,0:T(8,128)(2,1)} %collective-permute-done.4.refs_2_.refs_4_), custom_call_target="tpu_custom_call" | custom-call | tf_op jit(solution)/shard_map/project/pallas_call | solution.py:252
  42.9 5.6 %prep_grads.1 = (bf16[912,1024]{1,0:T(8,128)(2,1)}, bf16[912,256]{1,0:T(8,128)(2,1)}, bf16[912,768]{1,0:T(8,128)(2,1)}, f32[8,128]{1,0:T(8,128)}) custom-call(s32[2]{0:T(128)} %pad_add_fusion.refs_0_, bf16[12,150,1000]{2,1,0:T(8,128)(2,1)} %bitcast.87, bf16[12,150,1000]{2,1,0:T(8,128)(2,1)} %bitcast.88), custom_call_target="tpu_custom_call" | custom-call | tf_op jit(solution)/shard_map/prep_grads/pallas_call | solution.py:121
  48.5 2.9 collective-permute-done.7.refs_2_
  52.9 3.0 collective-permute-start.10
  55.9 12.9 %collective-permute-done.10.refs_2_ = bf16[128,1024]{1,0:T(8,128)(2,1)S(1)} collective-permute-done((bf16[128,1024]{1,0:T(8,128)(2,1)S(1)}, bf16[128,1024]{1,0:T(8,128)(2,1)S(1)}, u32[]{:S(2)}, u32[]{:S(2)}) %collective-permute-start.10) | collective-permute-done | bytes 262176 | tf_op jit(solution)/shard_map/ppermute | solution.py:823
  75.9 6.2 %project.5 = (f32[16,912,128]{2,1,0:T(8,128)}, f32[2,1024]{1,0:T(2,128)}) custom-call(bf16[912,512]{1,0:T(8,128)(2,1)} %copy-done.37, bf16[912,512]{1,0:T(8,128)(2,1)} %copy-done.38, bf16[512,1024]{1,0:T(8,128)(2,1)} %copy-done.6, bf16[512,1024]{1,0:T(8,128)(2,1)} %copy-done.7, ...), custom_call_target="tpu_custom_call", output_to_operand_aliasing={{0}: (4, {})} | custom-call | tf_op jit(solution)/shard_map/project/pallas_call | solution.py:252
  82.8 2.6 collective-permute-done.14.refs_5_.far_hbm0
  86.6 6.4 %project.6 = (f32[16,912,128]{2,1,0:T(8,128)}, f32[2,1024]{1,0:T(2,128)}) custom-call(bf16[912,512]{1,0:T(8,128)(2,1)} %copy-done.37, bf16[912,512]{1,0:T(8,128)(2,1)} %copy-done.38, bf16[512,1024]{1,0:T(8,128)(2,1)} %copy-done.41, bf16[512,1024]{1,0:T(8,128)(2,1)} %collective-permute-done.13.refs_3_.refs_4_, ...), custom_call_target="tpu_custom_call", output_to_operand_aliasing={{0}: (4, {})} | custom-call | tf_op jit(solution)/shard_map/project/pallas_call | solution.py:252
  112.2 20.5 %first_layer.1 = (bf16[912,2048]{1,0:T(8,128)(2,1)}, f32[16,912,128]{2,1,0:T(8,128)}, f32[1,2048]{1,0:T(1,128)}, f32[16,912,128]{2,1,0:T(8,128)}, f32[2,1024]{1,0:T(2,128)}) custom-call(f32[16,912,128]{2,1,0:T(8,128)} %get-tuple-element.200.proj_hbm.refs_11_.refs_3_, f32[2,2048]{1,0:T(2,128)} %add.146.sums.refs_12_.refs_4_, ...), custom_call_target="tpu_custom_call" | custom-call | tf_op jit(solution)/shard_map/first_layer/pallas_call | solution.py:424
  136.0 2.4 collective-permute-done.26.refs_7_.far_hbm1
  140.6 8.4 %project.7 = (f32[16,912,128]{2,1,0:T(8,128)}, f32[2,1024]{1,0:T(2,128)}) custom-call(bf16[912,2048]{1,0:T(8,128)(2,1)} %get-tuple-element.209.refs_0_.refs_1_.refs_2_.refs_10_, bf16[912,2048]{1,0:T(8,128)(2,1)} %get-tuple-element.209.refs_0_.refs_1_.refs_2_.refs_10_, ...), custom_call_target="tpu_custom_call", output_to_operand_aliasing={{0}: (6, {})} | custom-call | tf_op jit(solution)/shard_map/project/pallas_call | solution.py:252
  152.9 2.8 collective-permute-done.28
  161.9 2.7 collective-permute-done.30
  166.2 2.6 collective-permute-done.31
  170.1 22.1 %second_layer.1 = (bf16[912,1024]{1,0:T(8,128)(2,1)}, bf16[912,512]{1,0:T(8,128)(2,1)}, bf16[912,512]{1,0:T(8,128)(2,1)}, f32[16,912,128]{2,1,0:T(8,128)}, f32[3,2048]{1,0:T(4,128)}) custom-call(f32[16,912,128]{2,1,0:T(8,128)} %get-tuple-element.215.proj_hbm.refs_3_, f32[2,2048]{1,0:T(2,128)} %slice.233.sums.refs_4_, ...), custom_call_target="tpu_custom_call" | custom-call | tf_op jit(solution)/shard_map/second_layer/pallas_call | solution.py:488
  196.0 2.4 collective-permute-done.33
  199.7 2.8 collective-permute-done.35
  212.0 16.7 %weight_grad.4 = (bf16[912,2048]{1,0:T(8,128)(2,1)}, f32[1,2048]{1,0:T(1,128)}, bf16[1024,1024]{1,0:T(8,128)(2,1)}, bf16[1024,1024]{1,0:T(8,128)(2,1)}, f32[8,128]{1,0:T(8,128)}) custom-call(bf16[912,2048]{1,0:T(8,128)(2,1)} %get-tuple-element.209.refs_0_.refs_1_.refs_2_.refs_10_, f32[1,2048]{1,0:T(1,128)} %fusion.2.refs_1_, ...), custom_call_target="tpu_custom_call" | custom-call | tf_op jit(solution)/shard_map/weight_grad/pallas_call | solution.py:663
  230.8 8.4 %weight_grad.5 = (bf16[1024,1024]{1,0:T(8,128)(2,1)}, bf16[1024,1024]{1,0:T(8,128)(2,1)}, f32[8,128]{1,0:T(8,128)}) custom-call(bf16[912,2048]{1,0:T(8,128)(2,1)} %get-tuple-element.209.refs_0_.refs_1_.refs_2_.refs_10_, f32[1,2048]{1,0:T(1,128)} %fusion.2.refs_1_, bf16[912,2048]{1,0:T(8,128)(2,1)} %get-tuple-element.225.refs_2_.refs_0_), custom_call_target="tpu_custom_call" | custom-call | tf_op jit(solution)/shard_map/weight_grad/pallas_call | solution.py:663
  240.6 2.5 total.7
  244.4 3.6 fold.10
  249.7 3.4 collective-permute-done.34.refs_15_.refs_5_
  254.1 22.1 %first_back.1 = (f32[16,912,128]{2,1,0:T(8,128)}, f32[3,2048]{1,0:T(4,128)}) custom-call(bf16[912,2048]{1,0:T(8,128)(2,1)} %get-tuple-element.225.refs_2_.refs_0_, bf16[1024,1024]{1,0:T(8,128)(2,1)} %pad.14.top_hbm.refs_1_.refs_3_, bf16[1024,1024]{1,0:T(8,128)(2,1)} %copy-done, bf16[1024,1024]{1,0:T(8,128)(2,1)} %pad.14.top_hbm.refs_1_.refs_3_, ...), custom_call_target="tpu_custom_call" | custom-call | tf_op jit(solution)/shard_map/first_back/pallas_call | solution.py:552
  279.9 2.4 collective-permute-done.43
  286.4 2.9 fold.11
  296.5 2.9 collective-permute-done.46
  306.4 16.6 %weight_grad.6 = (bf16[912,2048]{1,0:T(8,128)(2,1)}, f32[1,2048]{1,0:T(1,128)}, bf16[1024,1024]{1,0:T(8,128)(2,1)}, bf16[1024,1024]{1,0:T(8,128)(2,1)}, f32[8,128]{1,0:T(8,128)}) custom-call(bf16[912,512]{1,0:T(8,128)(2,1)} %copy-done.37, bf16[912,512]{1,0:T(8,128)(2,1)} %copy-done.38, f32[16,912,128]{2,1,0:T(8,128)} %get-tuple-element.256.refs_2_, ...), custom_call_target="tpu_custom_call" | custom-call | tf_op jit(solution)/shard_map/weight_grad/pallas_call | solution.py:663
  325.6 8.4 %weight_grad.7 = (bf16[1024,1024]{1,0:T(8,128)(2,1)}, bf16[1024,1024]{1,0:T(8,128)(2,1)}, f32[8,128]{1,0:T(8,128)}) custom-call(bf16[912,1024]{1,0:T(8,128)(2,1)} %get-tuple-element.170.refs_0_.refs_1_, bf16[912,2048]{1,0:T(8,128)(2,1)} %get-tuple-element.262.refs_1_.refs_0_, f32[8,128]{1,0:T(8,128)} %copy-done.31), custom_call_target="tpu_custom_call" | custom-call | tf_op jit(solution)/shard_map/weight_grad/pallas_call | solution.py:663
  334.6 2.5 total.9
  339.9 3.5 fold.14
  346.6 8.8 %pull.2 = (bf16[912,1024]{1,0:T(8,128)(2,1)}, f32[8,128]{1,0:T(8,128)}) custom-call(bf16[912,2048]{1,0:T(8,128)(2,1)} %get-tuple-element.262.refs_1_.refs_0_, bf16[512,1024]{1,0:T(8,128)(2,1)} %copy-done.6, bf16[512,1024]{1,0:T(8,128)(2,1)} %copy-done.41, bf16[512,1024]{1,0:T(8,128)(2,1)} %copy-done.7, ...), custom_call_target="tpu_custom_call" | custom-call | tf_op jit(solution)/shard_map/pull/pallas_call | solution.py:708
  355.3 5.3 %collective-permute-done.51.refs_1_.refs_3_ = bf16[2,64,1024]{2,1,0:T(8,128)(2,1)S(1)} collective-permute-done((bf16[2,64,1024]{2,1,0:T(8,128)(2,1)}, bf16[2,64,1024]{2,1,0:T(8,128)(2,1)S(1)}, u32[]{:S(2)}, u32[]{:S(2)}) %collective-permute-start.51) | collective-permute-done | bytes 262176 | tf_op jit(solution)/shard_map/ppermute | solution.py:823
  364.5 4.5 combine.2
  371.3 2.9 fold.15
  378.7 9.0 %pull.3 = (f32[912,1024]{1,0:T(8,128)}, f32[8,128]{1,0:T(8,128)}) custom-call(bf16[912,2048]{1,0:T(8,128)(2,1)} %get-tuple-element.262.refs_1_.refs_0_, bf16[1024,1024]{1,0:T(8,128)(2,1)} %copy-done.33, bf16[1024,1024]{1,0:T(8,128)(2,1)} %collective-permute-done.4.refs_2_.refs_4_, bf16[1024,1024]{1,0:T(8,128)(2,1)} %copy-done.33, ...), custom_call_target="tpu_custom_call" | custom-call | tf_op jit(solution)/shard_map/pull/pallas_call | solution.py:708
  395.9 8.6 %collective-permute-done.61.refs_2_.refs_4_ = bf16[1,128,1024]{2,1,0:T(8,128)(2,1)S(1)} collective-permute-done((bf16[1,128,1024]{2,1,0:T(8,128)(2,1)S(1)}, bf16[1,128,1024]{2,1,0:T(8,128)(2,1)S(1)}, u32[]{:S(2)}, u32[]{:S(2)}) %collective-permute-start.61) | collective-permute-done | bytes 262176 | tf_op jit(solution)/shard_map/ppermute | solution.py:823
  409.4 7.9 %collective-permute-done.65.refs_1_ = bf16[1,64,1024]{2,1,0:T(8,128)(2,1)S(1)} collective-permute-done((bf16[1,64,1024]{2,1,0:T(8,128)(2,1)S(1)}, bf16[1,64,1024]{2,1,0:T(8,128)(2,1)S(1)}, u32[]{:S(2)}, u32[]{:S(2)}) %collective-permute-start.65) | collective-permute-done | bytes 131104 | tf_op jit(solution)/shard_map/ppermute | solution.py:823
  420.9 6.5 %collective-permute-done.67.refs_2_ = bf16[64,1024]{1,0:T(8,128)(2,1)S(1)} collective-permute-done((bf16[64,1024]{1,0:T(8,128)(2,1)S(1)}, bf16[64,1024]{1,0:T(8,128)(2,1)S(1)}, u32[]{:S(2)}, u32[]{:S(2)}) %collective-permute-start.67) | collective-permute-done | bytes 131104 | tf_op jit(solution)/shard_map/ppermute | solution.py:823
  431.2 4.6 %collective-permute-done.69.refs_2_ = bf16[128,1024]{1,0:T(8,128)(2,1)S(1)} collective-permute-done((bf16[128,1024]{1,0:T(8,128)(2,1)S(1)}, bf16[128,1024]{1,0:T(8,128)(2,1)S(1)}, u32[]{:S(2)}, u32[]{:S(2)}) %collective-permute-start.69) | collective-permute-done | bytes 262176 | tf_op jit(solution)/shard_map/ppermute | solution.py:823
  441.0 2.6 multiply_add_fusion
  445.2 4.5 combine.3
  449.8 5.5 %collective-permute-done.70.refs_2_ = bf16[256,1024]{1,0:T(8,128)(2,1)S(1)} collective-permute-done((bf16[256,1024]{1,0:T(8,128)(2,1)S(1)}, bf16[256,1024]{1,0:T(8,128)(2,1)S(1)}, u32[]{:S(2)}, u32[]{:S(2)}) %collective-permute-start.70) | collective-permute-done | bytes 524320 | tf_op jit(solution)/shard_map/ppermute | solution.py:823
  456.0 2.4 fusion
  (324 shorter events, 155.3 us)
Async XLA Ops:
  5.7 22.1 %collective-permute-start.4 = (bf16[1024,1024]{1,0:T(8,128)(2,1)S(1)}, bf16[1024,1024]{1,0:T(8,128)(2,1)}, u32[]{:S(2)}, u32[]{:S(2)}) collective-permute-start(bf16[1024,1024]{1,0:T(8,128)(2,1)S(1)} %pad.15.refs_1_.refs_3_), channel_id=1, source_target_pairs={{0,1},{1,0},{2,3},{3,2},{4,5},{5,4},{6,7},{7,6},{8,9},{9,8},{10,11... | collective-permute-start | bytes 6291464 | tf_op jit(solution)/shard_map/ppermute | solution.py:818
  6.2 12.8 %collective-permute-start = (bf16[128,1024]{1,0:T(8,128)(2,1)S(1)}, bf16[128,1024]{1,0:T(8,128)(2,1)S(1)}, u32[]{:S(2)}, u32[]{:S(2)}) collective-permute-start(bf16[128,1024]{1,0:T(8,128)(2,1)S(1)} %copy-done.47), channel_id=1, source_target_pairs={{0,2},{2,0},{1,3},{3,1},{4,6},{6,4},{5,7},{7,5},{8,10},{10,8},{9,1... | collective-permute-start | bytes 786440 | tf_op jit(solution)/shard_map/ppermute | solution.py:818
  8.8 12.5 %collective-permute-start.1 = (bf16[128,1024]{1,0:T(8,128)(2,1)S(1)}, bf16[128,1024]{1,0:T(8,128)(2,1)S(1)}, u32[]{:S(2)}, u32[]{:S(2)}) collective-permute-start(bf16[128,1024]{1,0:T(8,128)(2,1)S(1)} %copy-done.46), channel_id=1, source_target_pairs={{0,2},{2,0},{1,3},{3,1},{4,6},{6,4},{5,7},{7,5},{8,10},{10,8},{9,1... | collective-permute-start | bytes 786440 | tf_op jit(solution)/shard_map/ppermute | solution.py:818
  21.3 31.0 %collective-permute-start.2 = (bf16[912,512]{1,0:T(8,128)(2,1)S(1)}, bf16[912,512]{1,0:T(8,128)(2,1)S(1)}, u32[]{:S(2)}, u32[]{:S(2)}) collective-permute-start(bf16[912,512]{1,0:T(8,128)(2,1)S(1)} %copy-done.15), channel_id=1, source_target_pairs={{0,2},{2,0},{1,3},{3,1},{4,6},{6,4},{5,7},{7,5},{8,10},{10,8},{9,1... | collective-permute-start | bytes 2801672 | tf_op jit(solution)/shard_map/ppermute | solution.py:818
  23.1 48.7 %collective-permute-start.8 = (bf16[912,512]{1,0:T(8,128)(2,1)}, bf16[912,512]{1,0:T(8,128)(2,1)S(1)}, u32[]{:S(2)}, u32[]{:S(2)}) collective-permute-start(bf16[912,512]{1,0:T(8,128)(2,1)} %get-tuple-element.185.refs_4_), channel_id=1, source_target_pairs={{0,2},{2,0},{1,3},{3,1},{4,6},{6,4},{5,7},{7,5},{8,10},{10,8},{9,1... | collective-permute-start | bytes 2801672 | tf_op jit(solution)/shard_map/ppermute | solution.py:818
  23.4 13.4 %collective-permute-start.6 = (bf16[64,1024]{1,0:T(8,128)(2,1)S(1)}, bf16[64,1024]{1,0:T(8,128)(2,1)S(1)}, u32[]{:S(2)}, u32[]{:S(2)}) collective-permute-start(bf16[64,1024]{1,0:T(8,128)(2,1)S(1)} %get-tuple-element.326.refs_1_), channel_id=1, source_target_pairs={{0,4},{4,0},{8,12},{12,8},{16,20},{20,16},{24,28},{28,24},{1,5},{5... | collective-permute-start | bytes 393224 | tf_op jit(solution)/shard_map/ppermute | solution.py:823
  25.2 13.3 %collective-permute-start.3 = (bf16[64,1024]{1,0:T(8,128)(2,1)S(1)}, bf16[64,1024]{1,0:T(8,128)(2,1)S(1)}, u32[]{:S(2)}, u32[]{:S(2)}) collective-permute-start(bf16[64,1024]{1,0:T(8,128)(2,1)S(1)} %get-tuple-element.327.refs_1_), channel_id=1, source_target_pairs={{0,16},{4,20},{8,24},{12,28},{16,0},{20,4},{24,8},{28,12},{1,17},{... | collective-permute-start | bytes 393224 | tf_op jit(solution)/shard_map/ppermute | solution.py:823
  38.1 13.3 %collective-permute-start.7 = (bf16[128,1024]{1,0:T(8,128)(2,1)S(1)}, bf16[128,1024]{1,0:T(8,128)(2,1)S(1)}, u32[]{:S(2)}, u32[]{:S(2)}) collective-permute-start(bf16[128,1024]{1,0:T(8,128)(2,1)S(1)} %get-tuple-element.182.refs_1_), channel_id=1, source_target_pairs={{0,16},{4,20},{8,24},{12,28},{16,0},{20,4},{24,8},{28,12},{1,17},{... | collective-permute-start | bytes 786440 | tf_op jit(solution)/shard_map/ppermute | solution.py:823
  39.1 13.1 %collective-permute-start.5 = (bf16[128,1024]{1,0:T(8,128)(2,1)S(1)}, bf16[128,1024]{1,0:T(8,128)(2,1)S(1)}, u32[]{:S(2)}, u32[]{:S(2)}) collective-permute-start(bf16[128,1024]{1,0:T(8,128)(2,1)S(1)} %get-tuple-element.179.refs_1_), channel_id=1, source_target_pairs={{0,8},{4,12},{8,0},{12,4},{16,24},{20,28},{24,16},{28,20},{1,9},{5... | collective-permute-start | bytes 786440 | tf_op jit(solution)/shard_map/ppermute | solution.py:823
  52.3 16.6 %collective-permute-start.9 = (bf16[256,1024]{1,0:T(8,128)(2,1)S(1)}, bf16[256,1024]{1,0:T(8,128)(2,1)S(1)}, u32[]{:S(2)}, u32[]{:S(2)}) collective-permute-start(bf16[256,1024]{1,0:T(8,128)(2,1)S(1)} %get-tuple-element.186.refs_1_), channel_id=1, source_target_pairs={{0,4},{4,0},{8,12},{12,8},{16,20},{20,16},{24,28},{28,24},{1,5},{5... | collective-permute-start | bytes 1572872 | tf_op jit(solution)/shard_map/ppermute | solution.py:823
  52.9 18.2 %collective-permute-start.11 = (bf16[256,1024]{1,0:T(8,128)(2,1)S(1)}, bf16[256,1024]{1,0:T(8,128)(2,1)S(1)}, u32[]{:S(2)}, u32[]{:S(2)}) collective-permute-start(bf16[256,1024]{1,0:T(8,128)(2,1)S(1)} %get-tuple-element.192.refs_1_), channel_id=1, source_target_pairs={{0,8},{4,12},{8,0},{12,4},{16,24},{20,28},{24,16},{28,20},{1,9},{5... | collective-permute-start | bytes 1572872 | tf_op jit(solution)/shard_map/ppermute | solution.py:823
  52.9 15.9 %collective-permute-start.10 = (bf16[128,1024]{1,0:T(8,128)(2,1)S(1)}, bf16[128,1024]{1,0:T(8,128)(2,1)S(1)}, u32[]{:S(2)}, u32[]{:S(2)}) collective-permute-start(bf16[128,1024]{1,0:T(8,128)(2,1)S(1)} %collective-permute-done.1.refs_1_), channel_id=1, source_target_pairs={{0,16},{4,20},{8,24},{12,28},{16,0},{20,4},{24,8},{28,12},{1,17},{... | collective-permute-start | bytes 786440 | tf_op jit(solution)/shard_map/ppermute | solution.py:823
  71.8 13.6 %collective-permute-start.12 = (bf16[512,1024]{1,0:T(8,128)(2,1)S(1)}, bf16[512,1024]{1,0:T(8,128)(2,1)S(1)}, u32[]{:S(2)}, u32[]{:S(2)}) collective-permute-start(bf16[512,1024]{1,0:T(8,128)(2,1)S(1)} %get-tuple-element.195.refs_2_.refs_1_), channel_id=1, source_target_pairs={{0,1},{1,0},{2,3},{3,2},{4,5},{5,4},{6,7},{7,6},{8,9},{9,8},{10,11... | collective-permute-start | bytes 3145736 | tf_op jit(solution)/shard_map/ppermute | solution.py:818
  71.8 13.6 %collective-permute-start.13 = (bf16[512,1024]{1,0:T(8,128)(2,1)S(1)}, bf16[512,1024]{1,0:T(8,128)(2,1)}, u32[]{:S(2)}, u32[]{:S(2)}) collective-permute-start(bf16[512,1024]{1,0:T(8,128)(2,1)S(1)} %get-tuple-element.196.refs_3_), channel_id=1, source_target_pairs={{0,1},{1,0},{2,3},{3,2},{4,5},{5,4},{6,7},{7,6},{8,9},{9,8},{10,11... | collective-permute-start | bytes 3145736 | tf_op jit(solution)/shard_map/ppermute | solution.py:818
  72.3 39.9 %collective-permute-start.22 = (bf16[1024,1024]{1,0:T(8,128)(2,1)}, bf16[1024,1024]{1,0:T(8,128)(2,1)}, u32[]{:S(2)}, u32[]{:S(2)}) collective-permute-start(bf16[1024,1024]{1,0:T(8,128)(2,1)} %pad.14.top_hbm.refs_1_.refs_3_), channel_id=1, source_target_pairs={{0,1},{1,0},{2,3},{3,2},{4,5},{5,4},{6,7},{7,6},{8,9},{9,8},{10,11... | collective-permute-start | bytes 6291464 | tf_op jit(solution)/shard_map/ppermute | solution.py:818
  72.4 13.0 %collective-permute-start.14 = (bf16[912,256]{1,0:T(8,128)(2,1)S(1)}, bf16[912,256]{1,0:T(8,128)(2,1)S(1)}, u32[]{:S(2)}, u32[]{:S(2)}) collective-permute-start(bf16[912,256]{1,0:T(8,128)(2,1)S(1)} %copy-done.18), channel_id=1, source_target_pairs={{0,2},{2,0},{1,3},{3,1},{4,6},{6,4},{5,7},{7,5},{8,10},{10,8},{9,1... | collective-permute-start | bytes 1400840 | tf_op jit(solution)/shard_map/ppermute | solution.py:818
  73.8 25.2 %collective-permute-start.17 = (bf16[256,1024]{1,0:T(8,128)(2,1)S(1)}, bf16[256,1024]{1,0:T(8,128)(2,1)S(1)}, u32[]{:S(2)}, u32[]{:S(2)}) collective-permute-start(bf16[256,1024]{1,0:T(8,128)(2,1)S(1)} %get-tuple-element.205.refs_1_), channel_id=1, source_target_pairs={{0,8},{4,12},{8,0},{12,4},{16,24},{20,28},{24,16},{28,20},{1,9},{5... | collective-permute-start | bytes 1572872 | tf_op jit(solution)/shard_map/ppermute | solution.py:823
  101.4 31.3 %collective-permute-start.23 = (bf16[512,1024]{1,0:T(8,128)(2,1)S(1)}, bf16[512,1024]{1,0:T(8,128)(2,1)S(1)}, u32[]{:S(2)}, u32[]{:S(2)}) collective-permute-start(bf16[512,1024]{1,0:T(8,128)(2,1)S(1)} %get-tuple-element.210.refs_1_), channel_id=1, source_target_pairs={{0,4},{4,0},{8,12},{12,8},{16,20},{20,16},{24,28},{28,24},{1,5},{5... | collective-permute-start | bytes 3145736 | tf_op jit(solution)/shard_map/ppermute | solution.py:823
  105.2 33.1 %collective-permute-start.26 = (bf16[912,768]{1,0:T(8,128)(2,1)S(1)}, bf16[912,768]{1,0:T(8,128)(2,1)S(1)}, u32[]{:S(2)}, u32[]{:S(2)}) collective-permute-start(bf16[912,768]{1,0:T(8,128)(2,1)S(1)} %copy-done.13), channel_id=1, source_target_pairs={{0,2},{2,0},{1,3},{3,1},{4,6},{6,4},{5,7},{7,5},{8,10},{10,8},{9,1... | collective-permute-start | bytes 4202504 | tf_op jit(solution)/shard_map/ppermute | solution.py:818
  228.7 10.5 %collective-permute-start.39 = (bf16[1024,1024]{1,0:T(8,128)(2,1)}, bf16[1024,1024]{1,0:T(8,128)(2,1)S(1)}, u32[]{:S(2)}, u32[]{:S(2)}) collective-permute-start(bf16[1024,1024]{1,0:T(8,128)(2,1)} %get-tuple-element.230), channel_id=1, source_target_pairs={{0,1},{1,0},{2,3},{3,2},{4,5},{5,4},{6,7},{7,6},{8,9},{9,8},{10,11... | collective-permute-start | bytes 6291464 | tf_op jit(solution)/shard_map/ppermute | solution.py:818
  228.8 14.3 %collective-permute-start.38 = (bf16[1024,1024]{1,0:T(8,128)(2,1)}, bf16[1024,1024]{1,0:T(8,128)(2,1)S(1)}, u32[]{:S(2)}, u32[]{:S(2)}) collective-permute-start(bf16[1024,1024]{1,0:T(8,128)(2,1)} %get-tuple-element.228), channel_id=1, source_target_pairs={{0,1},{1,0},{2,3},{3,2},{4,5},{5,4},{6,7},{7,6},{8,9},{9,8},{10,11... | collective-permute-start | bytes 6291464 | tf_op jit(solution)/shard_map/ppermute | solution.py:818
  229.3 23.8 %collective-permute-start.34 = (bf16[912,512]{1,0:T(8,128)(2,1)}, bf16[912,512]{1,0:T(8,128)(2,1)S(1)}, u32[]{:S(2)}, u32[]{:S(2)}) collective-permute-start(bf16[912,512]{1,0:T(8,128)(2,1)} %get-tuple-element.222), channel_id=1, source_target_pairs={{0,2},{2,0},{1,3},{3,1},{4,6},{6,4},{5,7},{7,5},{8,10},{10,8},{9,1... | collective-permute-start | bytes 2801672 | tf_op jit(solution)/shard_map/ppermute | solution.py:818
  248.0 28.9 %collective-permute-start.40 = (bf16[2,256,1024]{2,1,0:T(8,128)(2,1)}, bf16[2,256,1024]{2,1,0:T(8,128)(2,1)S(1)}, u32[]{:S(2)}, u32[]{:S(2)}) collective-permute-start(bf16[2,256,1024]{2,1,0:T(8,128)(2,1)} %get-tuple-element.236), channel_id=1, source_target_pairs={{0,4},{4,0},{8,12},{12,8},{16,20},{20,16},{24,28},{28,24},{1,5},{5... | collective-permute-start | bytes 3145736 | tf_op jit(solution)/shard_map/ppermute | solution.py:823
  249.2 27.8 %collective-permute-start.41 = (bf16[512,1024]{1,0:T(8,128)(2,1)S(1)}, bf16[512,1024]{1,0:T(8,128)(2,1)S(1)}, u32[]{:S(2)}, u32[]{:S(2)}) collective-permute-start(bf16[512,1024]{1,0:T(8,128)(2,1)S(1)} %bitcast.111), channel_id=1, source_target_pairs={{0,2},{2,0},{1,3},{3,1},{4,6},{6,4},{5,7},{7,5},{8,10},{10,8},{9,1... | collective-permute-start | bytes 3145736 | tf_op jit(solution)/shard_map/ppermute | solution.py:818
  283.9 17.6 %collective-permute-start.49 = (bf16[256,1024]{1,0:T(8,128)(2,1)S(1)}, bf16[256,1024]{1,0:T(8,128)(2,1)S(1)}, u32[]{:S(2)}, u32[]{:S(2)}) collective-permute-start(bf16[256,1024]{1,0:T(8,128)(2,1)S(1)} %bitcast.60), channel_id=1, source_target_pairs={{0,2},{2,0},{1,3},{3,1},{4,6},{6,4},{5,7},{7,5},{8,10},{10,8},{9,1... | collective-permute-start | bytes 1572872 | tf_op jit(solution)/shard_map/ppermute | solution.py:818
  289.3 12.2 %collective-permute-start.48 = (bf16[1,256,1024]{2,1,0:T(8,128)(2,1)}, bf16[1,256,1024]{2,1,0:T(8,128)(2,1)S(1)}, u32[]{:S(2)}, u32[]{:S(2)}) collective-permute-start(bf16[1,256,1024]{2,1,0:T(8,128)(2,1)} %get-tuple-element.251), channel_id=1, source_target_pairs={{0,4},{4,0},{8,12},{12,8},{16,20},{20,16},{24,28},{28,24},{1,5},{5... | collective-permute-start | bytes 1572872 | tf_op jit(solution)/shard_map/ppermute | solution.py:823
  300.0 23.2 %collective-permute-start.47 = (bf16[912,512]{1,0:T(8,128)(2,1)}, bf16[912,512]{1,0:T(8,128)(2,1)S(1)}, u32[]{:S(2)}, u32[]{:S(2)}) collective-permute-start(bf16[912,512]{1,0:T(8,128)(2,1)} %get-tuple-element.249), channel_id=1, source_target_pairs={{0,2},{2,0},{1,3},{3,1},{4,6},{6,4},{5,7},{7,5},{8,10},{10,8},{9,1... | collective-permute-start | bytes 2801672 | tf_op jit(solution)/shard_map/ppermute | solution.py:818
  304.3 18.8 %collective-permute-start.50 = (bf16[2,128,1024]{2,1,0:T(8,128)(2,1)S(1)}, bf16[2,128,1024]{2,1,0:T(8,128)(2,1)S(1)}, u32[]{:S(2)}, u32[]{:S(2)}) collective-permute-start(bf16[2,128,1024]{2,1,0:T(8,128)(2,1)S(1)} %get-tuple-element.255), channel_id=1, source_target_pairs={{0,8},{4,12},{8,0},{12,4},{16,24},{20,28},{24,16},{28,20},{1,9},{5... | collective-permute-start | bytes 1572872 | tf_op jit(solution)/shard_map/ppermute | solution.py:823
  323.1 11.5 %collective-permute-start.53 = (bf16[1024,1024]{1,0:T(8,128)(2,1)}, bf16[1024,1024]{1,0:T(8,128)(2,1)}, u32[]{:S(2)}, u32[]{:S(2)}) collective-permute-start(bf16[1024,1024]{1,0:T(8,128)(2,1)} %get-tuple-element.267), channel_id=1, source_target_pairs={{0,1},{1,0},{2,3},{3,2},{4,5},{5,4},{6,7},{7,6},{8,9},{9,8},{10,11... | collective-permute-start | bytes 6291464 | tf_op jit(solution)/shard_map/ppermute | solution.py:818
  343.5 25.7 %collective-permute-start.56 = (bf16[2,256,1024]{2,1,0:T(8,128)(2,1)}, bf16[2,256,1024]{2,1,0:T(8,128)(2,1)S(1)}, u32[]{:S(2)}, u32[]{:S(2)}) collective-permute-start(bf16[2,256,1024]{2,1,0:T(8,128)(2,1)} %get-tuple-element.277), channel_id=1, source_target_pairs={{0,4},{4,0},{8,12},{12,8},{16,20},{20,16},{24,28},{28,24},{1,5},{5... | collective-permute-start | bytes 3145736 | tf_op jit(solution)/shard_map/ppermute | solution.py:823
  344.5 26.9 %collective-permute-start.55 = (bf16[512,1024]{1,0:T(8,128)(2,1)}, bf16[512,1024]{1,0:T(8,128)(2,1)}, u32[]{:S(2)}, u32[]{:S(2)}) collective-permute-start(bf16[512,1024]{1,0:T(8,128)(2,1)} %bitcast.30), channel_id=1, source_target_pairs={{0,2},{2,0},{1,3},{3,1},{4,6},{6,4},{5,7},{7,5},{8,10},{10,8},{9,1... | collective-permute-start | bytes 3145736 | tf_op jit(solution)/shard_map/ppermute | solution.py:818
  345.9 14.7 %collective-permute-start.51 = (bf16[2,64,1024]{2,1,0:T(8,128)(2,1)}, bf16[2,64,1024]{2,1,0:T(8,128)(2,1)S(1)}, u32[]{:S(2)}, u32[]{:S(2)}) collective-permute-start(bf16[2,64,1024]{2,1,0:T(8,128)(2,1)} %get-tuple-element.261), channel_id=1, source_target_pairs={{0,16},{4,20},{8,24},{12,28},{16,0},{20,4},{24,8},{28,12},{1,17},{... | collective-permute-start | bytes 786440 | tf_op jit(solution)/shard_map/ppermute | solution.py:823
  362.1 13.7 %collective-permute-start.54 = (bf16[128,1024]{1,0:T(8,128)(2,1)}, bf16[128,1024]{1,0:T(8,128)(2,1)}, u32[]{:S(2)}, u32[]{:S(2)}) collective-permute-start(bf16[128,1024]{1,0:T(8,128)(2,1)} %bitcast.29.refs_1_), channel_id=1, source_target_pairs={{0,16},{4,20},{8,24},{12,28},{16,0},{20,4},{24,8},{28,12},{1,17},{... | collective-permute-start | bytes 786440 | tf_op jit(solution)/shard_map/ppermute | solution.py:823
  370.0 17.7 %collective-permute-start.57 = (bf16[256,1024]{1,0:T(8,128)(2,1)S(1)}, bf16[256,1024]{1,0:T(8,128)(2,1)S(1)}, u32[]{:S(2)}, u32[]{:S(2)}) collective-permute-start(bf16[256,1024]{1,0:T(8,128)(2,1)S(1)} %bitcast.61), channel_id=1, source_target_pairs={{0,2},{2,0},{1,3},{3,1},{4,6},{6,4},{5,7},{7,5},{8,10},{10,8},{9,1... | collective-permute-start | bytes 1572872 | tf_op jit(solution)/shard_map/ppermute | solution.py:818
  374.2 14.8 %collective-permute-start.59 = (bf16[1,256,1024]{2,1,0:T(8,128)(2,1)}, bf16[1,256,1024]{2,1,0:T(8,128)(2,1)S(1)}, u32[]{:S(2)}, u32[]{:S(2)}) collective-permute-start(bf16[1,256,1024]{2,1,0:T(8,128)(2,1)} %get-tuple-element.289), channel_id=1, source_target_pairs={{0,4},{4,0},{8,12},{12,8},{16,20},{20,16},{24,28},{28,24},{1,5},{5... | collective-permute-start | bytes 1572872 | tf_op jit(solution)/shard_map/ppermute | solution.py:823
  378.2 13.9 %collective-permute-start.62 = (bf16[256,1024]{1,0:T(8,128)(2,1)S(1)}, bf16[256,1024]{1,0:T(8,128)(2,1)S(1)}, u32[]{:S(2)}, u32[]{:S(2)}) collective-permute-start(bf16[256,1024]{1,0:T(8,128)(2,1)S(1)} %get-tuple-element.295.refs_1_), channel_id=1, source_target_pairs={{0,8},{4,12},{8,0},{12,4},{16,24},{20,28},{24,16},{28,20},{1,9},{5... | collective-permute-start | bytes 1572872 | tf_op jit(solution)/shard_map/ppermute | solution.py:823
  392.2 25.4 %collective-permute-start.64 = (bf16[512,1024]{1,0:T(8,128)(2,1)S(1)}, bf16[512,1024]{1,0:T(8,128)(2,1)S(1)}, u32[]{:S(2)}, u32[]{:S(2)}) collective-permute-start(bf16[512,1024]{1,0:T(8,128)(2,1)S(1)} %get-tuple-element.301.refs_1_), channel_id=1, source_target_pairs={{0,4},{4,0},{8,12},{12,8},{16,20},{20,16},{24,28},{28,24},{1,5},{5... | collective-permute-start | bytes 3145736 | tf_op jit(solution)/shard_map/ppermute | solution.py:823
  393.1 50.4 %collective-permute-start.58 = (bf16[912,1024]{1,0:T(8,128)(2,1)S(1)}, bf16[912,1024]{1,0:T(8,128)(2,1)S(1)}, u32[]{:S(2)}, u32[]{:S(2)}) collective-permute-start(bf16[912,1024]{1,0:T(8,128)(2,1)S(1)} %copy-done.57), channel_id=1, source_target_pairs={{0,2},{2,0},{1,3},{3,1},{4,6},{6,4},{5,7},{7,5},{8,10},{10,8},{9,1... | collective-permute-start | bytes 5603336 | tf_op jit(solution)/shard_map/ppermute | solution.py:818
  393.8 10.6 %collective-permute-start.61 = (bf16[1,128,1024]{2,1,0:T(8,128)(2,1)S(1)}, bf16[1,128,1024]{2,1,0:T(8,128)(2,1)S(1)}, u32[]{:S(2)}, u32[]{:S(2)}) collective-permute-start(bf16[1,128,1024]{2,1,0:T(8,128)(2,1)S(1)} %get-tuple-element.294), channel_id=1, source_target_pairs={{0,8},{4,12},{8,0},{12,4},{16,24},{20,28},{24,16},{28,20},{1,9},{5... | collective-permute-start | bytes 786440 | tf_op jit(solution)/shard_map/ppermute | solution.py:823
  394.2 13.5 %collective-permute-start.60 = (bf16[1,128,1024]{2,1,0:T(8,128)(2,1)S(1)}, bf16[1,128,1024]{2,1,0:T(8,128)(2,1)S(1)}, u32[]{:S(2)}, u32[]{:S(2)}) collective-permute-start(bf16[1,128,1024]{2,1,0:T(8,128)(2,1)S(1)} %get-tuple-element.292), channel_id=1, source_target_pairs={{0,8},{4,12},{8,0},{12,4},{16,24},{20,28},{24,16},{28,20},{1,9},{5... | collective-permute-start | bytes 786440 | tf_op jit(solution)/shard_map/ppermute | solution.py:823
  404.8 12.6 %collective-permute-start.65 = (bf16[1,64,1024]{2,1,0:T(8,128)(2,1)S(1)}, bf16[1,64,1024]{2,1,0:T(8,128)(2,1)S(1)}, u32[]{:S(2)}, u32[]{:S(2)}) collective-permute-start(bf16[1,64,1024]{2,1,0:T(8,128)(2,1)S(1)} %get-tuple-element.303), channel_id=1, source_target_pairs={{0,16},{4,20},{8,24},{12,28},{16,0},{20,4},{24,8},{28,12},{1,17},{... | collective-permute-start | bytes 393224 | tf_op jit(solution)/shard_map/ppermute | solution.py:823
  408.0 12.2 %collective-permute-start.63 = (bf16[1,64,1024]{2,1,0:T(8,128)(2,1)S(1)}, bf16[1,64,1024]{2,1,0:T(8,128)(2,1)S(1)}, u32[]{:S(2)}, u32[]{:S(2)}) collective-permute-start(bf16[1,64,1024]{2,1,0:T(8,128)(2,1)S(1)} %get-tuple-element.300), channel_id=1, source_target_pairs={{0,16},{4,20},{8,24},{12,28},{16,0},{20,4},{24,8},{28,12},{1,17},{... | collective-permute-start | bytes 393224 | tf_op jit(solution)/shard_map/ppermute | solution.py:823
  417.5 9.9 %collective-permute-start.67 = (bf16[64,1024]{1,0:T(8,128)(2,1)S(1)}, bf16[64,1024]{1,0:T(8,128)(2,1)S(1)}, u32[]{:S(2)}, u32[]{:S(2)}) collective-permute-start(bf16[64,1024]{1,0:T(8,128)(2,1)S(1)} %bitcast.56), channel_id=1, source_target_pairs={{0,16},{4,20},{8,24},{12,28},{16,0},{20,4},{24,8},{28,12},{1,17},{... | collective-permute-start | bytes 393224 | tf_op jit(solution)/shard_map/ppermute | solution.py:823
  420.3 8.5 %collective-permute-start.66 = (bf16[64,1024]{1,0:T(8,128)(2,1)S(1)}, bf16[64,1024]{1,0:T(8,128)(2,1)S(1)}, u32[]{:S(2)}, u32[]{:S(2)}) collective-permute-start(bf16[64,1024]{1,0:T(8,128)(2,1)S(1)} %bitcast.58), channel_id=1, source_target_pairs={{0,16},{4,20},{8,24},{12,28},{16,0},{20,4},{24,8},{28,12},{1,17},{... | collective-permute-start | bytes 393224 | tf_op jit(solution)/shard_map/ppermute | solution.py:823
  427.5 8.3 %collective-permute-start.69 = (bf16[128,1024]{1,0:T(8,128)(2,1)S(1)}, bf16[128,1024]{1,0:T(8,128)(2,1)S(1)}, u32[]{:S(2)}, u32[]{:S(2)}) collective-permute-start(bf16[128,1024]{1,0:T(8,128)(2,1)S(1)} %get-tuple-element.312.refs_1_), channel_id=1, source_target_pairs={{0,8},{4,12},{8,0},{12,4},{16,24},{20,28},{24,16},{28,20},{1,9},{5... | collective-permute-start | bytes 786440 | tf_op jit(solution)/shard_map/ppermute | solution.py:823
  428.9 9.7 %collective-permute-start.68 = (bf16[128,1024]{1,0:T(8,128)(2,1)S(1)}, bf16[128,1024]{1,0:T(8,128)(2,1)S(1)}, u32[]{:S(2)}, u32[]{:S(2)}) collective-permute-start(bf16[128,1024]{1,0:T(8,128)(2,1)S(1)} %get-tuple-element.311.refs_1_), channel_id=1, source_target_pairs={{0,8},{4,12},{8,0},{12,4},{16,24},{20,28},{24,16},{28,20},{1,9},{5... | collective-permute-start | bytes 786440 | tf_op jit(solution)/shard_map/ppermute | solution.py:823
  435.8 13.8 %collective-permute-start.71 = (bf16[256,1024]{1,0:T(8,128)(2,1)S(1)}, bf16[256,1024]{1,0:T(8,128)(2,1)S(1)}, u32[]{:S(2)}, u32[]{:S(2)}) collective-permute-start(bf16[256,1024]{1,0:T(8,128)(2,1)S(1)} %get-tuple-element.318.refs_1_), channel_id=1, source_target_pairs={{0,4},{4,0},{8,12},{12,8},{16,20},{20,16},{24,28},{28,24},{1,5},{5... | collective-permute-start | bytes 1572872 | tf_op jit(solution)/shard_map/ppermute | solution.py:823
  438.7 16.6 %collective-permute-start.70 = (bf16[256,1024]{1,0:T(8,128)(2,1)S(1)}, bf16[256,1024]{1,0:T(8,128)(2,1)S(1)}, u32[]{:S(2)}, u32[]{:S(2)}) collective-permute-start(bf16[256,1024]{1,0:T(8,128)(2,1)S(1)} %get-tuple-element.317.refs_1_), channel_id=1, source_target_pairs={{0,4},{4,0},{8,12},{12,8},{16,20},{20,16},{24,28},{28,24},{1,5},{5... | collective-permute-start | bytes 1572872 | tf_op jit(solution)/shard_map/ppermute | solution.py:823
  (84 other events, 522.4 us)

commit v2 on v1

--- a/solution.py
+++ b/solution.py
@@ -290,12 +290,11 @@
         for j in range(tiles):
             arg = norm[j, at, :] + recur[j] * before[j]
             poly = gelu_inner * (arg * arg) + gelu_outer
-            tanh = jnp.tanh(arg * poly)
-            half = 0.5 * arg
-            state = half + half * tanh
+            gate = 0.5 * jnp.tanh(arg * poly) + 0.5
+            state = arg * gate
             states[j, at, :] = state
-            inner = 3.0 * poly - 2.0 * gelu_outer
-            slopes[j, at, :] = (0.5 * tanh + 0.5) + half * (1.0 - tanh * tanh) * inner
+            inner = 6.0 * poly - 4.0 * gelu_outer
+            slopes[j, at, :] = gate + state * (1.0 - gate) * inner
             now.append(state)
         return tuple(now)
 
@@ -503,13 +502,17 @@
 
 
 def first_back_kernel(
-    steps, seqs, count, nb, low, *refs,
+    steps, seqs, count, blocks, low, *refs,
 ):
+    nb = len(blocks)
     weights, refs = refs[: 2 * nb], refs[2 * nb :]
-    slopes_hbm, hidden_hbm, proj_hbm, sums, gains, grads_out, out, grads, slopes, hidden, proj, shifted, sems = refs
+    (
+        slopes_hbm, hidden_hbm, proj_hbm, sums, gains, grads_out, out,
+        grads, slopes, hidden, proj, shifted, held_blocks, sems, block_sems,
+    ) = refs
     tiles = proj.shape[0]
-    half = weights[0].shape[1]
     j = pl.program_id(0)
+    fetches = fetch_blocks(blocks, weights, held_blocks, block_sems)
     copies = [
         pltpu.make_async_copy(slopes_hbm, slopes, sems.at[0]),
         pltpu.make_async_copy(hidden_hbm, hidden, sems.at[1]),
@@ -518,16 +521,14 @@
 
     @pl.when(j == 0)
     def _():
-        for copy in copies:
+        for copy in fetches + copies:
             copy.start()
 
-    def go(left, right):
-        acc = dot(low[:, :half], left[...], ((1,), (1,))) + dot(low[:, half:], right[...], ((1,), (1,)))
+    @pl.when(j < nb)
+    def _():
+        acc = block_product(low, held_blocks, block_sems, j)
         for k in range(WIDE // LANES):
             grads[j * (WIDE // LANES) + k] = acc[:, k * LANES : (k + 1) * LANES]
-
-    for k in range(nb):
-        pl.when(j == k)(functools.partial(go, *weights[2 * k : 2 * k + 2]))
 
     @pl.when(j == nb)
     def _():
@@ -548,9 +549,9 @@
     nb = len(blocks)
     hbm = pl.BlockSpec(memory_space=pl.ANY)
     operands = [x for pair in blocks for x, _ in pair]
-    weights = [pl.BlockSpec((WIDE, half), lambda j, at=at: (at, 0)) for pair in blocks for _, at in pair]
+    weights = [hbm] * len(operands)
     return pl.pallas_call(
-        without(functools.partial(first_back_kernel, steps, seqs, count, nb), 6 + 2 * nb, len(deps)),
+        without(functools.partial(first_back_kernel, steps, seqs, count, blocks), 6 + 2 * nb, len(deps)),
         grid=(nb + 1,),
         in_specs=[whole((rows, width)), *weights, hbm, hbm, hbm, whole((2, width)), whole((3, width))] + after(deps),
         out_specs=[hbm, pl.BlockSpec((3, width), lambda j: (0, 0))],
@@ -564,7 +565,9 @@
             pltpu.VMEM((rows, width), bf16),
             pltpu.VMEM((tiles, rows, LANES), f32),
             pltpu.VMEM((rows, LANES), f32),
+            pltpu.VMEM((nb, 2, WIDE, half), bf16),
             pltpu.SemaphoreType.DMA((4,)),
+            pltpu.SemaphoreType.DMA((nb, 2)),
         ],
         compiler_params=params(),
         name="first_back",
@@ -608,7 +611,7 @@
             norm_back(steps, seqs, arg_grads, proj, sums, gains, totals, count, low_out, columns if centred else None)
             if not centred:
                 columns[...] = jnp.zeros_like(columns)
-            low[:, pl.ds(pl.multiple_of(j * BLOCK, BLOCK), BLOCK)] = low_out[...]
+            low[:, pl.ds(pl.multiple_of(j * WIDE, WIDE), WIDE)] = low_out[...]
     else:
         low, left, right = refs
     half = low.shape[1] // 2
@@ -635,7 +638,7 @@
     width = grads[0].shape[1] if made else grads[0].shape[0] * LANES
     half = width // 2
     nb = half // WIDE
-    norm_steps = 0 if made else width // BLOCK
+    norm_steps = 0 if made else width // WIDE
     specs, start = [], norm_steps
     for _, first, blocks in xs:
         specs.append(
@@ -651,8 +654,8 @@
     if made:
         specs.append(whole((rows, width)))
     else:
-        tile_spec = pl.BlockSpec((BLOCK // LANES, rows, LANES), lambda j: (held(j, 0, norm_steps), 0, 0))
-        lanes = lambda tall: pl.BlockSpec((tall, BLOCK), lambda j: (0, held(j, 0, norm_steps)))
+        tile_spec = pl.BlockSpec((WIDE // LANES, rows, LANES), lambda j: (held(j, 0, norm_steps), 0, 0))
+        lanes = lambda tall: pl.BlockSpec((tall, WIDE), lambda j: (0, held(j, 0, norm_steps)))
         specs += [tile_spec, tile_spec, lanes(2), lanes(3), lanes(3)]
         out_specs = [lanes(rows), lanes(1)] + out_specs
         out_shape = [jax.ShapeDtypeStruct((rows, width), bf16), jax.ShapeDtypeStruct((1, width), f32)] + out_shape
@@ -680,6 +683,24 @@
         else:
             pairs.append([(x, k) for k in range(x.shape[0] // WIDE)])
     return list(zip(*pairs))
+
+
+def fetch_blocks(blocks, arrays, held_blocks, sems):
+    copies = []
+    for k, pair in enumerate(blocks):
+        for side, (_, at) in enumerate(pair):
+            place = arrays[2 * k + side].at[pl.ds(at * WIDE, WIDE)]
+            copies.append(pltpu.make_async_copy(place, held_blocks.at[k, side], sems.at[k, side]))
+    return copies
+
+
+def block_product(low, held_blocks, sems, k):
+    half = low.shape[1] // 2
+    for side in range(2):
+        place = held_blocks.at[k, side]
+        pltpu.make_async_copy(place, place, sems.at[k, side]).wait()
+    acc = dot(low[:, :half], held_blocks[k, 0], ((1,), (1,)))
+    return acc + dot(low[:, half:], held_blocks[k, 1], ((1,), (1,)))
 
 
 def pull_kernel(nb, tiled, low, *refs):

time: 467 us -> 462 us (0.989)
  Pallas kernels: 219 us -> 214 us
  transfers between devices with their start and end apart: 72 -> 72, of which waited for: 41 -> 40; matrix products, arithmetic and copies ran while one was open for 3% -> 3% of each run, Pallas kernels for 36% -> 36%
where the time goes in v2:
time: 462 us; the launch traced here: 453 us
  Pallas kernels  214 us (46%)
  waiting for transfers between devices  116 us (25%)
  starting transfers between devices  77.3 us (17%)
  local copies, waits for them, and re-layouts  30.1 us (7%)
  other arithmetic  13.7 us (3%)
    ppermute x40, waiting for transfers between devices, across(): return lax.ppermute(value, 'dp', [(i, i ^ bit) for i in range(size)])  89.5 us
    ppermute x40, starting transfers between devices, across(): return lax.ppermute(value, 'dp', [(i, i ^ bit) for i in range(size)])  51.6 us
    pallas_call x4, Pallas kernels, weight_grad(): pl.pallas_call(without(kernel, len(specs), len(deps), -1 - len(scratch)),...  47.5 us
    pallas_call x4, Pallas kernels, project(): pl.pallas_call(without(kernel, len(operands), len(deps)), grid=(len(ws) *...  30 us
    ppermute x32, waiting for transfers between devices, over(): return lax.ppermute(value, axis, [(0, 1), (1, 0)])  26.9 us
    ppermute x32, starting transfers between devices, over(): return lax.ppermute(value, axis, [(0, 1), (1, 0)])  25.7 us
    unnamed x119, local copies, waits for them, and re-layouts  22.3 us
    pallas_call x1, Pallas kernels, second_layer(): pl.pallas_call(functools.partial(second_layer_kernel, steps, seqs, count)...  21.3 us
  transfers between devices with their start and end apart: 72, of which 40 were waited for; matrix products, arithmetic and copies ran while one was open for 3% of the time, Pallas kernels for 36%

profile of v2, /device:TPU:0, one launch (start us, length us, event | category | flops | bytes accessed | tf_op | source)
XLA Modules:
  0.0 453.4 jit_solution(3656924157154072812)
XLA Ops:
  1.3 2.5 cut.1
  6.2 2.6 collective-permute-start
  9.5 4.7 %prep.2 = (bf16[912,1024]{1,0:T(8,128)(2,1)}, bf16[912,512]{1,0:T(8,128)(2,1)}) custom-call(s32[2]{0:T(128)} %pad_add_fusion.1.refs_0_, bf16[150,24,1000]{2,1,0:T(8,128)(2,1)} %refs_1_.3, bf16[128,1024]{1,0:T(8,128)(2,1)} %get-tuple-element.173.refs_2_, bf16[128,1024]{1,0:T(8,128)(2,1)} %get-tuple-element.168.refs_3_), custom_call_target="tpu_custom_call" | custom-call | tf_op jit(solution)/shard_map/prep/pallas_call | solution.py:81
  14.2 4.8 %prep.3 = (bf16[912,1024]{1,0:T(8,128)(2,1)}, bf16[912,512]{1,0:T(8,128)(2,1)}) custom-call(s32[2]{0:T(128)} %pad_add_fusion.1.refs_0_, bf16[150,24,1000]{2,1,0:T(8,128)(2,1)} %refs_1_.3, bf16[912,1024]{1,0:T(8,128)(2,1)} %get-tuple-element.169.refs_2_), custom_call_target="tpu_custom_call", output_to_operand_aliasing={{0}: (2, {})} | custom-call | tf_op jit(solution)/shard_map/prep/pallas_call | solution.py:81
  25.2 2.6 collective-permute-start.3
  27.8 8.9 %project.4 = (f32[16,912,128]{2,1,0:T(8,128)}, f32[2,2048]{1,0:T(2,128)}) custom-call(bf16[912,1024]{1,0:T(8,128)(2,1)} %get-tuple-element.170.refs_0_.refs_1_, bf16[1024,1024]{1,0:T(8,128)(2,1)} %copy-done.33, bf16[1024,1024]{1,0:T(8,128)(2,1)} %collective-permute-done.4.refs_2_.refs_4_), custom_call_target="tpu_custom_call" | custom-call | tf_op jit(solution)/shard_map/project/pallas_call | solution.py:252
  42.9 5.6 %prep_grads.1 = (bf16[912,1024]{1,0:T(8,128)(2,1)}, bf16[912,256]{1,0:T(8,128)(2,1)}, bf16[912,768]{1,0:T(8,128)(2,1)}, f32[8,128]{1,0:T(8,128)}) custom-call(s32[2]{0:T(128)} %pad_add_fusion.refs_0_, bf16[12,150,1000]{2,1,0:T(8,128)(2,1)} %bitcast.87, bf16[12,150,1000]{2,1,0:T(8,128)(2,1)} %bitcast.88), custom_call_target="tpu_custom_call" | custom-call | tf_op jit(solution)/shard_map/prep_grads/pallas_call | solution.py:121
  48.5 2.9 collective-permute-done.7.refs_2_
  52.9 3.0 collective-permute-start.10
  55.9 12.9 %collective-permute-done.10.refs_2_ = bf16[128,1024]{1,0:T(8,128)(2,1)S(1)} collective-permute-done((bf16[128,1024]{1,0:T(8,128)(2,1)S(1)}, bf16[128,1024]{1,0:T(8,128)(2,1)S(1)}, u32[]{:S(2)}, u32[]{:S(2)}) %collective-permute-start.10) | collective-permute-done | bytes 262176 | tf_op jit(solution)/shard_map/ppermute | solution.py:844
  75.9 6.2 %project.5 = (f32[16,912,128]{2,1,0:T(8,128)}, f32[2,1024]{1,0:T(2,128)}) custom-call(bf16[912,512]{1,0:T(8,128)(2,1)} %copy-done.37, bf16[912,512]{1,0:T(8,128)(2,1)} %copy-done.38, bf16[512,1024]{1,0:T(8,128)(2,1)} %copy-done.6, bf16[512,1024]{1,0:T(8,128)(2,1)} %copy-done.7, ...), custom_call_target="tpu_custom_call", output_to_operand_aliasing={{0}: (4, {})} | custom-call | tf_op jit(solution)/shard_map/project/pallas_call | solution.py:252
  82.8 2.6 collective-permute-done.14.refs_5_.far_hbm0
  86.6 6.4 %project.6 = (f32[16,912,128]{2,1,0:T(8,128)}, f32[2,1024]{1,0:T(2,128)}) custom-call(bf16[912,512]{1,0:T(8,128)(2,1)} %copy-done.37, bf16[912,512]{1,0:T(8,128)(2,1)} %copy-done.38, bf16[512,1024]{1,0:T(8,128)(2,1)} %copy-done.41, bf16[512,1024]{1,0:T(8,128)(2,1)} %collective-permute-done.13.refs_3_.refs_4_, ...), custom_call_target="tpu_custom_call", output_to_operand_aliasing={{0}: (4, {})} | custom-call | tf_op jit(solution)/shard_map/project/pallas_call | solution.py:252
  112.2 20.0 %first_layer.1 = (bf16[912,2048]{1,0:T(8,128)(2,1)}, f32[16,912,128]{2,1,0:T(8,128)}, f32[1,2048]{1,0:T(1,128)}, f32[16,912,128]{2,1,0:T(8,128)}, f32[2,1024]{1,0:T(2,128)}) custom-call(f32[16,912,128]{2,1,0:T(8,128)} %get-tuple-element.200.proj_hbm.refs_11_.refs_3_, f32[2,2048]{1,0:T(2,128)} %add.146.sums.refs_12_.refs_4_, ...), custom_call_target="tpu_custom_call" | custom-call | tf_op jit(solution)/shard_map/first_layer/pallas_call | solution.py:423
  135.4 2.9 collective-permute-done.26.refs_7_.far_hbm1
  140.1 8.4 %project.7 = (f32[16,912,128]{2,1,0:T(8,128)}, f32[2,1024]{1,0:T(2,128)}) custom-call(bf16[912,2048]{1,0:T(8,128)(2,1)} %get-tuple-element.209.refs_0_.refs_1_.refs_2_.refs_10_, bf16[912,2048]{1,0:T(8,128)(2,1)} %get-tuple-element.209.refs_0_.refs_1_.refs_2_.refs_10_, ...), custom_call_target="tpu_custom_call", output_to_operand_aliasing={{0}: (6, {})} | custom-call | tf_op jit(solution)/shard_map/project/pallas_call | solution.py:252
  152.4 2.8 collective-permute-done.28
  161.4 2.8 collective-permute-done.30
  165.8 2.6 collective-permute-done.31
  169.6 21.3 %second_layer.1 = (bf16[912,1024]{1,0:T(8,128)(2,1)}, bf16[912,512]{1,0:T(8,128)(2,1)}, bf16[912,512]{1,0:T(8,128)(2,1)}, f32[16,912,128]{2,1,0:T(8,128)}, f32[3,2048]{1,0:T(4,128)}) custom-call(f32[16,912,128]{2,1,0:T(8,128)} %get-tuple-element.215.proj_hbm.refs_3_, f32[2,2048]{1,0:T(2,128)} %slice.233.sums.refs_4_, ...), custom_call_target="tpu_custom_call" | custom-call | tf_op jit(solution)/shard_map/second_layer/pallas_call | solution.py:487
  194.8 2.4 collective-permute-done.33
  198.4 2.8 collective-permute-done.35
  210.7 15.4 %weight_grad.4 = (bf16[912,2048]{1,0:T(8,128)(2,1)}, f32[1,2048]{1,0:T(1,128)}, bf16[1024,1024]{1,0:T(8,128)(2,1)}, bf16[1024,1024]{1,0:T(8,128)(2,1)}, f32[8,128]{1,0:T(8,128)}) custom-call(bf16[912,2048]{1,0:T(8,128)(2,1)} %get-tuple-element.209.refs_0_.refs_1_.refs_2_.refs_10_, f32[1,2048]{1,0:T(1,128)} %fusion.2.refs_1_, ...), custom_call_target="tpu_custom_call" | custom-call | tf_op jit(solution)/shard_map/weight_grad/pallas_call | solution.py:666
  228.2 8.4 %weight_grad.5 = (bf16[1024,1024]{1,0:T(8,128)(2,1)}, bf16[1024,1024]{1,0:T(8,128)(2,1)}, f32[8,128]{1,0:T(8,128)}) custom-call(bf16[912,2048]{1,0:T(8,128)(2,1)} %get-tuple-element.209.refs_0_.refs_1_.refs_2_.refs_10_, f32[1,2048]{1,0:T(1,128)} %fusion.2.refs_1_, bf16[912,2048]{1,0:T(8,128)(2,1)} %get-tuple-element.225.refs_2_.refs_0_), custom_call_target="tpu_custom_call" | custom-call | tf_op jit(solution)/shard_map/weight_grad/pallas_call | solution.py:666
  238.0 2.5 total.7
  241.8 3.6 fold.10
  247.0 3.4 collective-permute-done.34.refs_15_.refs_5_
  251.4 20.8 %first_back.1 = (f32[16,912,128]{2,1,0:T(8,128)}, f32[3,2048]{1,0:T(4,128)}) custom-call(bf16[912,2048]{1,0:T(8,128)(2,1)} %get-tuple-element.225.refs_2_.refs_0_, bf16[1024,1024]{1,0:T(8,128)(2,1)} %pad.14.top_hbm.refs_1_.refs_3_, bf16[1024,1024]{1,0:T(8,128)(2,1)} %copy-done, bf16[1024,1024]{1,0:T(8,128)(2,1)} %pad.14.top_hbm.refs_1_.refs_3_, ...), custom_call_target="tpu_custom_call" | custom-call | tf_op jit(solution)/shard_map/first_back/pallas_call | solution.py:553
  275.9 2.4 collective-permute-done.43
  282.4 2.9 fold.11
  292.4 2.9 collective-permute-done.46
  302.4 15.3 %weight_grad.6 = (bf16[912,2048]{1,0:T(8,128)(2,1)}, f32[1,2048]{1,0:T(1,128)}, bf16[1024,1024]{1,0:T(8,128)(2,1)}, bf16[1024,1024]{1,0:T(8,128)(2,1)}, f32[8,128]{1,0:T(8,128)}) custom-call(bf16[912,512]{1,0:T(8,128)(2,1)} %copy-done.37, bf16[912,512]{1,0:T(8,128)(2,1)} %copy-done.38, f32[16,912,128]{2,1,0:T(8,128)} %get-tuple-element.256.refs_2_, ...), custom_call_target="tpu_custom_call" | custom-call | tf_op jit(solution)/shard_map/weight_grad/pallas_call | solution.py:666
  320.2 8.4 %weight_grad.7 = (bf16[1024,1024]{1,0:T(8,128)(2,1)}, bf16[1024,1024]{1,0:T(8,128)(2,1)}, f32[8,128]{1,0:T(8,128)}) custom-call(bf16[912,1024]{1,0:T(8,128)(2,1)} %get-tuple-element.170.refs_0_.refs_1_, bf16[912,2048]{1,0:T(8,128)(2,1)} %get-tuple-element.262.refs_1_.refs_0_, f32[8,128]{1,0:T(8,128)} %copy-done.31), custom_call_target="tpu_custom_call" | custom-call | tf_op jit(solution)/shard_map/weight_grad/pallas_call | solution.py:666
  329.2 2.5 total.9
  334.5 3.5 fold.14
  341.2 8.8 %pull.2 = (bf16[912,1024]{1,0:T(8,128)(2,1)}, f32[8,128]{1,0:T(8,128)}) custom-call(bf16[912,2048]{1,0:T(8,128)(2,1)} %get-tuple-element.262.refs_1_.refs_0_, bf16[512,1024]{1,0:T(8,128)(2,1)} %copy-done.6, bf16[512,1024]{1,0:T(8,128)(2,1)} %copy-done.41, bf16[512,1024]{1,0:T(8,128)(2,1)} %copy-done.7, ...), custom_call_target="tpu_custom_call" | custom-call | tf_op jit(solution)/shard_map/pull/pallas_call | solution.py:729
  350.0 5.3 %collective-permute-done.51.refs_1_.refs_3_ = bf16[2,64,1024]{2,1,0:T(8,128)(2,1)S(1)} collective-permute-done((bf16[2,64,1024]{2,1,0:T(8,128)(2,1)}, bf16[2,64,1024]{2,1,0:T(8,128)(2,1)S(1)}, u32[]{:S(2)}, u32[]{:S(2)}) %collective-permute-start.51) | collective-permute-done | bytes 262176 | tf_op jit(solution)/shard_map/ppermute | solution.py:844
  359.1 4.5 combine.2
  366.0 2.9 fold.15
  373.3 9.0 %pull.3 = (f32[912,1024]{1,0:T(8,128)}, f32[8,128]{1,0:T(8,128)}) custom-call(bf16[912,2048]{1,0:T(8,128)(2,1)} %get-tuple-element.262.refs_1_.refs_0_, bf16[1024,1024]{1,0:T(8,128)(2,1)} %copy-done.33, bf16[1024,1024]{1,0:T(8,128)(2,1)} %collective-permute-done.4.refs_2_.refs_4_, bf16[1024,1024]{1,0:T(8,128)(2,1)} %copy-done.33, ...), custom_call_target="tpu_custom_call" | custom-call | tf_op jit(solution)/shard_map/pull/pallas_call | solution.py:729
  390.5 8.6 %collective-permute-done.61.refs_2_.refs_4_ = bf16[1,128,1024]{2,1,0:T(8,128)(2,1)S(1)} collective-permute-done((bf16[1,128,1024]{2,1,0:T(8,128)(2,1)S(1)}, bf16[1,128,1024]{2,1,0:T(8,128)(2,1)S(1)}, u32[]{:S(2)}, u32[]{:S(2)}) %collective-permute-start.61) | collective-permute-done | bytes 262176 | tf_op jit(solution)/shard_map/ppermute | solution.py:844
  404.1 7.9 %collective-permute-done.65.refs_1_ = bf16[1,64,1024]{2,1,0:T(8,128)(2,1)S(1)} collective-permute-done((bf16[1,64,1024]{2,1,0:T(8,128)(2,1)S(1)}, bf16[1,64,1024]{2,1,0:T(8,128)(2,1)S(1)}, u32[]{:S(2)}, u32[]{:S(2)}) %collective-permute-start.65) | collective-permute-done | bytes 131104 | tf_op jit(solution)/shard_map/ppermute | solution.py:844
  415.5 6.5 %collective-permute-done.67.refs_2_ = bf16[64,1024]{1,0:T(8,128)(2,1)S(1)} collective-permute-done((bf16[64,1024]{1,0:T(8,128)(2,1)S(1)}, bf16[64,1024]{1,0:T(8,128)(2,1)S(1)}, u32[]{:S(2)}, u32[]{:S(2)}) %collective-permute-start.67) | collective-permute-done | bytes 131104 | tf_op jit(solution)/shard_map/ppermute | solution.py:844
  425.8 4.6 %collective-permute-done.69.refs_2_ = bf16[128,1024]{1,0:T(8,128)(2,1)S(1)} collective-permute-done((bf16[128,1024]{1,0:T(8,128)(2,1)S(1)}, bf16[128,1024]{1,0:T(8,128)(2,1)S(1)}, u32[]{:S(2)}, u32[]{:S(2)}) %collective-permute-start.69) | collective-permute-done | bytes 262176 | tf_op jit(solution)/shard_map/ppermute | solution.py:844
  435.6 2.6 multiply_add_fusion
  439.8 4.5 combine.3
  444.4 5.5 %collective-permute-done.70.refs_2_ = bf16[256,1024]{1,0:T(8,128)(2,1)S(1)} collective-permute-done((bf16[256,1024]{1,0:T(8,128)(2,1)S(1)}, bf16[256,1024]{1,0:T(8,128)(2,1)S(1)}, u32[]{:S(2)}, u32[]{:S(2)}) %collective-permute-start.70) | collective-permute-done | bytes 524320 | tf_op jit(solution)/shard_map/ppermute | solution.py:844
  450.6 2.4 fusion
  (324 shorter events, 154.8 us)
Async XLA Ops:
  5.7 22.1 %collective-permute-start.4 = (bf16[1024,1024]{1,0:T(8,128)(2,1)S(1)}, bf16[1024,1024]{1,0:T(8,128)(2,1)}, u32[]{:S(2)}, u32[]{:S(2)}) collective-permute-start(bf16[1024,1024]{1,0:T(8,128)(2,1)S(1)} %pad.15.refs_1_.refs_3_), channel_id=1, source_target_pairs={{0,1},{1,0},{2,3},{3,2},{4,5},{5,4},{6,7},{7,6},{8,9},{9,8},{10,11... | collective-permute-start | bytes 6291464 | tf_op jit(solution)/shard_map/ppermute | solution.py:839
  6.2 12.8 %collective-permute-start = (bf16[128,1024]{1,0:T(8,128)(2,1)S(1)}, bf16[128,1024]{1,0:T(8,128)(2,1)S(1)}, u32[]{:S(2)}, u32[]{:S(2)}) collective-permute-start(bf16[128,1024]{1,0:T(8,128)(2,1)S(1)} %copy-done.47), channel_id=1, source_target_pairs={{0,2},{2,0},{1,3},{3,1},{4,6},{6,4},{5,7},{7,5},{8,10},{10,8},{9,1... | collective-permute-start | bytes 786440 | tf_op jit(solution)/shard_map/ppermute | solution.py:839
  8.8 12.5 %collective-permute-start.1 = (bf16[128,1024]{1,0:T(8,128)(2,1)S(1)}, bf16[128,1024]{1,0:T(8,128)(2,1)S(1)}, u32[]{:S(2)}, u32[]{:S(2)}) collective-permute-start(bf16[128,1024]{1,0:T(8,128)(2,1)S(1)} %copy-done.46), channel_id=1, source_target_pairs={{0,2},{2,0},{1,3},{3,1},{4,6},{6,4},{5,7},{7,5},{8,10},{10,8},{9,1... | collective-permute-start | bytes 786440 | tf_op jit(solution)/shard_map/ppermute | solution.py:839
  21.3 31.0 %collective-permute-start.2 = (bf16[912,512]{1,0:T(8,128)(2,1)S(1)}, bf16[912,512]{1,0:T(8,128)(2,1)S(1)}, u32[]{:S(2)}, u32[]{:S(2)}) collective-permute-start(bf16[912,512]{1,0:T(8,128)(2,1)S(1)} %copy-done.15), channel_id=1, source_target_pairs={{0,2},{2,0},{1,3},{3,1},{4,6},{6,4},{5,7},{7,5},{8,10},{10,8},{9,1... | collective-permute-start | bytes 2801672 | tf_op jit(solution)/shard_map/ppermute | solution.py:839
  23.1 48.7 %collective-permute-start.8 = (bf16[912,512]{1,0:T(8,128)(2,1)}, bf16[912,512]{1,0:T(8,128)(2,1)S(1)}, u32[]{:S(2)}, u32[]{:S(2)}) collective-permute-start(bf16[912,512]{1,0:T(8,128)(2,1)} %get-tuple-element.185.refs_4_), channel_id=1, source_target_pairs={{0,2},{2,0},{1,3},{3,1},{4,6},{6,4},{5,7},{7,5},{8,10},{10,8},{9,1... | collective-permute-start | bytes 2801672 | tf_op jit(solution)/shard_map/ppermute | solution.py:839
  23.4 13.4 %collective-permute-start.6 = (bf16[64,1024]{1,0:T(8,128)(2,1)S(1)}, bf16[64,1024]{1,0:T(8,128)(2,1)S(1)}, u32[]{:S(2)}, u32[]{:S(2)}) collective-permute-start(bf16[64,1024]{1,0:T(8,128)(2,1)S(1)} %get-tuple-element.326.refs_1_), channel_id=1, source_target_pairs={{0,4},{4,0},{8,12},{12,8},{16,20},{20,16},{24,28},{28,24},{1,5},{5... | collective-permute-start | bytes 393224 | tf_op jit(solution)/shard_map/ppermute | solution.py:844
  25.2 13.3 %collective-permute-start.3 = (bf16[64,1024]{1,0:T(8,128)(2,1)S(1)}, bf16[64,1024]{1,0:T(8,128)(2,1)S(1)}, u32[]{:S(2)}, u32[]{:S(2)}) collective-permute-start(bf16[64,1024]{1,0:T(8,128)(2,1)S(1)} %get-tuple-element.327.refs_1_), channel_id=1, source_target_pairs={{0,16},{4,20},{8,24},{12,28},{16,0},{20,4},{24,8},{28,12},{1,17},{... | collective-permute-start | bytes 393224 | tf_op jit(solution)/shard_map/ppermute | solution.py:844
  38.1 13.3 %collective-permute-start.7 = (bf16[128,1024]{1,0:T(8,128)(2,1)S(1)}, bf16[128,1024]{1,0:T(8,128)(2,1)S(1)}, u32[]{:S(2)}, u32[]{:S(2)}) collective-permute-start(bf16[128,1024]{1,0:T(8,128)(2,1)S(1)} %get-tuple-element.182.refs_1_), channel_id=1, source_target_pairs={{0,16},{4,20},{8,24},{12,28},{16,0},{20,4},{24,8},{28,12},{1,17},{... | collective-permute-start | bytes 786440 | tf_op jit(solution)/shard_map/ppermute | solution.py:844
  39.1 13.0 %collective-permute-start.5 = (bf16[128,1024]{1,0:T(8,128)(2,1)S(1)}, bf16[128,1024]{1,0:T(8,128)(2,1)S(1)}, u32[]{:S(2)}, u32[]{:S(2)}) collective-permute-start(bf16[128,1024]{1,0:T(8,128)(2,1)S(1)} %get-tuple-element.179.refs_1_), channel_id=1, source_target_pairs={{0,8},{4,12},{8,0},{12,4},{16,24},{20,28},{24,16},{28,20},{1,9},{5... | collective-permute-start | bytes 786440 | tf_op jit(solution)/shard_map/ppermute | solution.py:844
  52.3 16.7 %collective-permute-start.9 = (bf16[256,1024]{1,0:T(8,128)(2,1)S(1)}, bf16[256,1024]{1,0:T(8,128)(2,1)S(1)}, u32[]{:S(2)}, u32[]{:S(2)}) collective-permute-start(bf16[256,1024]{1,0:T(8,128)(2,1)S(1)} %get-tuple-element.186.refs_1_), channel_id=1, source_target_pairs={{0,4},{4,0},{8,12},{12,8},{16,20},{20,16},{24,28},{28,24},{1,5},{5... | collective-permute-start | bytes 1572872 | tf_op jit(solution)/shard_map/ppermute | solution.py:844
  52.9 18.2 %collective-permute-start.11 = (bf16[256,1024]{1,0:T(8,128)(2,1)S(1)}, bf16[256,1024]{1,0:T(8,128)(2,1)S(1)}, u32[]{:S(2)}, u32[]{:S(2)}) collective-permute-start(bf16[256,1024]{1,0:T(8,128)(2,1)S(1)} %get-tuple-element.192.refs_1_), channel_id=1, source_target_pairs={{0,8},{4,12},{8,0},{12,4},{16,24},{20,28},{24,16},{28,20},{1,9},{5... | collective-permute-start | bytes 1572872 | tf_op jit(solution)/shard_map/ppermute | solution.py:844
  52.9 15.9 %collective-permute-start.10 = (bf16[128,1024]{1,0:T(8,128)(2,1)S(1)}, bf16[128,1024]{1,0:T(8,128)(2,1)S(1)}, u32[]{:S(2)}, u32[]{:S(2)}) collective-permute-start(bf16[128,1024]{1,0:T(8,128)(2,1)S(1)} %collective-permute-done.1.refs_1_), channel_id=1, source_target_pairs={{0,16},{4,20},{8,24},{12,28},{16,0},{20,4},{24,8},{28,12},{1,17},{... | collective-permute-start | bytes 786440 | tf_op jit(solution)/shard_map/ppermute | solution.py:844
  71.8 13.6 %collective-permute-start.12 = (bf16[512,1024]{1,0:T(8,128)(2,1)S(1)}, bf16[512,1024]{1,0:T(8,128)(2,1)S(1)}, u32[]{:S(2)}, u32[]{:S(2)}) collective-permute-start(bf16[512,1024]{1,0:T(8,128)(2,1)S(1)} %get-tuple-element.195.refs_2_.refs_1_), channel_id=1, source_target_pairs={{0,1},{1,0},{2,3},{3,2},{4,5},{5,4},{6,7},{7,6},{8,9},{9,8},{10,11... | collective-permute-start | bytes 3145736 | tf_op jit(solution)/shard_map/ppermute | solution.py:839
  71.8 13.6 %collective-permute-start.13 = (bf16[512,1024]{1,0:T(8,128)(2,1)S(1)}, bf16[512,1024]{1,0:T(8,128)(2,1)}, u32[]{:S(2)}, u32[]{:S(2)}) collective-permute-start(bf16[512,1024]{1,0:T(8,128)(2,1)S(1)} %get-tuple-element.196.refs_3_), channel_id=1, source_target_pairs={{0,1},{1,0},{2,3},{3,2},{4,5},{5,4},{6,7},{7,6},{8,9},{9,8},{10,11... | collective-permute-start | bytes 3145736 | tf_op jit(solution)/shard_map/ppermute | solution.py:839
  72.3 39.9 %collective-permute-start.22 = (bf16[1024,1024]{1,0:T(8,128)(2,1)}, bf16[1024,1024]{1,0:T(8,128)(2,1)}, u32[]{:S(2)}, u32[]{:S(2)}) collective-permute-start(bf16[1024,1024]{1,0:T(8,128)(2,1)} %pad.14.top_hbm.refs_1_.refs_3_), channel_id=1, source_target_pairs={{0,1},{1,0},{2,3},{3,2},{4,5},{5,4},{6,7},{7,6},{8,9},{9,8},{10,11... | collective-permute-start | bytes 6291464 | tf_op jit(solution)/shard_map/ppermute | solution.py:839
  72.4 13.0 %collective-permute-start.14 = (bf16[912,256]{1,0:T(8,128)(2,1)S(1)}, bf16[912,256]{1,0:T(8,128)(2,1)S(1)}, u32[]{:S(2)}, u32[]{:S(2)}) collective-permute-start(bf16[912,256]{1,0:T(8,128)(2,1)S(1)} %copy-done.18), channel_id=1, source_target_pairs={{0,2},{2,0},{1,3},{3,1},{4,6},{6,4},{5,7},{7,5},{8,10},{10,8},{9,1... | collective-permute-start | bytes 1400840 | tf_op jit(solution)/shard_map/ppermute | solution.py:839
  73.8 25.2 %collective-permute-start.17 = (bf16[256,1024]{1,0:T(8,128)(2,1)S(1)}, bf16[256,1024]{1,0:T(8,128)(2,1)S(1)}, u32[]{:S(2)}, u32[]{:S(2)}) collective-permute-start(bf16[256,1024]{1,0:T(8,128)(2,1)S(1)} %get-tuple-element.205.refs_1_), channel_id=1, source_target_pairs={{0,8},{4,12},{8,0},{12,4},{16,24},{20,28},{24,16},{28,20},{1,9},{5... | collective-permute-start | bytes 1572872 | tf_op jit(solution)/shard_map/ppermute | solution.py:844
  101.4 30.8 %collective-permute-start.23 = (bf16[512,1024]{1,0:T(8,128)(2,1)S(1)}, bf16[512,1024]{1,0:T(8,128)(2,1)S(1)}, u32[]{:S(2)}, u32[]{:S(2)}) collective-permute-start(bf16[512,1024]{1,0:T(8,128)(2,1)S(1)} %get-tuple-element.210.refs_1_), channel_id=1, source_target_pairs={{0,4},{4,0},{8,12},{12,8},{16,20},{20,16},{24,28},{28,24},{1,5},{5... | collective-permute-start | bytes 3145736 | tf_op jit(solution)/shard_map/ppermute | solution.py:844
  105.2 33.1 %collective-permute-start.26 = (bf16[912,768]{1,0:T(8,128)(2,1)S(1)}, bf16[912,768]{1,0:T(8,128)(2,1)S(1)}, u32[]{:S(2)}, u32[]{:S(2)}) collective-permute-start(bf16[912,768]{1,0:T(8,128)(2,1)S(1)} %copy-done.13), channel_id=1, source_target_pairs={{0,2},{2,0},{1,3},{3,1},{4,6},{6,4},{5,7},{7,5},{8,10},{10,8},{9,1... | collective-permute-start | bytes 4202504 | tf_op jit(solution)/shard_map/ppermute | solution.py:839
  226.1 10.5 %collective-permute-start.39 = (bf16[1024,1024]{1,0:T(8,128)(2,1)}, bf16[1024,1024]{1,0:T(8,128)(2,1)S(1)}, u32[]{:S(2)}, u32[]{:S(2)}) collective-permute-start(bf16[1024,1024]{1,0:T(8,128)(2,1)} %get-tuple-element.230), channel_id=1, source_target_pairs={{0,1},{1,0},{2,3},{3,2},{4,5},{5,4},{6,7},{7,6},{8,9},{9,8},{10,11... | collective-permute-start | bytes 6291464 | tf_op jit(solution)/shard_map/ppermute | solution.py:839
  226.2 14.3 %collective-permute-start.38 = (bf16[1024,1024]{1,0:T(8,128)(2,1)}, bf16[1024,1024]{1,0:T(8,128)(2,1)S(1)}, u32[]{:S(2)}, u32[]{:S(2)}) collective-permute-start(bf16[1024,1024]{1,0:T(8,128)(2,1)} %get-tuple-element.228), channel_id=1, source_target_pairs={{0,1},{1,0},{2,3},{3,2},{4,5},{5,4},{6,7},{7,6},{8,9},{9,8},{10,11... | collective-permute-start | bytes 6291464 | tf_op jit(solution)/shard_map/ppermute | solution.py:839
  226.7 23.8 %collective-permute-start.34 = (bf16[912,512]{1,0:T(8,128)(2,1)}, bf16[912,512]{1,0:T(8,128)(2,1)S(1)}, u32[]{:S(2)}, u32[]{:S(2)}) collective-permute-start(bf16[912,512]{1,0:T(8,128)(2,1)} %get-tuple-element.222), channel_id=1, source_target_pairs={{0,2},{2,0},{1,3},{3,1},{4,6},{6,4},{5,7},{7,5},{8,10},{10,8},{9,1... | collective-permute-start | bytes 2801672 | tf_op jit(solution)/shard_map/ppermute | solution.py:839
  245.4 27.5 %collective-permute-start.40 = (bf16[2,256,1024]{2,1,0:T(8,128)(2,1)}, bf16[2,256,1024]{2,1,0:T(8,128)(2,1)S(1)}, u32[]{:S(2)}, u32[]{:S(2)}) collective-permute-start(bf16[2,256,1024]{2,1,0:T(8,128)(2,1)} %get-tuple-element.236), channel_id=1, source_target_pairs={{0,4},{4,0},{8,12},{12,8},{16,20},{20,16},{24,28},{28,24},{1,5},{5... | collective-permute-start | bytes 3145736 | tf_op jit(solution)/shard_map/ppermute | solution.py:844
  246.5 26.4 %collective-permute-start.41 = (bf16[512,1024]{1,0:T(8,128)(2,1)S(1)}, bf16[512,1024]{1,0:T(8,128)(2,1)S(1)}, u32[]{:S(2)}, u32[]{:S(2)}) collective-permute-start(bf16[512,1024]{1,0:T(8,128)(2,1)S(1)} %bitcast.111), channel_id=1, source_target_pairs={{0,2},{2,0},{1,3},{3,1},{4,6},{6,4},{5,7},{7,5},{8,10},{10,8},{9,1... | collective-permute-start | bytes 3145736 | tf_op jit(solution)/shard_map/ppermute | solution.py:839
  279.9 17.5 %collective-permute-start.49 = (bf16[256,1024]{1,0:T(8,128)(2,1)S(1)}, bf16[256,1024]{1,0:T(8,128)(2,1)S(1)}, u32[]{:S(2)}, u32[]{:S(2)}) collective-permute-start(bf16[256,1024]{1,0:T(8,128)(2,1)S(1)} %bitcast.60), channel_id=1, source_target_pairs={{0,2},{2,0},{1,3},{3,1},{4,6},{6,4},{5,7},{7,5},{8,10},{10,8},{9,1... | collective-permute-start | bytes 1572872 | tf_op jit(solution)/shard_map/ppermute | solution.py:839
  285.3 12.1 %collective-permute-start.48 = (bf16[1,256,1024]{2,1,0:T(8,128)(2,1)}, bf16[1,256,1024]{2,1,0:T(8,128)(2,1)S(1)}, u32[]{:S(2)}, u32[]{:S(2)}) collective-permute-start(bf16[1,256,1024]{2,1,0:T(8,128)(2,1)} %get-tuple-element.251), channel_id=1, source_target_pairs={{0,4},{4,0},{8,12},{12,8},{16,20},{20,16},{24,28},{28,24},{1,5},{5... | collective-permute-start | bytes 1572872 | tf_op jit(solution)/shard_map/ppermute | solution.py:844
  295.9 21.8 %collective-permute-start.47 = (bf16[912,512]{1,0:T(8,128)(2,1)}, bf16[912,512]{1,0:T(8,128)(2,1)S(1)}, u32[]{:S(2)}, u32[]{:S(2)}) collective-permute-start(bf16[912,512]{1,0:T(8,128)(2,1)} %get-tuple-element.249), channel_id=1, source_target_pairs={{0,2},{2,0},{1,3},{3,1},{4,6},{6,4},{5,7},{7,5},{8,10},{10,8},{9,1... | collective-permute-start | bytes 2801672 | tf_op jit(solution)/shard_map/ppermute | solution.py:839
  300.3 17.5 %collective-permute-start.50 = (bf16[2,128,1024]{2,1,0:T(8,128)(2,1)S(1)}, bf16[2,128,1024]{2,1,0:T(8,128)(2,1)S(1)}, u32[]{:S(2)}, u32[]{:S(2)}) collective-permute-start(bf16[2,128,1024]{2,1,0:T(8,128)(2,1)S(1)} %get-tuple-element.255), channel_id=1, source_target_pairs={{0,8},{4,12},{8,0},{12,4},{16,24},{20,28},{24,16},{28,20},{1,9},{5... | collective-permute-start | bytes 1572872 | tf_op jit(solution)/shard_map/ppermute | solution.py:844
  317.7 11.5 %collective-permute-start.53 = (bf16[1024,1024]{1,0:T(8,128)(2,1)}, bf16[1024,1024]{1,0:T(8,128)(2,1)}, u32[]{:S(2)}, u32[]{:S(2)}) collective-permute-start(bf16[1024,1024]{1,0:T(8,128)(2,1)} %get-tuple-element.267), channel_id=1, source_target_pairs={{0,1},{1,0},{2,3},{3,2},{4,5},{5,4},{6,7},{7,6},{8,9},{9,8},{10,11... | collective-permute-start | bytes 6291464 | tf_op jit(solution)/shard_map/ppermute | solution.py:839
  338.0 25.7 %collective-permute-start.56 = (bf16[2,256,1024]{2,1,0:T(8,128)(2,1)}, bf16[2,256,1024]{2,1,0:T(8,128)(2,1)S(1)}, u32[]{:S(2)}, u32[]{:S(2)}) collective-permute-start(bf16[2,256,1024]{2,1,0:T(8,128)(2,1)} %get-tuple-element.277), channel_id=1, source_target_pairs={{0,4},{4,0},{8,12},{12,8},{16,20},{20,16},{24,28},{28,24},{1,5},{5... | collective-permute-start | bytes 3145736 | tf_op jit(solution)/shard_map/ppermute | solution.py:844
  339.1 26.9 %collective-permute-start.55 = (bf16[512,1024]{1,0:T(8,128)(2,1)}, bf16[512,1024]{1,0:T(8,128)(2,1)}, u32[]{:S(2)}, u32[]{:S(2)}) collective-permute-start(bf16[512,1024]{1,0:T(8,128)(2,1)} %bitcast.30), channel_id=1, source_target_pairs={{0,2},{2,0},{1,3},{3,1},{4,6},{6,4},{5,7},{7,5},{8,10},{10,8},{9,1... | collective-permute-start | bytes 3145736 | tf_op jit(solution)/shard_map/ppermute | solution.py:839
  340.6 14.7 %collective-permute-start.51 = (bf16[2,64,1024]{2,1,0:T(8,128)(2,1)}, bf16[2,64,1024]{2,1,0:T(8,128)(2,1)S(1)}, u32[]{:S(2)}, u32[]{:S(2)}) collective-permute-start(bf16[2,64,1024]{2,1,0:T(8,128)(2,1)} %get-tuple-element.261), channel_id=1, source_target_pairs={{0,16},{4,20},{8,24},{12,28},{16,0},{20,4},{24,8},{28,12},{1,17},{... | collective-permute-start | bytes 786440 | tf_op jit(solution)/shard_map/ppermute | solution.py:844
  356.7 13.6 %collective-permute-start.54 = (bf16[128,1024]{1,0:T(8,128)(2,1)}, bf16[128,1024]{1,0:T(8,128)(2,1)}, u32[]{:S(2)}, u32[]{:S(2)}) collective-permute-start(bf16[128,1024]{1,0:T(8,128)(2,1)} %bitcast.29.refs_1_), channel_id=1, source_target_pairs={{0,16},{4,20},{8,24},{12,28},{16,0},{20,4},{24,8},{28,12},{1,17},{... | collective-permute-start | bytes 786440 | tf_op jit(solution)/shard_map/ppermute | solution.py:844
  364.6 17.8 %collective-permute-start.57 = (bf16[256,1024]{1,0:T(8,128)(2,1)S(1)}, bf16[256,1024]{1,0:T(8,128)(2,1)S(1)}, u32[]{:S(2)}, u32[]{:S(2)}) collective-permute-start(bf16[256,1024]{1,0:T(8,128)(2,1)S(1)} %bitcast.61), channel_id=1, source_target_pairs={{0,2},{2,0},{1,3},{3,1},{4,6},{6,4},{5,7},{7,5},{8,10},{10,8},{9,1... | collective-permute-start | bytes 1572872 | tf_op jit(solution)/shard_map/ppermute | solution.py:839
  368.8 14.8 %collective-permute-start.59 = (bf16[1,256,1024]{2,1,0:T(8,128)(2,1)}, bf16[1,256,1024]{2,1,0:T(8,128)(2,1)S(1)}, u32[]{:S(2)}, u32[]{:S(2)}) collective-permute-start(bf16[1,256,1024]{2,1,0:T(8,128)(2,1)} %get-tuple-element.289), channel_id=1, source_target_pairs={{0,4},{4,0},{8,12},{12,8},{16,20},{20,16},{24,28},{28,24},{1,5},{5... | collective-permute-start | bytes 1572872 | tf_op jit(solution)/shard_map/ppermute | solution.py:844
  372.8 13.9 %collective-permute-start.62 = (bf16[256,1024]{1,0:T(8,128)(2,1)S(1)}, bf16[256,1024]{1,0:T(8,128)(2,1)S(1)}, u32[]{:S(2)}, u32[]{:S(2)}) collective-permute-start(bf16[256,1024]{1,0:T(8,128)(2,1)S(1)} %get-tuple-element.295.refs_1_), channel_id=1, source_target_pairs={{0,8},{4,12},{8,0},{12,4},{16,24},{20,28},{24,16},{28,20},{1,9},{5... | collective-permute-start | bytes 1572872 | tf_op jit(solution)/shard_map/ppermute | solution.py:844
  386.8 25.4 %collective-permute-start.64 = (bf16[512,1024]{1,0:T(8,128)(2,1)S(1)}, bf16[512,1024]{1,0:T(8,128)(2,1)S(1)}, u32[]{:S(2)}, u32[]{:S(2)}) collective-permute-start(bf16[512,1024]{1,0:T(8,128)(2,1)S(1)} %get-tuple-element.301.refs_1_), channel_id=1, source_target_pairs={{0,4},{4,0},{8,12},{12,8},{16,20},{20,16},{24,28},{28,24},{1,5},{5... | collective-permute-start | bytes 3145736 | tf_op jit(solution)/shard_map/ppermute | solution.py:844
  387.8 50.4 %collective-permute-start.58 = (bf16[912,1024]{1,0:T(8,128)(2,1)S(1)}, bf16[912,1024]{1,0:T(8,128)(2,1)S(1)}, u32[]{:S(2)}, u32[]{:S(2)}) collective-permute-start(bf16[912,1024]{1,0:T(8,128)(2,1)S(1)} %copy-done.57), channel_id=1, source_target_pairs={{0,2},{2,0},{1,3},{3,1},{4,6},{6,4},{5,7},{7,5},{8,10},{10,8},{9,1... | collective-permute-start | bytes 5603336 | tf_op jit(solution)/shard_map/ppermute | solution.py:839
  388.4 10.6 %collective-permute-start.61 = (bf16[1,128,1024]{2,1,0:T(8,128)(2,1)S(1)}, bf16[1,128,1024]{2,1,0:T(8,128)(2,1)S(1)}, u32[]{:S(2)}, u32[]{:S(2)}) collective-permute-start(bf16[1,128,1024]{2,1,0:T(8,128)(2,1)S(1)} %get-tuple-element.294), channel_id=1, source_target_pairs={{0,8},{4,12},{8,0},{12,4},{16,24},{20,28},{24,16},{28,20},{1,9},{5... | collective-permute-start | bytes 786440 | tf_op jit(solution)/shard_map/ppermute | solution.py:844
  388.8 13.5 %collective-permute-start.60 = (bf16[1,128,1024]{2,1,0:T(8,128)(2,1)S(1)}, bf16[1,128,1024]{2,1,0:T(8,128)(2,1)S(1)}, u32[]{:S(2)}, u32[]{:S(2)}) collective-permute-start(bf16[1,128,1024]{2,1,0:T(8,128)(2,1)S(1)} %get-tuple-element.292), channel_id=1, source_target_pairs={{0,8},{4,12},{8,0},{12,4},{16,24},{20,28},{24,16},{28,20},{1,9},{5... | collective-permute-start | bytes 786440 | tf_op jit(solution)/shard_map/ppermute | solution.py:844
  399.4 12.6 %collective-permute-start.65 = (bf16[1,64,1024]{2,1,0:T(8,128)(2,1)S(1)}, bf16[1,64,1024]{2,1,0:T(8,128)(2,1)S(1)}, u32[]{:S(2)}, u32[]{:S(2)}) collective-permute-start(bf16[1,64,1024]{2,1,0:T(8,128)(2,1)S(1)} %get-tuple-element.303), channel_id=1, source_target_pairs={{0,16},{4,20},{8,24},{12,28},{16,0},{20,4},{24,8},{28,12},{1,17},{... | collective-permute-start | bytes 393224 | tf_op jit(solution)/shard_map/ppermute | solution.py:844
  402.6 12.2 %collective-permute-start.63 = (bf16[1,64,1024]{2,1,0:T(8,128)(2,1)S(1)}, bf16[1,64,1024]{2,1,0:T(8,128)(2,1)S(1)}, u32[]{:S(2)}, u32[]{:S(2)}) collective-permute-start(bf16[1,64,1024]{2,1,0:T(8,128)(2,1)S(1)} %get-tuple-element.300), channel_id=1, source_target_pairs={{0,16},{4,20},{8,24},{12,28},{16,0},{20,4},{24,8},{28,12},{1,17},{... | collective-permute-start | bytes 393224 | tf_op jit(solution)/shard_map/ppermute | solution.py:844
  412.1 9.9 %collective-permute-start.67 = (bf16[64,1024]{1,0:T(8,128)(2,1)S(1)}, bf16[64,1024]{1,0:T(8,128)(2,1)S(1)}, u32[]{:S(2)}, u32[]{:S(2)}) collective-permute-start(bf16[64,1024]{1,0:T(8,128)(2,1)S(1)} %bitcast.56), channel_id=1, source_target_pairs={{0,16},{4,20},{8,24},{12,28},{16,0},{20,4},{24,8},{28,12},{1,17},{... | collective-permute-start | bytes 393224 | tf_op jit(solution)/shard_map/ppermute | solution.py:844
  414.9 8.5 %collective-permute-start.66 = (bf16[64,1024]{1,0:T(8,128)(2,1)S(1)}, bf16[64,1024]{1,0:T(8,128)(2,1)S(1)}, u32[]{:S(2)}, u32[]{:S(2)}) collective-permute-start(bf16[64,1024]{1,0:T(8,128)(2,1)S(1)} %bitcast.58), channel_id=1, source_target_pairs={{0,16},{4,20},{8,24},{12,28},{16,0},{20,4},{24,8},{28,12},{1,17},{... | collective-permute-start | bytes 393224 | tf_op jit(solution)/shard_map/ppermute | solution.py:844
  422.1 8.3 %collective-permute-start.69 = (bf16[128,1024]{1,0:T(8,128)(2,1)S(1)}, bf16[128,1024]{1,0:T(8,128)(2,1)S(1)}, u32[]{:S(2)}, u32[]{:S(2)}) collective-permute-start(bf16[128,1024]{1,0:T(8,128)(2,1)S(1)} %get-tuple-element.312.refs_1_), channel_id=1, source_target_pairs={{0,8},{4,12},{8,0},{12,4},{16,24},{20,28},{24,16},{28,20},{1,9},{5... | collective-permute-start | bytes 786440 | tf_op jit(solution)/shard_map/ppermute | solution.py:844
  423.5 9.7 %collective-permute-start.68 = (bf16[128,1024]{1,0:T(8,128)(2,1)S(1)}, bf16[128,1024]{1,0:T(8,128)(2,1)S(1)}, u32[]{:S(2)}, u32[]{:S(2)}) collective-permute-start(bf16[128,1024]{1,0:T(8,128)(2,1)S(1)} %get-tuple-element.311.refs_1_), channel_id=1, source_target_pairs={{0,8},{4,12},{8,0},{12,4},{16,24},{20,28},{24,16},{28,20},{1,9},{5... | collective-permute-start | bytes 786440 | tf_op jit(solution)/shard_map/ppermute | solution.py:844
  430.4 13.8 %collective-permute-start.71 = (bf16[256,1024]{1,0:T(8,128)(2,1)S(1)}, bf16[256,1024]{1,0:T(8,128)(2,1)S(1)}, u32[]{:S(2)}, u32[]{:S(2)}) collective-permute-start(bf16[256,1024]{1,0:T(8,128)(2,1)S(1)} %get-tuple-element.318.refs_1_), channel_id=1, source_target_pairs={{0,4},{4,0},{8,12},{12,8},{16,20},{20,16},{24,28},{28,24},{1,5},{5... | collective-permute-start | bytes 1572872 | tf_op jit(solution)/shard_map/ppermute | solution.py:844
  433.3 16.6 %collective-permute-start.70 = (bf16[256,1024]{1,0:T(8,128)(2,1)S(1)}, bf16[256,1024]{1,0:T(8,128)(2,1)S(1)}, u32[]{:S(2)}, u32[]{:S(2)}) collective-permute-start(bf16[256,1024]{1,0:T(8,128)(2,1)S(1)} %get-tuple-element.317.refs_1_), channel_id=1, source_target_pairs={{0,4},{4,0},{8,12},{12,8},{16,20},{20,16},{24,28},{28,24},{1,5},{5... | collective-permute-start | bytes 1572872 | tf_op jit(solution)/shard_map/ppermute | solution.py:844
  (84 other events, 519.7 us)
